TPU v7x, 32 devices: a whole 2x2x4 slice. The times are simulated.
32 devices in a mesh: dp: 8 (over z, x), mp: 4 (over y, core).
Axes of the slice: x: 2, y: 2, z: 4, core: 2. Of those that a mesh axis runs over, the one named last changes fastest.
Arguments:
- tokens: bfloat16 [16384, 768], P('dp')
- latents: bfloat16 [512, 768], P('dp'), may hold values from -6 to 6
- image_of_group: int32 [64], replicated, may hold values from 0 to 4, as said below
- token_valid: int32 [16384], P('dp'), may hold values from 0 to 1, as said below
- norm1_gain: float32 [768], replicated, may hold values from 0.5 to 1.5
- norm1_shift: float32 [768], replicated, may hold values from -2 to 2
- w_qkv: bfloat16 [3, 768, 768], P(None, None, 'mp'), may hold values from -0.21875 to 0.21875
- b_qv: float32 [2, 768], P(None, 'mp'), may hold values from -2 to 2
- w_out: bfloat16 [768, 768], P('mp'), may hold values from -0.875 to 0.875
- b_out: float32 [768], replicated, may hold values from -2 to 2
- norm2_gain: float32 [768], replicated, may hold values from 0.5 to 1.5
- norm2_shift: float32 [768], replicated, may hold values from -2 to 2
- w_up: bfloat16 [768, 3072], P(None, 'mp'), may hold values from -0.21875 to 0.21875
- b_up: float32 [3072], P('mp'), may hold values from -3 to 3
- w_down: bfloat16 [3072, 768], P('mp'), may hold values from -0.21875 to 0.21875
- b_down: float32 [768], replicated, may hold values from -2 to 2
- cot_tokens: bfloat16 [16384, 768], P('dp'), may hold values from -6 to 6
- cot_latents: bfloat16 [512, 768], P('dp'), may hold values from -6 to 6
Outputs:
- out_tokens: bfloat16 [16384, 768], P('dp')
- out_latents: bfloat16 [512, 768], P('dp')
- grad_tokens: bfloat16 [16384, 768], P('dp')
- grad_latents: bfloat16 [512, 768], P('dp')
- grad_norm1_gain: float32 [768], replicated
- grad_norm1_shift: float32 [768], replicated
- grad_w_qkv: float32 [3, 768, 768], P(None, None, 'mp')
- grad_b_qv: float32 [2, 768], P(None, 'mp')
- grad_w_out: float32 [768, 768], P('mp')
- grad_b_out: float32 [768], replicated
- grad_norm2_gain: float32 [768], replicated
- grad_norm2_shift: float32 [768], replicated
- grad_w_up: float32 [768, 3072], P(None, 'mp')
- grad_b_up: float32 [3072], P('mp')
- grad_w_down: float32 [3072, 768], P('mp')
- grad_b_down: float32 [768], replicated
- root_means: float32 [3], replicated
Inputs may be any that keep to these rules, and one draw needn't show every extreme that they name: Each image's groups are the groups g with image_of_group[g] equal to it; every image has at least one group. `token_valid`: within a group the real tokens are a prefix; every group of an image is full except the image's highest-numbered group, which holds 1 to 256 real tokens.
All inputs are finite; a program needn't handle non-finite values.
Results may differ from a plain program's by a relative error of at most 0.018.
Values may be sent and summed in bfloat16 or wider, within the bound.
No kernel may reach another device: no remote copies, remote signals or barrier semaphores. Data moves between devices by JAX's collectives and lax.ppermute only.
A program may use at most 256 MiB of HBM per device.

v0:
```python
import jax
import jax.numpy as jnp
from jax import lax
from jax.sharding import PartitionSpec as P

HEAD = 64
GROUP = 256
LAT = 8


def layer_norm(values, gain, shift):
    center = values - jnp.mean(values, axis=-1, keepdims=True)
    spread = jnp.mean(center * center, axis=-1, keepdims=True)
    return center * lax.rsqrt(spread + 1e-06) * gain + shift


def gelu_tanh(values):
    return (
        0.5
        * values
        * (1.0 + jnp.tanh(0.7978845608028654 * (values + 0.044715 * values * values * values)))
    )


def masked_scores(queries, key_rows, allowed):
    scores = (
        jnp.einsum("gqhe,gkhe->ghqk", queries, key_rows, preferred_element_type=jnp.float32) * 0.125
    )
    return jnp.where(allowed[:, None, None, :], scores, -1e30)


def attend_forward(queries, key_rows, value_rows, allowed):
    scores = masked_scores(queries, key_rows, allowed)
    row_top = jnp.max(scores, axis=-1, keepdims=True)
    expo_terms = jnp.exp(scores - row_top)
    row_total = jnp.sum(expo_terms, axis=-1, keepdims=True)
    weights = (expo_terms / row_total).astype(jnp.bfloat16)
    mixed_rows = jnp.einsum(
        "ghqk,gkhe->gqhe", weights, value_rows, preferred_element_type=jnp.float32
    )
    return (mixed_rows, row_top + jnp.log(row_total))


def attend_backward(queries, key_rows, value_rows, allowed, log_total, grad_mixed):
    weights = jnp.exp(masked_scores(queries, key_rows, allowed) - log_total)
    grad_values = jnp.einsum(
        "ghqk,gqhe->gkhe",
        weights.astype(jnp.bfloat16),
        grad_mixed,
        preferred_element_type=jnp.float32,
    )
    grad_weights = jnp.einsum(
        "gqhe,gkhe->ghqk", grad_mixed, value_rows, preferred_element_type=jnp.float32
    )
    grad_scores = weights * (grad_weights - jnp.sum(weights * grad_weights, axis=-1, keepdims=True))
    grad_scores = grad_scores.astype(jnp.bfloat16)
    grad_queries = (
        jnp.einsum("ghqk,gkhe->gqhe", grad_scores, key_rows, preferred_element_type=jnp.float32)
        * 0.125
    )
    grad_keys = (
        jnp.einsum("ghqk,gqhe->gkhe", grad_scores, queries, preferred_element_type=jnp.float32)
        * 0.125
    )
    return (grad_queries, grad_keys, grad_values)


def per_device(
    tokens,
    latents,
    image_of_group,
    token_valid,
    norm1_gain,
    norm1_shift,
    w_qkv,
    b_qv,
    w_out,
    b_out,
    norm2_gain,
    norm2_shift,
    w_up,
    b_up,
    w_down,
    b_down,
    cot_tokens,
    cot_latents,
):
    tok_count = tokens.shape[0]
    lat_count = latents.shape[0]
    group_count = lat_count // LAT
    width_here = w_qkv.shape[2]
    heads_here = width_here // HEAD
    own_images = lax.dynamic_slice_in_dim(
        image_of_group, lax.axis_index("dp") * group_count, group_count
    )
    every_image = jnp.repeat(image_of_group, LAT)
    same_image = own_images[:, None] == every_image[None, :]
    valid_bool = token_valid.reshape(group_count, GROUP) > 0
    allowed_near = jnp.concatenate([valid_bool, jnp.ones((group_count, LAT), jnp.bool_)], 1)
    allowed_far = jnp.concatenate([valid_bool, same_image], 1)
    stream = jnp.concatenate([tokens, latents], 0).astype(jnp.float32)
    row_valid = jnp.concatenate(
        [token_valid.astype(jnp.float32), jnp.zeros((lat_count,), jnp.float32)], 0
    )

    def reduce_rows(partial_rows):
        return lax.psum(partial_rows.astype(jnp.bfloat16), "mp").astype(jnp.float32)

    def split_heads(values):
        tok_part = values[:tok_count].reshape(group_count, GROUP, heads_here, HEAD)
        lat_part = values[tok_count:].reshape(group_count, LAT, heads_here, HEAD)
        return (tok_part, lat_part)

    def far_keys(tok_part, every_rows):
        every_heads = every_rows.reshape(1, every_rows.shape[0], heads_here, HEAD)
        spread_all = jnp.broadcast_to(
            every_heads, (group_count, every_rows.shape[0], heads_here, HEAD)
        )
        return jnp.concatenate([tok_part, spread_all], 1)

    normed = layer_norm(stream, norm1_gain, norm1_shift).astype(jnp.bfloat16)
    project = jnp.einsum("rd,tde->tre", normed, w_qkv, preferred_element_type=jnp.float32)
    queries = (project[0] + b_qv[0]).astype(jnp.bfloat16)
    key_rows = project[1].astype(jnp.bfloat16)
    value_rows = (project[2] + b_qv[1]).astype(jnp.bfloat16)
    lat_keys = key_rows[tok_count:]
    lat_values = value_rows[tok_count:]
    every_keys, every_values = (
        lax.all_gather(lat_keys, "dp", axis=0, tiled=True),
        lax.all_gather(lat_values, "dp", axis=0, tiled=True),
    )
    query_tok, query_lat = split_heads(queries)
    key_tok, key_lat = split_heads(key_rows)
    value_tok, value_lat = split_heads(value_rows)
    near_keys = jnp.concatenate([key_tok, key_lat], 1)
    near_values = jnp.concatenate([value_tok, value_lat], 1)
    mixed_tok, total_tok = attend_forward(query_tok, near_keys, near_values, allowed_near)
    mixed_lat, total_lat = attend_forward(
        query_lat, far_keys(key_tok, every_keys), far_keys(value_tok, every_values), allowed_far
    )
    mixed_rows = jnp.concatenate(
        [mixed_tok.reshape(tok_count, width_here), mixed_lat.reshape(lat_count, width_here)], 0
    ).astype(jnp.bfloat16)
    attn_held = reduce_rows(jnp.dot(mixed_rows, w_out, preferred_element_type=jnp.float32)) + b_out
    residual = stream + attn_held
    normed_two = layer_norm(residual, norm2_gain, norm2_shift).astype(jnp.bfloat16)
    up_pre = jnp.dot(normed_two, w_up, preferred_element_type=jnp.float32) + b_up
    activated = gelu_tanh(up_pre).astype(jnp.bfloat16)
    branch = reduce_rows(jnp.dot(activated, w_down, preferred_element_type=jnp.float32)) + b_down
    out_held = residual + branch
    out_rows = out_held.astype(jnp.bfloat16)
    statistics = jnp.stack(
        [
            jnp.sum(row_valid * jnp.sum(out_held * out_held, -1)),
            jnp.sum(row_valid * jnp.sum(attn_held * attn_held, -1)),
            jnp.sum(row_valid * jnp.sum(branch * branch, -1)),
            jnp.sum(row_valid),
        ]
    )
    cot_rows = jnp.concatenate([cot_tokens, cot_latents], 0)
    grad_w_down = jnp.einsum("rf,rd->fd", activated, cot_rows, preferred_element_type=jnp.float32)
    grad_b_down = jnp.sum(cot_rows.astype(jnp.float32), 0)
    grad_active = jnp.einsum("rd,fd->rf", cot_rows, w_down, preferred_element_type=jnp.float32)
    grad_up = jax.vjp(gelu_tanh, up_pre)[1](grad_active)[0].astype(jnp.bfloat16)
    grad_w_up = jnp.einsum("rd,rf->df", normed_two, grad_up, preferred_element_type=jnp.float32)
    grad_b_up = jnp.sum(grad_up.astype(jnp.float32), 0)
    grad_normed_two = reduce_rows(
        jnp.einsum("rf,df->rd", grad_up, w_up, preferred_element_type=jnp.float32)
    )
    pull_two = jax.vjp(layer_norm, residual, norm2_gain, norm2_shift)[1]
    grad_norm_part, grad_gain_two, grad_shift_two = pull_two(grad_normed_two)
    grad_residual = cot_rows.astype(jnp.float32) + grad_norm_part
    grad_branch_held = grad_residual.astype(jnp.bfloat16)
    grad_b_out = jnp.sum(grad_branch_held.astype(jnp.float32), 0)
    grad_w_out = jnp.einsum(
        "re,rd->ed", mixed_rows, grad_branch_held, preferred_element_type=jnp.float32
    )
    grad_mixed = jnp.einsum(
        "rd,ed->re", grad_branch_held, w_out, preferred_element_type=jnp.float32
    ).astype(jnp.bfloat16)
    grad_mix_tok, grad_mix_lat = split_heads(grad_mixed)
    grad_query_tok, grad_near_keys, grad_near_values = attend_backward(
        query_tok, near_keys, near_values, allowed_near, total_tok, grad_mix_tok
    )
    grad_query_lat, grad_far_keys, grad_far_values = attend_backward(
        query_lat,
        far_keys(key_tok, every_keys),
        far_keys(value_tok, every_values),
        allowed_far,
        total_lat,
        grad_mix_lat,
    )
    every_grad_keys = jnp.sum(grad_far_keys[:, GROUP:], 0).reshape(-1, width_here)
    every_grad_values = jnp.sum(grad_far_values[:, GROUP:], 0).reshape(-1, width_here)
    back_keys, back_values = (
        lax.psum_scatter(every_grad_keys, "dp", scatter_dimension=0, tiled=True),
        lax.psum_scatter(every_grad_values, "dp", scatter_dimension=0, tiled=True),
    )
    grad_keys = jnp.concatenate(
        [
            (grad_near_keys[:, :GROUP] + grad_far_keys[:, :GROUP]).reshape(tok_count, width_here),
            grad_near_keys[:, GROUP:].reshape(lat_count, width_here) + back_keys,
        ],
        0,
    )
    grad_values = jnp.concatenate(
        [
            (grad_near_values[:, :GROUP] + grad_far_values[:, :GROUP]).reshape(
                tok_count, width_here
            ),
            grad_near_values[:, GROUP:].reshape(lat_count, width_here) + back_values,
        ],
        0,
    )
    grad_queries = jnp.concatenate(
        [
            grad_query_tok.reshape(tok_count, width_here),
            grad_query_lat.reshape(lat_count, width_here),
        ],
        0,
    )
    grad_project = jnp.stack([grad_queries, grad_keys, grad_values]).astype(jnp.bfloat16)
    grad_w_qkv = jnp.einsum("rd,tre->tde", normed, grad_project, preferred_element_type=jnp.float32)
    grad_b_qv = jnp.sum(grad_project[0::2].astype(jnp.float32), 1)
    grad_normed = reduce_rows(
        jnp.einsum("tre,tde->rd", grad_project, w_qkv, preferred_element_type=jnp.float32)
    )
    pull_one = jax.vjp(layer_norm, stream, norm1_gain, norm1_shift)[1]
    grad_stream_part, grad_gain_one, grad_shift_one = pull_one(grad_normed)
    grad_rows = (grad_residual + grad_stream_part).astype(jnp.bfloat16)
    weight_sums = lax.psum(
        (grad_w_qkv, grad_b_qv, grad_w_out, grad_w_up, grad_b_up, grad_w_down), "dp"
    )
    small_terms = (
        grad_gain_one,
        grad_shift_one,
        grad_b_out,
        grad_gain_two,
        grad_shift_two,
        grad_b_down,
        statistics,
    )
    small_sums = lax.psum(
        (
            small_terms[0],
            small_terms[1],
            small_terms[2],
            small_terms[3],
            small_terms[4],
            small_terms[5],
            small_terms[6],
        ),
        "dp",
    )
    root_means = jnp.sqrt(small_sums[6][:3] / (small_sums[6][3] * tokens.shape[1]))
    return (
        out_rows[:tok_count],
        out_rows[tok_count:],
        grad_rows[:tok_count],
        grad_rows[tok_count:],
        small_sums[0],
        small_sums[1],
        weight_sums[0],
        weight_sums[1],
        weight_sums[2],
        small_sums[2],
        small_sums[3],
        small_sums[4],
        weight_sums[3],
        weight_sums[4],
        weight_sums[5],
        small_sums[5],
        root_means,
    )


def solution(mesh):
    placed = (
        P("dp", None),
        P("dp", None),
        P(),
        P("dp"),
        P(),
        P(),
        P(None, None, "mp"),
        P(None, "mp"),
        P("mp", None),
        P(),
        P(),
        P(),
        P(None, "mp"),
        P("mp"),
        P("mp", None),
        P(),
        P("dp", None),
        P("dp", None),
    )
    return jax.shard_map(
        per_device,
        mesh=mesh,
        in_specs=placed,
        out_specs=(
            P("dp", None),
            P("dp", None),
            P("dp", None),
            P("dp", None),
            P(),
            P(),
            P(None, None, "mp"),
            P(None, "mp"),
            P("mp", None),
            P(),
            P(),
            P(),
            P(None, "mp"),
            P("mp"),
            P("mp", None),
            P(),
            P(),
        ),
        check_vma=False,
    )
```

profile of v0, /device:TPU:0, one launch (start us, length us, event | category | flops | bytes accessed | tf_op | source)
XLA Modules:
  0.0 838.4 jit_solution(11775554604311262187)
XLA Ops:
  18.3 32.5 %all_gather.6 = bf16[512,192]{1,0:T(8,128)(2,1)S(1)} all-gather(bf16[64,192]{1,0:T(8,128)(2,1)S(1)} %copy.113), channel_id=1, replica_groups=mesh['dp'=8,'mp'=4] {'dp'}, dimensions={0}, use_global_device_ids=true | all-gather | bytes 221184 | tf_op jit(solution)/shard_map/all_gather | solution.py:130
  51.6 31.0 %all-gather = bf16[1,512,192]{2,1,0:T(8,128)(2,1)S(1)} all-gather(bf16[1,64,192]{2,1,0:T(8,128)(2,1)S(1)} %copy.116), channel_id=2, replica_groups=mesh['dp'=8,'mp'=4] {'dp'}, dimensions={1}, use_global_device_ids=true | all-gather | bytes 221184 | tf_op jit(solution)/shard_map/all_gather | solution.py:129
  98.2 2.9 fusion.104
  108.8 3.7 constant_dynamic-update-slice_fusion.1
  113.2 66.2 %all-reduce.10.cloned.1.call-done = bf16[2112,768]{1,0:T(8,128)(2,1)} async-done(((bf16[2112,768]{1,0:T(8,128)(2,1)}), bf16[2112,768]{1,0:T(8,128)(2,1)}) %all-reduce.10.cloned.1.call-update) | async-done | bytes 3244048 | tf_op jit(solution)/shard_map/psum | solution.py:107
  179.4 3.6 fusion.25
  186.3 4.0 fusion.93
  190.3 9.9 %convert_reduce_fusion.4 = (f32[768]{0:T(1024)}, bf16[2112,768]{1,0:T(8,128)(2,1)S(1)}, bf16[2112,768]{1,0:T(8,128)(2,1)S(1)}) fusion(f32[2112,768]{1,0:T(8,128)S(1)} %fusion.93, f32[768]{0:T(1024)S(1)} %copy-done.68, bf16[2112,768]{1,0:T(8,128)(2,1)} %constant_dynamic-update-slice_fusion, bf16[768,768]{1,0:T(8,128)(2,1)S(1)} %copy-done), kind=kOutput, calls=%fused_computation.42 | convolution fusion | flops 2538454272 | bytes 17405952 | tf_op jit(solution)/shard_map/rd,fd->rf/dot_general | solution.py:163
  200.2 4.1 convolution_convert_fusion.1
  204.3 4.1 convolution_convert_fusion.2
  208.8 8.9 %fusion.92 = f32[768,768]{1,0:T(8,128)} fusion(bf16[2112,768]{1,0:T(8,128)(2,1)} %copy-done.73, f32[768]{0:T(1024)S(1)} %copy-done.69, f32[768]{0:T(1024)S(1)} %copy-done.51, f32[2112]{0:T(1024)S(1)} %fusion.81, bf16[2112,768]{1,0:T(8,128)(2,1)} %all-reduce.10.cloned.1.call-done, f32[2112]{0:T(1024)S(1)} %broadcast_multiply_fusion, ...), kind=kOutput, calls=%fused_computation.174 | convolution fusion | flops 2510880768 | bytes 12117504 | tf_op jit(solution)/shard_map/rd,rf->df/dot_general | solution.py:165
  217.7 114.0 %all-reduce.16.cloned.1.call-done = (bf16[2112,768]{1,0:T(8,128)(2,1)}, bf16[2112,768]{1,0:T(8,128)(2,1)}) async-done(((bf16[2112,768]{1,0:T(8,128)(2,1)}, bf16[2112,768]{1,0:T(8,128)(2,1)}), (bf16[2112,768]{1,0:T(8,128)(2,1)}, bf16[2112,768]{1,0:T(8,128)(2,1)})) %all-reduce.16.cloned.1.call-update) | async-done | bytes 6488080 | tf_op jit(solution)/shard_map/psum | solution.py:107
  331.7 9.9 %multiply_reduce_fusion.2 = (f32[2112]{0:T(1024)S(1)}, f32[2112]{0:T(1024)S(1)}, f32[2112]{0:T(1024)S(1)}, f32[2112]{0:T(1024)S(1)}, f32[768]{0:T(1024)}, /*index=5*/bf16[2112,768]{1,0:T(8,128)(2,1)}) fusion(bf16[2112,768]{1,0:T(8,128)(2,1)} %get-tuple-element.45, bf16[2112,768]{1,0:T(8,128)(2,1)} %all-reduce.10.cloned.1.call-done, f32[768]{0:T(1024)S(1)} %copy-done.62, ...), kind=kLoop, calls=%fused_computation.41 | loop fusion | flops 37297152 | bytes 16274688 | tf_op jit(solution)/shard_map/reduce_sum | solution.py:154
  342.2 4.9 fusion.19
  347.1 6.9 convert_reduce_fusion.5
  366.2 2.9 multiply_bitcast_fusion
  369.2 4.1 multiply_reduce_fusion.3
  377.3 6.1 multiply_convert_fusion
  391.3 2.8 fusion.53
  395.1 44.1 %reduce-scatter.9.cloned.1.call-done = f32[64,192]{1,0:T(8,128)} async-done(((f32[512,192]{1,0:T(8,128)}), f32[64,192]{1,0:T(8,128)}) %reduce-scatter.9.cloned.1.call-update) | async-done | bytes 49168
  440.2 63.7 %reduce-scatter.7.cloned.1.call-done = f32[64,192]{1,0:T(8,128)} async-done(((f32[512,192]{1,0:T(8,128)}), f32[64,192]{1,0:T(8,128)}) %reduce-scatter.7.cloned.1.call-update) | async-done | bytes 49168
  506.1 5.6 bitcast_convert_fusion
  512.3 7.4 fusion.105
  521.7 3.8 fusion.48
  527.0 3.8 slice.127
  534.1 46.8 %all-reduce.12.cloned.1.call-done = bf16[2112,768]{1,0:T(8,128)(2,1)} async-done(((bf16[2112,768]{1,0:T(8,128)(2,1)}), bf16[2112,768]{1,0:T(8,128)(2,1)}) %all-reduce.12.cloned.1.call-update) | async-done | bytes 3244048 | tf_op jit(solution)/shard_map/psum | solution.py:107
  580.9 4.6 convert_reduce_fusion
  585.6 5.6 fusion.20
  591.3 8.5 %convert_reduce_fusion.3 = (f32[768]{0:T(1024)S(1)}, bf16[2112,768]{1,0:T(8,128)(2,1)S(1)}) fusion(bf16[2112,768]{1,0:T(8,128)(2,1)} %constant_dynamic-update-slice_fusion, f32[2112]{0:T(1024)S(1)} %negate_multiply_fusion, f32[2112]{0:T(1024)S(1)} %multiply_multiply_fusion.2, f32[2112]{0:T(1024)S(1)} %broadcast_multiply_fusion.1, f32[2112]{0:T(1024)S(1)} %copy-done.45, ...), kind=kLoop, calls=%fused_computation.19 | loop fusion | flops 45415680 | bytes 19544064 | tf_op jit(solution)/shard_map/reduce_sum | solution.py:162
  602.4 40.1 %all-reduce.2 = (f32[768]{0:T(1024)}, f32[768]{0:T(1024)}, f32[2,192]{1,0:T(2,128)}, f32[768]{0:T(1024)}, f32[768]{0:T(1024)}, /*index=5*/f32[768]{0:T(1024)}, f32[768]{0:T(1024)}, f32[768]{0:T(1024)}, f32[4]{0:T(128)S(1)}) all-reduce(f32[768]{0:T(1024)S(1)} %get-tuple-element.19, ...), channel_id=1, replica_groups=mesh['dp'=8,'mp'=4] {'dp'}, use_global_device_ids=true, to_apply=%region_23.24 | all-reduce | flops 5764 | bytes 46112 | tf_op jit(solution)/shard_map/psum | solution.py:243
  644.3 179.3 %all-reduce.14.cloned.1.call-done = (f32[3,768,192]{1,2,0:T(8,128)}, f32[192,768]{1,0:T(8,128)}, f32[768,768]{1,0:T(8,128)}, f32[768,768]{1,0:T(8,128)}) async-done(((f32[3,768,192]{1,2,0:T(8,128)}, f32[192,768]{1,0:T(8,128)}, f32[768,768]{1,0:T(8,128)}, f32[768,768]{1,0:T(8,128)}), (f32[3,768,192]{1,2,0:T(8,128)}, f32[192,768]{1,0:T(8,128)}, f32[768,768]{1,0:T(8,128)}, ...) | async-done | bytes 7077904 | tf_op jit(solution)/shard_map/psum | solution.py:231
  823.6 2.9 copy.192
  (287 shorter events, 83.1 us)
Async XLA Ops:
  7.2 183.1 %copy-start = (bf16[768,768]{1,0:T(8,128)(2,1)S(1)}, bf16[768,768]{1,0:T(8,128)(2,1)}, u32[]{:S(2)}) copy-start(bf16[768,768]{1,0:T(8,128)(2,1)} %param.32) | copy-start | bytes 3538948
  7.2 5.8 copy-start.15
  7.2 172.2 %all-reduce.10.cloned.1.call-start = ((), (), s32[]{:S(2)}) async-start(), calls=%async_computation.2 | async-start | bytes 6488064 | tf_op jit(solution)/shard_map/psum | solution.py:107
  15.8 66.9 %copy-start.57 = (s32[2048]{0:T(1024)S(1)}, s32[2048]{0:T(1024)}, u32[]{:S(2)}) copy-start(s32[2048]{0:T(1024)} %param.21) | copy-start | bytes 24580
  15.8 66.9 %copy-start.63 = (s32[64]{0:T(128)S(1)}, s32[64]{0:T(128)}, u32[]{:S(2)}) copy-start(s32[64]{0:T(128)} %param.20) | copy-start | bytes 772
  83.3 14.9 %copy-start.24 = (bf16[24,8,8,256]{3,2,1,0:T(8,128)(2,1)}, bf16[24,8,8,256]{3,2,1,0:T(8,128)(2,1)S(1)}, u32[]{:S(2)}) copy-start(bf16[24,8,8,256]{3,2,1,0:T(8,128)(2,1)S(1)} %copy.152) | copy-start | bytes 2359300
  85.7 16.5 %copy-start.22 = (bf16[8,256,3,64]{1,3,2,0:T(8,128)(2,1)}, bf16[8,256,3,64]{1,3,2,0:T(8,128)(2,1)S(1)}, u32[]{:S(2)}) copy-start(bf16[8,256,3,64]{1,3,2,0:T(8,128)(2,1)S(1)} %copy.114) | copy-start | bytes 2359300
  90.0 6.3 copy-start.34
  90.2 12.0 %copy-start.32 = (bf16[8,8,3,64]{1,3,2,0:T(8,128)(2,1)}, bf16[8,8,3,64]{1,3,2,0:T(8,128)(2,1)S(1)}, u32[]{:S(2)}) copy-start(bf16[8,8,3,64]{1,3,2,0:T(8,128)(2,1)S(1)} %copy.115) | copy-start | bytes 73732
  98.2 6.3 copy-start.53
  108.2 71.2 %copy-start.41 = (f32[768]{0:T(1024)S(1)}, f32[768]{0:T(1024)}, u32[]{:S(2)}) copy-start(f32[768]{0:T(1024)} %param.27) | copy-start | bytes 9220
  108.2 223.4 %all-reduce.16.cloned.1.call-start = ((), (), s32[]{:S(2)}) async-start(), calls=%async_computation.7 | async-start | bytes 12976128 | tf_op jit(solution)/shard_map/psum | solution.py:107
  208.5 230.8 %reduce-scatter.9.cloned.1.call-start = ((), (), s32[]{:S(2)}) async-start(), calls=%async_computation.5 | async-start | bytes 589824
  208.7 122.9 %copy-start.62 = (f32[768]{0:T(1024)S(1)}, f32[768]{0:T(1024)}, u32[]{:S(2)}) copy-start(f32[768]{0:T(1024)} %param.33) | copy-start | bytes 9220
  331.7 10.5 %copy-start.4 = (bf16[2048,768]{1,0:T(8,128)(2,1)S(1)}, bf16[2048,768]{1,0:T(8,128)(2,1)}, u32[]{:S(2)}) copy-start(bf16[2048,768]{1,0:T(8,128)(2,1)} %param.18) | copy-start | bytes 9437188
  331.7 10.5 %copy-start.8 = (bf16[2112,768]{1,0:T(8,128)(2,1)S(1)}, bf16[2112,768]{1,0:T(8,128)(2,1)}, u32[]{:S(2)}) copy-start(bf16[2112,768]{1,0:T(8,128)(2,1)} %all-reduce.10.cloned.1.call-done) | copy-start | bytes 9732100
  331.7 10.5 %copy-start.11 = (bf16[2112,768]{1,0:T(8,128)(2,1)S(1)}, bf16[2112,768]{1,0:T(8,128)(2,1)}, u32[]{:S(2)}) copy-start(bf16[2112,768]{1,0:T(8,128)(2,1)} %get-tuple-element.46) | copy-start | bytes 9732100
  347.1 7.0 copy-start.46
  347.1 8.6 %copy-start.67 = (bf16[192,768]{1,0:T(8,128)(2,1)S(1)}, bf16[192,768]{1,0:T(8,128)(2,1)}, u32[]{:S(2)}) copy-start(bf16[192,768]{1,0:T(8,128)(2,1)} %param.26) | copy-start | bytes 884740
  355.7 5.8 slice-start
  376.9 9.1 %slice-start.2 = ((s8[4718592]{0:T(1024)(128)(4,1)}), s8[524288]{0:T(1024)(128)(4,1)S(1)}, s32[]{:S(2)}) async-start(s8[4718592]{0:T(1024)(128)(4,1)} %bitcast.125), calls=%async_computation.10 | async-start | bytes 1048576
  377.0 127.0 %reduce-scatter.7.cloned.1.call-start = ((), (), s32[]{:S(2)}) async-start(), calls=%async_computation.4 | async-start | bytes 589824
  377.3 6.1 copy-start.25
  377.3 8.7 %slice-start.3 = ((s8[4718592]{0:T(1024)(128)(4,1)}), s8[4194304]{0:T(1024)(128)(4,1)S(1)}, s32[]{:S(2)}) async-start(s8[4718592]{0:T(1024)(128)(4,1)} %bitcast.125), calls=%async_computation.11 | async-start | bytes 8388608
  395.0 185.9 %all-reduce.12.cloned.1.call-start = ((), (), s32[]{:S(2)}) async-start(), calls=%async_computation.3 | async-start | bytes 6488064 | tf_op jit(solution)/shard_map/psum | solution.py:107
  511.8 8.0 copy-start.54
  511.8 311.8 %all-reduce.14.cloned.1.call-start = ((), (), s32[]{:S(2)}) async-start(), calls=%async_computation.6 | async-start | bytes 14155776 | tf_op jit(solution)/shard_map/psum | solution.py:231
  512.3 7.5 copy-start.21
  512.3 7.5 copy-start.36
  533.8 51.8 %copy-start.49 = (f32[2112]{0:T(1024)S(1)}, f32[2112]{0:T(1024)}, u32[]{:S(2)}) copy-start(f32[2112]{0:T(1024)} %copy-done.48) | copy-start | bytes 25348
  580.9 10.3 %copy-start.12 = (bf16[2112,768]{1,0:T(8,128)(2,1)S(1)}, bf16[2112,768]{1,0:T(8,128)(2,1)}, u32[]{:S(2)}) copy-start(bf16[2112,768]{1,0:T(8,128)(2,1)} %get-tuple-element.46) | copy-start | bytes 9732100
  823.6 6.4 copy-start.27
  (54 other events, 182.8 us)
Sparse Core Ops, SparseCore 0:
  108.4 70.9 all-reduce.9
  208.6 123.0 all-reduce.15
  377.1 62.0 reduce-scatter.8
  443.0 60.9 reduce-scatter.6
  511.9 68.9 all-reduce.11
  587.0 236.5 all-reduce.13
where the time goes:
time: 844 us; the launch traced here: 838 us
  waiting for transfers between devices  514 us (61%)
  blocking collectives  104 us (12%)
  matrix products  80.5 us (10%)
  other arithmetic  68.5 us (8%)
  local copies, waits for them, and re-layouts  53.7 us (6%)
  between operations  16.2 us (2%)
    psum x3, waiting for transfers between devices, reduce_rows(): return lax.psum(partial_rows.astype(jnp.bfloat16), 'mp').astype(jnp.float32)  227 us
    psum x1, waiting for transfers between devices, per_device(): lax.psum((grad_w_qkv, grad_b_qv, grad_w_out, grad_w_up, grad_b_up, grad_w...  179 us
    unnamed x8, waiting for transfers between devices  108 us
    psum x1, blocking collectives, per_device(): lax.psum((small_terms[0], small_terms[1], small_terms[2], small_terms[3],...  40.1 us
    all_gather x1, blocking collectives, per_device(): lax.all_gather(lat_values, 'dp', axis=0, tiled=True)  32.5 us
    all_gather x1, blocking collectives, per_device(): lax.all_gather(lat_keys, 'dp', axis=0, tiled=True)  31 us
    unnamed x173, local copies, waits for them, and re-layouts  27.8 us
  transfers between devices with their start and end apart: 6, of which 6 were waited for; matrix products, arithmetic and copies ran while one was open for 9% of the time, Pallas kernels for 0%

commit v1 on v0

v1 whole, which is shorter than its diff:
```python
import jax
import jax.numpy as jnp
from jax import lax
from jax.experimental import pallas as pl
from jax.experimental.pallas import tpu as pltpu
from jax.sharding import PartitionSpec as P

HEAD = 64
GROUP = 256
LAT = 8
BF = jnp.bfloat16
F32 = jnp.float32
FAR = -1e30
MIB = 1 << 20


def dot(a, b, ca, cb):
    return lax.dot_general(a, b, (((ca,), (cb,)), ((), ())), preferred_element_type=F32)


def norm_parts(values):
    center = values - jnp.mean(values, axis=-1, keepdims=True)
    spread = jnp.mean(center * center, axis=-1, keepdims=True)
    inverse = lax.rsqrt(spread + 1e-06)
    return center * inverse, inverse


def norm_back(grad, unit, inverse, gain):
    scaled = grad * gain
    inner = jnp.mean(scaled * unit, axis=-1, keepdims=True)
    return inverse * (scaled - jnp.mean(scaled, axis=-1, keepdims=True) - unit * inner)


def gelu_both(values):
    square = values * values
    inner = jnp.tanh(values * (0.7978845608028654 + 0.035677408136300125 * square))
    half = 0.5 + 0.5 * inner
    slope = values * (0.3989422804014327 + 0.05351611220494518 * square)
    return values * half, half + (1.0 - inner * inner) * slope


def split3(v):
    hi = v.astype(BF)
    mid = (v - hi.astype(F32)).astype(BF)
    low = (v - hi.astype(F32) - mid.astype(F32)).astype(BF)
    return hi, mid, low


def head_lanes(v, h):
    lane = lax.broadcasted_iota(jnp.int32, v.shape, v.ndim - 1)
    return jnp.where((lane >= h * HEAD) & (lane < (h + 1) * HEAD), v, jnp.zeros_like(v))


def whole(shape):
    return pl.BlockSpec(shape, lambda *_: (0,) * len(shape), pipeline_mode=pl.Buffered(1))


def kept(shape):
    return pl.BlockSpec(shape, lambda *_: (0,) * len(shape))


def call(body, *, grid, scalars, ins, outs, name, scratch=(), flops=0, moved=0):
    def run(*args):
        return pl.pallas_call(
            body,
            name=name,
            out_shape=[jax.ShapeDtypeStruct(s, d) for s, d, _ in outs],
            grid_spec=pltpu.PrefetchScalarGridSpec(
                num_scalar_prefetch=scalars,
                grid=grid,
                in_specs=ins,
                out_specs=[spec for _, _, spec in outs],
                scratch_shapes=list(scratch),
            ),
            compiler_params=pltpu.CompilerParams(
                dimension_semantics=("arbitrary",) * len(grid), vmem_limit_bytes=56 * MIB
            ),
            cost_estimate=pl.CostEstimate(flops=flops, bytes_accessed=moved, transcendentals=0),
        )(*args)

    return run


def key_stack(tok, lat8):
    pad = jnp.concatenate([lat8, jnp.zeros_like(lat8)], 0).astype(BF)
    return jnp.concatenate([tok, pad], 0)


def near_mask(count, columns):
    row = lax.broadcasted_iota(jnp.int32, (GROUP + 2 * LAT, columns), 0)
    return (row < count) | ((row >= GROUP) & (row < GROUP + LAT))


def forward_near(order, count, tok, lat, gain, shift, w, bias, normed, q, k, v, m0, m1, m2, m3, log, ql, kl, vl):
    step = pl.program_id(0)
    wide = w.shape[1]

    def project(rows):
        unit, _ = norm_parts(rows.astype(F32))
        rows = (unit * gain[...] + shift[...]).astype(BF)
        return (
            rows,
            (dot(rows, w[0], 1, 1) + bias[0:1]).astype(BF),
            dot(rows, w[1], 1, 1).astype(BF),
            (dot(rows, w[2], 1, 1) + bias[1:2]).astype(BF),
        )

    @pl.when(step == 0)
    def _():
        _, a, b, c = project(lat[...])
        ql[...], kl[...], vl[...] = a.astype(F32), b.astype(F32), c.astype(F32)

    rows, qs, ks, vs = project(tok[...])
    normed[...], q[...], k[...], v[...] = rows, qs, ks, vs
    here = pl.ds(pl.multiple_of(step * LAT, LAT), LAT)
    keys = key_stack(ks, kl[here, :])
    values = key_stack(vs, vl[here, :]).T
    mask = near_mask(count[step], GROUP)
    qs = qs * jnp.asarray(0.125, BF)
    logs, outs = [], []
    for h in range(wide // HEAD):
        s = jnp.where(mask, dot(head_lanes(keys, h), qs, 1, 1), FAR)
        top = jnp.max(s, 0, keepdims=True)
        e = jnp.exp(s - top)
        total = jnp.sum(e, 0, keepdims=True)
        logs.append(top + jnp.log(total))
        outs.append(dot(values[h * HEAD : (h + 1) * HEAD], e.astype(BF), 1, 0) * (1.0 / total))
    log[0] = jnp.concatenate(logs + [jnp.zeros((8 - len(logs), GROUP), F32)], 0)
    mixed = jnp.concatenate(outs, 0).T.astype(BF)
    for slot, ref in enumerate((m0, m1, m2, m3)):

        @pl.when(step // 2 == slot)
        def _(ref=ref):
            ref[...] = mixed


def forward_far(count, lat, gain, shift, w, bias, own_im, key_im, k, v, normed, qa, ka, va, m0, m1, m2, m3, far, logs_out):
    step = pl.program_id(0)
    wide = w.shape[1]
    rows_step = lat.shape[0]
    own = normed.shape[0]
    unit, _ = norm_parts(lat[...].astype(F32))
    rows = (unit * gain[...] + shift[...]).astype(BF)
    here = pl.ds(pl.multiple_of(step * rows_step, rows_step), rows_step)
    qa[here, :] = (dot(rows, w[0], 1, 1) + bias[0:1]).astype(BF)
    ka[here, :] = dot(rows, w[1], 1, 1).astype(BF)
    va[here, :] = (dot(rows, w[2], 1, 1) + bias[1:2]).astype(BF)

    @pl.when(step == 0)
    def _():
        normed[...] = rows[:own]

    @pl.when(step == pl.num_programs(0) - 1)
    def _():
        q = qa[0:own, :] * jnp.asarray(0.125, BF)
        q32 = q.astype(F32)
        groups = own // LAT
        mask = own_im[...] == key_im[...]
        lane = lax.broadcasted_iota(jnp.int32, (LAT, GROUP), 1)
        full = jnp.zeros((own, wide), F32)
        logs = []
        for h in range(wide // HEAD):
            qh = head_lanes(q32, h)
            s_lat = jnp.where(mask, dot(qh.astype(BF), ka[...], 1, 1), FAR)
            s_tok = jnp.concatenate(
                [
                    jnp.where(
                        lane < count[g],
                        dot(qh[g * LAT : (g + 1) * LAT].astype(BF), k[g * GROUP : (g + 1) * GROUP, :], 1, 1),
                        FAR,
                    )
                    for g in range(groups)
                ],
                0,
            )
            top = jnp.maximum(jnp.max(s_lat, 1, keepdims=True), jnp.max(s_tok, 1, keepdims=True))
            e_lat, e_tok = jnp.exp(s_lat - top), jnp.exp(s_tok - top)
            total = jnp.sum(e_lat, 1, keepdims=True) + jnp.sum(e_tok, 1, keepdims=True)
            logs.append(top + jnp.log(total))
            near = jnp.concatenate(
                [
                    dot(e_tok[g * LAT : (g + 1) * LAT].astype(BF), v[g * GROUP : (g + 1) * GROUP, :], 1, 0)
                    for g in range(groups)
                ],
                0,
            )
            full = full + head_lanes((dot(e_lat.astype(BF), va[...], 1, 0) + near) * (1.0 / total), h)
        mixed = full.astype(BF)
        for slot, ref in enumerate((m0, m1, m2, m3)):
            n = own // 4
            ref[...] = mixed[slot * n : (slot + 1) * n]
        parts = [split3(x) for x in logs]
        cols = [p[i] for i in range(3) for p in parts]
        lane = lax.broadcasted_iota(jnp.int32, (own, 2 * HEAD), 1)
        extra = jnp.zeros((own, 2 * HEAD), F32)
        for i, c in enumerate(cols):
            extra = jnp.where(lane == i, c.astype(F32), extra)
        far[...] = mixed
        logs_out[...] = extra.astype(BF)


def hidden_part(n2, cot, up_w, down_w, bias, branch, back, act_out, grad_out, bias_out):
    cut = 256
    for at in range(0, up_w.shape[1], cut):
        cols = slice(at, at + cut)
        wu, wd = up_w[:, cols], down_w[cols, :]
        up = dot(n2, wu, 1, 0) + bias[:, cols]
        active, slope = gelu_both(up)
        active = active.astype(BF)
        branch[...] += dot(active, wd, 1, 0)
        grad_up = (dot(cot, wd, 1, 1) * slope).astype(BF)
        back[...] += dot(grad_up, wu, 1, 1)
        act_out[:, cols] = active
        grad_out[:, cols] = grad_up
        bias_out[:, cols] = jnp.sum(grad_up.astype(F32), 0, keepdims=True)


def bias_row(pack, base):
    rows = pack[base : base + 16, :].astype(F32)
    return rows[0:1] + rows[1:2] + rows[2:3]


def valid_rows(count, at, rows):
    row = lax.broadcasted_iota(jnp.int32, (rows, 1), 0)
    first = (row < GROUP) & (row < count[at])
    return first | ((row >= GROUP) & (row < GROUP + count[at + 1]))


def middle_one(
    where, count, t0, t1, t2, t3, l0, l1, l2, l3, o0, o1, o2, o3, tok, lat, cot_tok, cot_lat, b_out, gain, shift,
    up0, down0, up1, down1, residual, n2_out, branch, back, cot, stats, bsum, pack0, pack1, act, grad,
):
    width = tok.shape[1]
    n, m = tok.shape[0], lat.shape[0]
    wide = t0.shape[1]
    attn_tok = dot(t0[...], o0[0:wide, :], 1, 0)
    attn_lat = dot(l0[...], o0[0:wide, :], 1, 0)
    for t, l, o in ((t1, l1, o1), (t2, l2, o2), (t3, l3, o3)):
        attn_tok += dot(t[...], o[0:wide, :], 1, 0)
        attn_lat += dot(l[...], o[0:wide, :], 1, 0)
    attn_tok += b_out[...]
    attn_lat += b_out[...]
    real = valid_rows(count, 0, n)
    stats[...] = jnp.zeros_like(stats)
    stats[0:1, :] = jnp.sum(jnp.where(real, attn_tok * attn_tok, 0.0), 0, keepdims=True)
    residual[0:n, :] = tok[...].astype(F32) + attn_tok
    residual[n : n + m, :] = lat[...].astype(F32) + attn_lat
    unit, _ = norm_parts(residual[...])
    n2_out[...] = (unit * gain[...] + shift[...]).astype(BF)
    cot[0:n, :] = cot_tok[...]
    cot[n : n + m, :] = cot_lat[...]
    branch[...] = jnp.zeros_like(branch)
    back[...] = jnp.zeros_like(back)
    n2, ct = n2_out[...], cot[...]
    n2_t = n2.T
    for i, (up_w, down_w, o, pack) in enumerate(((up0, down0, o0, pack0), (up1, down1, o1, pack1))):
        hidden = up_w.shape[1]
        hidden_part(n2, ct, up_w, down_w, bias_row(o, wide), branch, back, act, grad, bsum.at[i : i + 1])
        pack[0:width, :] = dot(n2_t, grad[...], 1, 0).astype(BF)
        pack[width : width + hidden, :] = dot(act[...], ct, 0, 0).astype(BF)


def middle_two(
    count, residual, n2, cot, branch_in, back_in, o0, o1, o2, o3, p2, p3, b_down, gain,
    out_rows, grad_res, g0, g1, g2, g3, grad_attn, act2, grad2, act3, grad3, stats, bsum, branch, back,
):
    width = residual.shape[1]
    wide = g0.shape[1]
    hidden = p2.shape[0] - width
    branch[...] = branch_in[...]
    back[...] = back_in[...]
    nn, ct = n2[...], cot[...]
    for i, (p, o, act, grad) in enumerate(((p2, o2, act2, grad2), (p3, o3, act3, grad3))):
        up_w, down_w = p.at[0:width], p.at[width : width + hidden]
        hidden_part(nn, ct, up_w, down_w, bias_row(o, wide), branch, back, act, grad, bsum.at[i : i + 1])
    res = residual[...]
    br = branch[...] + b_down[...]
    out = res + br
    out_rows[...] = out.astype(BF)
    tok_rows = 2 * GROUP
    real = valid_rows(count, 0, tok_rows)
    stats[...] = jnp.zeros_like(stats)
    for i, x in enumerate((out, br)):
        x = x[0:tok_rows]
        stats[i : i + 1, :] = jnp.sum(jnp.where(real, x * x, 0.0), 0, keepdims=True)
    unit, inverse = norm_parts(res)
    bk = back[...]
    stats[2:3, :] = jnp.sum(bk * unit, 0, keepdims=True)
    stats[3:4, :] = jnp.sum(bk, 0, keepdims=True)
    cot32 = ct.astype(F32)
    gr = cot32 + norm_back(bk, unit, inverse, gain[...])
    grad_res[...] = gr
    ga = gr.astype(BF)
    grad_attn[...] = ga
    stats[4:5, :] = jnp.sum(ga.astype(F32), 0, keepdims=True)
    stats[5:6, :] = jnp.sum(cot32, 0, keepdims=True)
    for o, g in ((o0, g0), (o1, g1), (o2, g2), (o3, g3)):
        g[...] = dot(ga, o[0:wide, :], 1, 1).astype(BF)


def middle_grads(n2, cot, grad_attn, t0, t1, t2, t3, l0, l1, l2, l3, act2, grad2, act3, grad3, own_out, send_out, pair_out):
    width = n2.shape[1]
    hidden = act2.shape[1]
    wide = t0.shape[1]
    tok_rows = t0.shape[0]
    n2_t = n2[...].T
    ct, ga = cot[...], grad_attn[...]

    def out_grad(t, l):
        return (dot(t[...], ga[0:tok_rows], 0, 0) + dot(l[...], ga[tok_rows:], 0, 0)).astype(BF)

    for act, grad, dst, t, l in ((act3, grad3, send_out, t3, l3), (act2, grad2, pair_out, t2, l2)):
        dst[0:width, :] = dot(n2_t, grad[...], 1, 0).astype(BF)
        dst[width : width + hidden, :] = dot(act[...], ct, 0, 0).astype(BF)
        dst[width + hidden : width + hidden + wide, :] = out_grad(t, l)
    send_out[width + hidden + wide : width + hidden + 2 * wide, :] = out_grad(t1, l1)
    own_out[...] = out_grad(t0, l0)


def backward_near(
    order, count, normed, q, k, v, ql, kl, vl, log, far, logs_far, da, db, la, lb, w,
    part, grad_w, bias, dq_far, dk_near, dv_near,
):
    step = pl.program_id(0)
    wide = q.shape[1]
    heads = wide // HEAD
    first = step < 2
    d_tok = jnp.where(first, da[...], db[...])
    d_lat16 = jnp.where(first, la[...], lb[...]).astype(F32)
    d_lat = jnp.where(step % 2 == 0, d_lat16[0:LAT], d_lat16[LAT : 2 * LAT])
    number = count[step]
    eighth = jnp.asarray(0.125, BF)
    qs, ks, vs = q[...] * eighth, k[...], v[...]
    keys, values = key_stack(ks, kl[...]), key_stack(vs, vl[...])
    keys_t = keys.T
    mask = near_mask(number, GROUP)
    ps, gs, dq_t, d_heads, q_heads = [], [], [], [], []
    for h in range(heads):
        s = dot(head_lanes(keys, h), qs, 1, 1)
        p = jnp.where(mask, jnp.exp(s - log[0, h : h + 1, :]), 0.0)
        gp = p * dot(head_lanes(values, h), d_tok, 1, 1)
        g = (gp - p * jnp.sum(gp, 0, keepdims=True)).astype(BF)
        dq_t.append(dot(keys_t[h * HEAD : (h + 1) * HEAD], g, 1, 0))
        ps.append(p.astype(BF))
        gs.append(g)
        d_heads.append(head_lanes(d_tok, h))
        q_heads.append(head_lanes(qs, h))
    dv = dot(jnp.concatenate(ps, 1), jnp.concatenate(d_heads, 0), 1, 0)
    dk = dot(jnp.concatenate(gs, 1), jnp.concatenate(q_heads, 0), 1, 0)
    dq = (jnp.concatenate(dq_t, 0).T * 0.125).astype(BF)
    pad = jnp.zeros((LAT, wide), F32)
    q8, o8 = ql[...] * 0.125, far[...].astype(F32)[0 : 2 * LAT]
    o8 = jnp.where(step % 2 == 0, o8[0:LAT], o8[LAT : 2 * LAT])
    lg = logs_far[...].astype(F32)
    lg = jnp.where(step % 2 == 0, lg[0:LAT], lg[LAT : 2 * LAT])
    q_rows, d_rows, log_col, del_col = [], [], [], []
    big = jnp.full((LAT, 1), 1e30, F32)
    zero = jnp.zeros((LAT, 1), F32)
    for h in range(heads):
        q_rows += [head_lanes(q8, h), pad]
        dh = head_lanes(d_lat, h)
        d_rows += [dh, pad]
        log_col += [lg[:, h : h + 1] + lg[:, heads + h : heads + h + 1] + lg[:, 2 * heads + h : 2 * heads + h + 1], big]
        del_col += [jnp.sum(dh * o8, 1, keepdims=True), zero]
    q_f, d_f = jnp.concatenate(q_rows, 0).astype(BF), jnp.concatenate(d_rows, 0).astype(BF)
    l_f, x_f = jnp.concatenate(log_col, 0), jnp.concatenate(del_col, 0)
    lane = lax.broadcasted_iota(jnp.int32, (2 * LAT * heads, GROUP), 1)
    p_f = jnp.where(lane < number, jnp.exp(dot(q_f, ks, 1, 1) - l_f), 0.0)
    g_f = (p_f * (dot(d_f, vs, 1, 1) - x_f)).astype(BF)
    dk_tok = (dk[0:GROUP] + dot(g_f, q_f, 0, 0)).astype(BF)
    dv_tok = (dv[0:GROUP] + dot(p_f.astype(BF), d_f, 0, 0)).astype(BF)
    dk_near[...] = dk[GROUP : GROUP + LAT]
    dv_near[...] = dv[GROUP : GROUP + LAT]
    dq_all = dot(g_f, ks, 1, 0)
    dq_lat = jnp.zeros((LAT, wide), F32)
    for h in range(heads):
        dq_lat += head_lanes(dq_all[2 * LAT * h : 2 * LAT * h + LAT], h)
    dq_far[...] = dq_lat
    rows = normed[...]

    @pl.when(step == 0)
    def _():
        grad_w[...] = jnp.zeros_like(grad_w)
        bias[...] = jnp.zeros_like(bias)

    total = dot(dq, w[0], 1, 0) + dot(dk_tok, w[1], 1, 0) + dot(dv_tok, w[2], 1, 0)
    part[...] = total.astype(BF)
    for i, g in enumerate((dq, dk_tok, dv_tok)):
        grad_w[i] += dot(g, rows, 0, 0)
    bias[0:1, :] += jnp.sum(dq.astype(F32), 0, keepdims=True)
    bias[1:2, :] += jnp.sum(dv_tok.astype(F32), 0, keepdims=True)


def backward_far(
    own_im, key_im, own_im_row, key_im_col, qa, ka, va, bundle, normed, dq_a, dq_b, dk_a, dk_b, dv_a, dv_b,
    w, gw_a, gw_b, bias_a, bias_b, part, grad_w, bias,
):
    own = normed.shape[0]
    wide = qa.shape[1]
    heads = wide // HEAD
    eighth = jnp.asarray(0.125, BF)
    q_all, k_all, v_all = qa[...] * eighth, ka[...], va[...]
    part_wide = 4 * HEAD
    d_all, o_all = bundle[:, 0:wide], bundle[:, part_wide : part_wide + wide]
    extra = bundle[:, 2 * part_wide : 2 * part_wide + 2 * HEAD].astype(F32)
    prod = d_all.astype(F32) * o_all.astype(F32)
    q_own, k_own, v_own, d_own = q_all[0:own], k_all[0:own], v_all[0:own], d_all[0:own]
    mask_q = own_im[...] == key_im[...]
    mask_k = key_im_col[...] == own_im_row[...]
    dq = jnp.concatenate([dq_a[...], dq_b[...]], 0)
    dk = jnp.concatenate([dk_a[...], dk_b[...]], 0)
    dv = jnp.concatenate([dv_a[...], dv_b[...]], 0)
    for h in range(heads):
        log = extra[:, h : h + 1] + extra[:, heads + h : heads + h + 1] + extra[:, 2 * heads + h : 2 * heads + h + 1]
        delta = jnp.sum(head_lanes(prod, h), 1, keepdims=True)
        s = dot(head_lanes(q_own, h), k_all, 1, 1)
        p = jnp.where(mask_q, jnp.exp(s - log[0:own]), 0.0)
        g = (p * (dot(head_lanes(d_own, h), v_all, 1, 1) - delta[0:own])).astype(BF)
        dq += head_lanes(dot(g, k_all, 1, 0), h)
        s = dot(q_all, head_lanes(k_own, h), 1, 1)
        p = jnp.where(mask_k, jnp.exp(s - log), 0.0)
        g = (p * (dot(d_all, head_lanes(v_own, h), 1, 1) - delta)).astype(BF)
        dk += head_lanes(dot(g, q_all, 0, 0), h)
        dv += head_lanes(dot(p.astype(BF), d_all, 0, 0), h)
    dq, dk, dv = (dq * 0.125).astype(BF), dk.astype(BF), dv.astype(BF)
    part[...] = (dot(dq, w[0], 1, 0) + dot(dk, w[1], 1, 0) + dot(dv, w[2], 1, 0)).astype(BF)
    rows = normed[...]
    for i, g in enumerate((dq, dk, dv)):
        grad_w[i] = (gw_a[i] + gw_b[i] + dot(g, rows, 0, 0)).astype(BF)
    bias[...] = bias_a[...] + bias_b[...]
    bias[0:1, :] += jnp.sum(dq.astype(F32), 0, keepdims=True)
    bias[1:2, :] += jnp.sum(dv.astype(F32), 0, keepdims=True)


def final_rows(where, tok, lat, a, b, c, grad_res, gain, out, stats):
    n, m = tok.shape[0], lat.shape[0]
    stats[...] = jnp.zeros_like(stats)
    for x, at in ((tok, slice(0, n)), (lat, slice(n, n + m))):
        grad = a[at, :].astype(F32) + b[at, :].astype(F32) + c[at, :].astype(F32)
        unit, inverse = norm_parts(x[...].astype(F32))
        out[at, :] = (grad_res[at, :] + norm_back(grad, unit, inverse, gain[...])).astype(BF)
        stats[0:1, :] += jnp.sum(grad * unit, 0, keepdims=True)
        stats[1:2, :] += jnp.sum(grad, 0, keepdims=True)


def place_rows(order, a, b, c, d, tok_out, lat_out):
    n = tok_out.shape[0]
    for i, ref in enumerate((a, b, c, d)):

        @pl.when(pl.program_id(0) == i)
        def _(ref=ref):
            tok_out[...] = ref[0:n, :]
            lat_out[...] = ref[n:, :]


def make(mesh):
    dp_size, mp_size = mesh.shape["dp"], mesh.shape["mp"]
    assert mp_size == 4
    dp_bits = [1 << i for i in range(dp_size.bit_length() - 1)]
    assert 1 << len(dp_bits) == dp_size

    def swap(v, dp_bit, mp_bit):
        pairs = [
            (d * mp_size + m, (d ^ dp_bit) * mp_size + (m ^ mp_bit))
            for d in range(dp_size)
            for m in range(mp_size)
        ]
        return lax.ppermute(v, ("dp", "mp"), pairs)

    def per_device(
        tokens,
        latents,
        image_of_group,
        token_valid,
        norm1_gain,
        norm1_shift,
        w_qkv,
        b_qv,
        w_out,
        b_out,
        norm2_gain,
        norm2_shift,
        w_up,
        b_up,
        w_down,
        b_down,
        cot_tokens,
        cot_latents,
    ):
        dp_at, mp_at = lax.axis_index("dp"), lax.axis_index("mp")
        tok_count, width = tokens.shape
        lat_count = latents.shape[0]
        groups = lat_count // LAT
        wide = w_qkv.shape[2]
        hidden = w_up.shape[1]
        tok_own, lat_own = tok_count // 4, lat_count // 4
        rows_own = tok_own + lat_own
        order = (mp_at ^ jnp.arange(4, dtype=jnp.int32)).astype(jnp.int32)
        where = jnp.reshape(mp_at, (1,)).astype(jnp.int32)
        all_lat = dp_size * lat_count

        def by_slot(v):
            return jnp.take(v.reshape((4, v.shape[0] // 4) + v.shape[1:]), order, axis=0)

        def row(v):
            return v.reshape(1, -1)

        lat_rel = by_slot(latents).reshape(lat_count, width)
        lat_all = lat_rel
        for bit in dp_bits:
            lat_all = jnp.concatenate([lat_all, swap(lat_all, bit, 0)], 0)
        bias_rows = jnp.stack(list(split3(b_up)) + [jnp.zeros((width,), BF)] * 13)
        o0 = jnp.concatenate([w_out, bias_rows], 0)
        o1 = swap(o0, 0, 1)
        o2 = swap(o0, 0, 2)
        o3 = swap(o2, 0, 1)
        pack = jnp.concatenate([w_up, w_down], 0)
        x_bit = dp_at & 1
        half = pack.shape[0] // 2
        got = swap(lax.dynamic_slice_in_dim(pack, x_bit * half, half), 0, 2)
        other = swap(got, 1, 0)
        p1 = swap(pack, 0, 1)
        p2 = jnp.where(x_bit == 0, jnp.concatenate([got, other], 0), jnp.concatenate([other, got], 0))
        p3 = swap(p2, 0, 1)

        image_abs = image_of_group.reshape(dp_size, 4, groups // 4)
        image_rel = image_abs[(dp_at ^ jnp.arange(dp_size))[:, None], order[None, :]].reshape(-1)
        key_im = jnp.repeat(image_rel, LAT)
        own_im = key_im[:lat_count]
        count = by_slot(jnp.sum(token_valid.reshape(groups, GROUP), 1)).reshape(groups).astype(jnp.int32)

        gain1, shift1, gain2, shift2 = (row(v) for v in (norm1_gain, norm1_shift, norm2_gain, norm2_shift))
        w_t = jnp.transpose(w_qkv, (0, 2, 1))
        group_rows = pl.BlockSpec((GROUP, wide), lambda i, *_: (i, 0))

        def slot_rows(s):
            return pl.BlockSpec((GROUP, wide), lambda i, *_: (jnp.clip(i - 2 * s, 0, 1), 0))

        normed, q, k, v, t0, t1, t2, t3, log, ql, kl, vl = call(
            forward_near,
            name="forward_near",
            grid=(groups,),
            scalars=2,
            ins=[
                pl.BlockSpec((GROUP, width), lambda i, order, _: (order[i // 2] * 2 + i % 2, 0)),
                kept((lat_count, width)),
                kept((1, width)),
                kept((1, width)),
                kept((3, wide, width)),
                kept((2, wide)),
            ],
            outs=[((tok_count, width), BF, pl.BlockSpec((GROUP, width), lambda i, *_: (i, 0)))]
            + [((tok_count, wide), BF, group_rows)] * 3
            + [((tok_own, wide), BF, slot_rows(s)) for s in range(4)]
            + [((groups, 8, GROUP), F32, pl.BlockSpec((1, 8, GROUP), lambda i, *_: (i, 0, 0)))]
            + [((lat_count, wide), F32, kept((lat_count, wide)))] * 3,
            flops=tok_count * (width * wide * 6 + GROUP * wide * 4),
            moved=8 << 20,
        )(order, count, tokens, lat_rel, gain1, shift1, w_t, b_qv)

        chunk = min(512, all_lat)
        normed_lat, qa, ka, va, l0, l1, l2, l3, far, far_logs = call(
            forward_far,
            name="forward_far",
            grid=(all_lat // chunk,),
            scalars=1,
            ins=[
                pl.BlockSpec((chunk, width), lambda i, *_: (i, 0)),
                kept((1, width)),
                kept((1, width)),
                whole((3, wide, width)),
                kept((2, wide)),
                kept((lat_count, 1)),
                kept((1, all_lat)),
                whole((tok_count, wide)),
                whole((tok_count, wide)),
            ],
            outs=[((lat_count, width), BF, kept((lat_count, width)))]
            + [((all_lat, wide), BF, whole((all_lat, wide)))] * 3
            + [((lat_own, wide), BF, kept((lat_own, wide)))] * 4
            + [((lat_count, wide), BF, kept((lat_count, wide)))]
            + [((lat_count, 2 * HEAD), BF, kept((lat_count, 2 * HEAD)))],
            flops=all_lat * width * wide * 6,
            moved=5 << 20,
        )(count, lat_all, gain1, shift1, w_t, b_qv, own_im[:, None], key_im[None, :], k, v)

        t1, t2, t3 = (swap(t, 0, i) for i, t in ((1, t1), (2, t2), (3, t3)))
        l1, l2, l3 = (swap(t, 0, i) for i, t in ((1, l1), (2, l2), (3, l3)))

        own_tok = pl.BlockSpec((tok_own, width), lambda i, where, _: (where[0], 0), pipeline_mode=pl.Buffered(1))
        own_lat = pl.BlockSpec((lat_own, width), lambda i, where, _: (where[0], 0), pipeline_mode=pl.Buffered(1))
        big = (rows_own, width)
        square = lambda at: pl.BlockSpec((width, hidden), lambda *_: (at, 0), pipeline_mode=pl.Buffered(1))

        def full(shape, kind):
            return (shape, kind, whole(shape))

        outs_shape = (wide + 16, width)
        residual, n2, branch, back, cot, stats1, bsum1, pack0, pack1 = call(
            middle_one,
            name="middle_one",
            grid=(1,),
            scalars=2,
            ins=[whole((tok_own, wide))] * 4
            + [whole((lat_own, wide))] * 4
            + [whole(outs_shape)] * 4
            + [own_tok, whole((lat_own, width)), own_tok, own_lat]
            + [whole((1, width))] * 3
            + [square(0), square(0), square(0), square(1)],
            outs=[
                full(big, F32),
                full(big, BF),
                full(big, F32),
                full(big, F32),
                full(big, BF),
                full((8, width), F32),
                full((2, hidden), F32),
                full((width + hidden, width), BF),
                full((width + hidden, width), BF),
            ],
            scratch=[pltpu.VMEM((rows_own, hidden), BF)] * 2,
            flops=rows_own * width * (wide * 8 + hidden * 24),
            moved=20 << 20,
        )(
            where, count, t0, t1, t2, t3, l0, l1, l2, l3, o0, o1, o2, o3, tokens, lat_rel, cot_tokens, cot_latents,
            row(b_out), gain2, shift2, w_up, w_down, p1, p1,
        )

        out_rows, grad_res, g0, g1, g2, g3, grad_attn, act2, grad2, act3, grad3, stats2, bsum2 = call(
            middle_two,
            name="middle_two",
            grid=(1,),
            scalars=1,
            ins=[whole(big)] * 5
            + [whole(outs_shape)] * 4
            + [whole((width + hidden, width))] * 2
            + [whole((1, width))] * 2,
            outs=[full(big, BF), full(big, F32)]
            + [full((rows_own, wide), BF)] * 4
            + [full(big, BF)]
            + [full((rows_own, hidden), BF)] * 4
            + [full((8, width), F32), full((2, hidden), F32)],
            scratch=[pltpu.VMEM(big, F32)] * 2,
            flops=rows_own * width * (wide * 8 + hidden * 16),
            moved=20 << 20,
        )(count, residual, n2, cot, branch, back, o0, o1, o2, o3, p2, p3, row(b_down), gain2)

        g1, g2, g3 = (swap(t, 0, i) for i, t in ((1, g1), (2, g2), (3, g3)))

        own_out, send_out, pair_out = call(
            middle_grads,
            name="middle_grads",
            grid=(1,),
            scalars=0,
            ins=[whole(big)] * 3
            + [whole((tok_own, wide))] * 4
            + [whole((lat_own, wide))] * 4
            + [whole((rows_own, hidden))] * 4,
            outs=[
                full((wide, width), BF),
                full((width + hidden + 2 * wide, width), BF),
                full((width + hidden + wide, width), BF),
            ],
            flops=rows_own * width * (wide * 8 + hidden * 8),
            moved=20 << 20,
        )(n2, cot, grad_attn, t0, t1, t2, t3, l0, l1, l2, l3, act2, grad2, act3, grad3)

        def add(a, b):
            return (a.astype(F32) + b.astype(F32)).astype(BF)

        def scatter(v, bits):
            for bit in bits:
                n = v.shape[0] // 2
                at = jnp.where((dp_at & bit) == 0, 0, 1)
                mine = lax.dynamic_slice_in_dim(v, at * n, n)
                sent = lax.dynamic_slice_in_dim(v, (1 - at) * n, n)
                v = add(mine, swap(sent, bit, 0))
            return v

        def gather(v, bits):
            for bit in bits:
                got = swap(v, bit, 0)
                v = jnp.where(
                    (dp_at & bit) == 0, jnp.concatenate([v, got], 0), jnp.concatenate([got, v], 0)
                )
            return v

        def dp_sum(v, bits):
            rows = v.shape[0]
            spare = -rows % dp_size
            if spare:
                v = jnp.concatenate([v, jnp.zeros((spare,) + v.shape[1:], v.dtype)], 0)
            return gather(scatter(v, bits), bits[::-1])[:rows]

        got1 = swap(pack1, 0, 1)
        got3 = swap(send_out, 0, 1)
        rows = width + hidden
        keep = jnp.concatenate([add(pack0, got1), add(own_out, got3[rows + wide :])], 0)
        send = add(pair_out, got3[: rows + wide])
        keep = add(keep, swap(send, 0, 2))
        cut = keep.shape[0] // 2
        part_a = dp_sum(keep[:cut], dp_bits)
        part_b = dp_sum(keep[cut:], dp_bits[1:] + dp_bits[:1])
        sums = jnp.concatenate([part_a, part_b], 0).astype(F32)
        grad_w_up, grad_w_down, grad_w_out = sums[:width], sums[width:rows], sums[rows:]

        zeros = jnp.zeros((lat_count, HEAD), BF)
        d_lat = jnp.concatenate([g[tok_own:] for g in (g0, g1, g2, g3)], 0)
        bundle = jnp.concatenate([d_lat, zeros, far, zeros, far_logs], 1)
        for bit in dp_bits:
            bundle = jnp.concatenate([bundle, swap(bundle, bit, 0)], 0)

        def near(at, da, db):
            four = 4 * at
            tok_block = lambda which: pl.BlockSpec(
                (GROUP, wide), lambda i, *_: (jnp.clip(i - 2 * which, 0, 1), 0)
            )
            lat_block = pl.BlockSpec((lat_own, wide), lambda *_: (tok_own // lat_own, 0))
            eight = pl.BlockSpec((LAT, wide), lambda i, *_: (i + four, 0))
            return call(
                backward_near,
                name="backward_near",
                grid=(4,),
                scalars=2,
                ins=[
                    pl.BlockSpec((GROUP, width), lambda i, *_: (i + four, 0)),
                    *[pl.BlockSpec((GROUP, wide), lambda i, *_: (i + four, 0))] * 3,
                    eight,
                    eight,
                    eight,
                    pl.BlockSpec((1, 8, GROUP), lambda i, *_: (i + four, 0, 0)),
                    pl.BlockSpec((2 * LAT, wide), lambda i, *_: ((i + four) // 2, 0)),
                    pl.BlockSpec((2 * LAT, 2 * HEAD), lambda i, *_: ((i + four) // 2, 0)),
                    tok_block(0),
                    tok_block(1),
                    lat_block,
                    lat_block,
                    kept((3, wide, width)),
                ],
                outs=[
                    ((4 * GROUP, width), BF, pl.BlockSpec((GROUP, width), lambda i, *_: (i, 0))),
                    ((3, wide, width), F32, kept((3, wide, width))),
                    ((8, wide), F32, kept((8, wide))),
                    *[((4 * LAT, wide), F32, pl.BlockSpec((LAT, wide), lambda i, *_: (i, 0)))] * 3,
                ],
                flops=4 * GROUP * (width * wide * 12 + GROUP * wide * 10),
                moved=10 << 20,
            )(order, count[four : four + 4], normed, q, k, v, ql, kl, vl, log, far, far_logs, da, db, da, db, w_t)

        part_a1, gw_a, bias_a, dq_a, dk_a, dv_a = near(0, g0, g1)
        part_b1, gw_b, bias_b, dq_b, dk_b, dv_b = near(1, g2, g3)
        part_lat, grad_w, bias = call(
            backward_far,
            name="backward_far",
            grid=(1,),
            scalars=0,
            ins=[
                whole((lat_count, 1)),
                whole((1, all_lat)),
                whole((1, lat_count)),
                whole((all_lat, 1)),
                *[whole((all_lat, wide))] * 3,
                whole((all_lat, 10 * HEAD)),
                whole((lat_count, width)),
                *[whole((lat_count // 2, wide))] * 6,
                whole((3, wide, width)),
                *[whole((3, wide, width))] * 2,
                *[whole((8, wide))] * 2,
            ],
            outs=[full((lat_count, width), BF), full((3, wide, width), BF), full((8, wide), F32)],
            flops=all_lat * lat_count * wide * 14,
            moved=10 << 20,
        )(
            own_im[:, None], key_im[None, :], own_im[None, :], key_im[:, None], qa, ka, va, bundle, normed_lat,
            dq_a, dq_b, dk_a, dk_b, dv_a, dv_b, w_t, gw_a, gw_b, bias_a, bias_b,
        )

        grad_w = grad_w.reshape(3 * wide, width)
        cut = 3 * wide // 2
        gw = [dp_sum(grad_w[:cut], dp_bits), dp_sum(grad_w[cut:], dp_bits[1:] + dp_bits[:1])]
        grad_w_qkv = jnp.concatenate(gw, 0).astype(F32).reshape(3, wide, width).transpose(0, 2, 1)

        def slot_part(s):
            tok = (part_a1, part_b1)[s // 2][(s % 2) * tok_own : (s % 2 + 1) * tok_own]
            return jnp.concatenate([tok, part_lat[s * lat_own : (s + 1) * lat_own]], 0)

        got = swap(jnp.concatenate([slot_part(1), slot_part(3)], 0), 0, 1)
        there = add(slot_part(2), got[rows_own:])
        from_y = swap(there, 0, 2)
        grad_rows, stats3 = call(
            final_rows,
            name="final_rows",
            grid=(1,),
            scalars=1,
            ins=[
                pl.BlockSpec((tok_own, width), lambda i, where: (where[0], 0), pipeline_mode=pl.Buffered(1)),
                whole((lat_own, width)),
                *[whole(big)] * 4,
                whole((1, width)),
            ],
            outs=[full(big, BF), full((8, width), F32)],
            moved=8 << 20,
        )(where, tokens, lat_rel, slot_part(0), got[:rows_own], from_y, grad_res, gain1)

        def all_rows(v):
            v_y = swap(v, 0, 2)
            v_c = swap(v, 0, 1)
            v_yc = swap(v_y, 0, 1)
            return call(
                place_rows,
                name="place_rows",
                grid=(4,),
                scalars=1,
                ins=[kept(big)] * 4,
                outs=[
                    ((tok_count, width), BF, pl.BlockSpec((tok_own, width), lambda i, order: (order[i], 0))),
                    ((lat_count, width), BF, pl.BlockSpec((lat_own, width), lambda i, order: (order[i], 0))),
                ],
                moved=8 << 20,
            )(order, v, v_c, v_y, v_yc)

        out_tok, out_lat = all_rows(out_rows)
        grad_tok, grad_lat = all_rows(grad_rows)

        def place(v):
            return lax.dynamic_update_slice_in_dim(jnp.zeros((4 * wide,), F32), v, mp_at * wide, 0)

        bias_up = jnp.concatenate([bsum1, bsum2], 0)
        small = jnp.concatenate(
            [
                stats1[:1],
                stats2[:6],
                stats3[:2],
                place(bias[0])[None],
                place(bias[1])[None],
                jnp.take(bias_up, order, axis=0),
                jnp.full((1, width), 0.25 * jnp.sum(token_valid).astype(F32)),
            ],
            0,
        )
        for bit in (1, 2):
            small = small + swap(small, 0, bit)
        for bit in dp_bits:
            small = small + swap(small, bit, 0)
        squares = jnp.sum(jnp.stack([small[1], small[0], small[2]]), 1)
        root_means = jnp.sqrt(squares / (small[15, 0] * width))
        grad_b_qv = lax.dynamic_slice_in_dim(small[9:11], mp_at * wide, wide, 1)
        grad_b_up = lax.dynamic_index_in_dim(small[11:15], mp_at, 0, keepdims=False)
        return (
            out_tok,
            out_lat,
            grad_tok,
            grad_lat,
            small[7],
            small[8],
            grad_w_qkv,
            grad_b_qv,
            grad_w_out,
            small[5],
            small[3],
            small[4],
            grad_w_up,
            grad_b_up,
            grad_w_down,
            small[6],
            root_means,
        )

    return per_device


def solution(mesh):
    rows, whole = P("dp", None), P()
    return jax.shard_map(
        make(mesh),
        mesh=mesh,
        in_specs=(
            rows,
            rows,
            whole,
            P("dp"),
            whole,
            whole,
            P(None, None, "mp"),
            P(None, "mp"),
            P("mp", None),
            whole,
            whole,
            whole,
            P(None, "mp"),
            P("mp"),
            P("mp", None),
            whole,
            rows,
            rows,
        ),
        out_specs=(
            rows,
            rows,
            rows,
            rows,
            whole,
            whole,
            P(None, None, "mp"),
            P(None, "mp"),
            P("mp", None),
            whole,
            whole,
            whole,
            P(None, "mp"),
            P("mp"),
            P("mp", None),
            whole,
            whole,
        ),
        check_vma=False,
    )
```

time: 844 us -> 407 us (0.48)
  waiting for transfers between devices: 514 us -> 154 us
  Pallas kernels: 0 us -> 114 us
  blocking collectives: 104 us -> 0 us
  matrix products: 80.5 us -> 0 us
  starting transfers between devices: 1.66 us -> 55.6 us
  other arithmetic: 68.5 us -> 35.4 us
  local copies, waits for them, and re-layouts: 53.7 us -> 40.5 us
  between operations: 16.2 us -> 3.33 us
    psum x4 -> x0, waiting for transfers between devices: 406 us -> none  [the longest x3 227 us: reduce_rows(): return lax.psum(partial_rows.astype(jnp.bfloat16), 'mp').astype(jnp.float32)]
    ppermute x0 -> x62, waiting for transfers between devices: none -> 154 us  [swap(): return lax.ppermute(v, ('dp', 'mp'), pairs)]
    pallas_call x0 -> x11, Pallas kernels: none -> 114 us  [run(): pl.pallas_call(body, name=name, out_shape=[jax.ShapeDtypeStruct(s, d) for...]
    unnamed x8 -> x0, waiting for transfers between devices: 108 us -> none
    dot_general x23 -> x0, matrix products: 78 us -> none  [the longest x1 9.93 us: per_device(): jnp.einsum('rd,fd->rf', cot_rows, w_down, preferred_element_type=jnp.floa...]
    all_gather x2 -> x0, blocking collectives: 63.5 us -> none  [the longest x1 32.5 us: per_device(): lax.all_gather(lat_values, 'dp', axis=0, tiled=True)]
    ppermute x0 -> x62, starting transfers between devices: none -> 55.6 us  [swap(): return lax.ppermute(v, ('dp', 'mp'), pairs)]
    reduce_sum x16 -> x3, other arithmetic: 53.5 us -> 0.91 us  [the longest x1 0.66 us: per_device(): jnp.sum(token_valid).astype(F32)]
  transfers between devices with their start and end apart: 6 -> 62, of which waited for: 6 -> 28; matrix products, arithmetic and copies ran while one was open for 9% -> 15% of each run, Pallas kernels for 0% -> 28%
where the time goes in v1:
time: 407 us; the launch traced here: 403 us
  waiting for transfers between devices  154 us (38%)
  Pallas kernels  114 us (28%)
  starting transfers between devices  55.6 us (14%)
  local copies, waits for them, and re-layouts  40.5 us (10%)
  other arithmetic  35.4 us (9%)
    ppermute x62, waiting for transfers between devices, swap(): return lax.ppermute(v, ('dp', 'mp'), pairs)  154 us
    pallas_call x11, Pallas kernels, run(): pl.pallas_call(body, name=name, out_shape=[jax.ShapeDtypeStruct(s, d) for...  114 us
    ppermute x62, starting transfers between devices, swap(): return lax.ppermute(v, ('dp', 'mp'), pairs)  55.6 us
    convert_element_type x17, other arithmetic, add(): return (a.astype(F32) + b.astype(F32)).astype(BF)  15 us
  transfers between devices with their start and end apart: 62, of which 28 were waited for; matrix products, arithmetic and copies ran while one was open for 15% of the time, Pallas kernels for 28%

profile of v1, /device:TPU:0, one launch (start us, length us, event | category | flops | bytes accessed | tf_op | source)
XLA Modules:
  0.0 402.8 jit_solution(4839063542459678261)
XLA Ops:
  4.6 3.0 collective-permute-start.13
  10.7 23.1 %collective-permute-done.13 = bf16[768,768]{1,0:T(8,128)(2,1)} collective-permute-done((bf16[768,768]{1,0:T(8,128)(2,1)}, bf16[768,768]{1,0:T(8,128)(2,1)}, u32[]{:S(2)}, u32[]{:S(2)}) %collective-permute-start.13) | collective-permute-done | bytes 1179680 | tf_op jit(solution)/shard_map/ppermute | solution.py:468
  38.0 17.5 %forward_near.1 = (bf16[2048,768]{1,0:T(8,128)(2,1)}, bf16[2048,192]{1,0:T(8,128)(2,1)}, bf16[2048,192]{1,0:T(8,128)(2,1)}, bf16[2048,192]{1,0:T(8,128)(2,1)}, b...) custom-call(s32[4]{0:T(128)} %get-tuple-element.190.order, ...), custom_call_target="tpu_custom_call" | custom-call | flops 2214592512 | bytes 8388608 | tf_op jit(solution)/shard_map/forward_near/pallas_call | solution.py:64
  74.9 4.1 %maximum_select_fusion.p2 = bf16[1536,768]{1,0:T(8,128)(2,1)} fusion(bf16[768,768]{1,0:T(8,128)(2,1)} %collective-permute-done.14, bf16[768,768]{1,0:T(8,128)(2,1)} %collective-permute-done.13, pred[]{:T(512)S(6)} %eq.6), kind=kLoop, calls=%fused_computation.7 | loop fusion | flops 10616832 | bytes 4718593 | tf_op jit(solution)/shard_map/jit(_where)/select_n | solution.py:523
  79.0 7.1 %collective-permute-done.5 = bf16[256,768]{1,0:T(8,128)(2,1)S(1)} collective-permute-done((bf16[256,768]{1,0:T(8,128)(2,1)S(1)}, bf16[256,768]{1,0:T(8,128)(2,1)S(1)}, u32[]{:S(2)}, u32[]{:S(2)}) %collective-permute-start.5) | collective-permute-done | bytes 393248 | tf_op jit(solution)/shard_map/ppermute | solution.py:468
  87.1 6.4 %forward_far.1 = (bf16[64,768]{1,0:T(8,128)(2,1)}, bf16[512,192]{1,0:T(8,128)(2,1)}, bf16[512,192]{1,0:T(8,128)(2,1)}, bf16[512,192]{1,0:T(8,128)(2,1)}, bf16[16...) custom-call(s32[8]{0:T(128)} %select_n.248.count, ...), custom_call_target="tpu_custom_call" | custom-call | flops 452984832 | bytes 5242880 | tf_op jit(solution)/shard_map/forward_far/pallas_call | solution.py:64
  99.6 17.6 %middle_one.1 = (f32[528,768]{1,0:T(8,128)}, bf16[528,768]{1,0:T(8,128)(2,1)}, f32[528,768]{1,0:T(8,128)}, f32[528,768]{1,0:T(8,128)}, bf16[528,768]{1,0:T(8,128...) custom-call(s32[1]{0:T(128)} %bitcast.1.where, ...), custom_call_target="tpu_custom_call" | custom-call | flops 8097103872 | bytes 20971520 | tf_op jit(solution)/shard_map/middle_one/pallas_call | solution.py:64
  122.6 15.1 %middle_two.1 = (bf16[528,768]{1,0:T(8,128)(2,1)}, f32[528,768]{1,0:T(8,128)}, bf16[528,192]{1,0:T(8,128)(2,1)}, bf16[528,192]{1,0:T(8,128)(2,1)}, bf16[528,192]...) custom-call(s32[8]{0:T(128)} %select_n.248.count, ...), custom_call_target="tpu_custom_call" | custom-call | flops 5605687296 | bytes 20971520 | tf_op jit(solution)/shard_map/middle_two/pallas_call | solution.py:64
  139.9 10.8 %middle_grads.1 = (bf16[192,768]{1,0:T(8,128)(2,1)}, bf16[1920,768]{1,0:T(8,128)(2,1)}, bf16[1728,768]{1,0:T(8,128)(2,1)}) custom-call(bf16[528,768]{1,0:T(8,128)(2,1)} %get-tuple-element.96.n2, bf16[528,768]{1,0:T(8,128)(2,1)} %get-tuple-element.97.cot, bf16[528,768]{1,0:T(8,128)(2,1)} %get-tuple-element.145.grad_attn, ...), custom_call_target="tpu_custom_call" | custom-call | flops 3114270720 | bytes 20971520 | tf_op jit(solution)/shard_map/middle_grads/pallas_call | solution.py:64
  156.9 12.9 %backward_near.3 = (bf16[1024,768]{1,0:T(8,128)(2,1)}, f32[3,192,768]{2,1,0:T(8,128)}, f32[8,192]{1,0:T(8,128)}, f32[32,192]{1,0:T(8,128)}, f32[32,192]{1,0:T(8,128)}, /*index=5*/f32[32,192]{1,0:T(8,128)}) custom-call(s32[4]{0:T(128)} %get-tuple-element.190.order, s32[4]{0:T(128)} %slice.150.count, bf16[2048,768]{1,0:T(8,128)(2,1)} %get-tuple-element.103.normed, ...), custom_call_target="tpu_custom_call" | custom-call | flops 2315255808 | bytes 10485760 | tf_op jit(solution)/shard_map/backward_near/pallas_call | solution.py:64
  173.0 3.4 collective-permute-done.23
  178.8 12.9 %backward_near.2 = (bf16[1024,768]{1,0:T(8,128)(2,1)}, f32[3,192,768]{2,1,0:T(8,128)}, f32[8,192]{1,0:T(8,128)}, f32[32,192]{1,0:T(8,128)}, f32[32,192]{1,0:T(8,128)}, /*index=5*/f32[32,192]{1,0:T(8,128)}) custom-call(s32[4]{0:T(128)} %get-tuple-element.190.order, s32[4]{0:T(128)} %slice.143.count, bf16[2048,768]{1,0:T(8,128)(2,1)} %get-tuple-element.103.normed, ...), custom_call_target="tpu_custom_call" | custom-call | flops 2315255808 | bytes 10485760 | tf_op jit(solution)/shard_map/backward_near/pallas_call | solution.py:64
  194.5 6.4 %backward_far.1 = (bf16[64,768]{1,0:T(8,128)(2,1)}, bf16[3,192,768]{2,1,0:T(8,128)(2,1)}, f32[8,192]{1,0:T(8,128)}) custom-call(s32[64,1]{1,0:T(8,128)} %broadcast_in_dim.80.own_im, s32[1,512]{1,0:T(1,128)} %broadcast_in_dim_reshape.7.key_im, s32[1,64]{1,0:T(1,128)} %broadcast_in_dim.74.own_im_row, s32[512,1]{1,0:T(8,128)} %broadcast_in_dim_reshape.9.key_im_col, ...), custom_call_target="tpu_custom_call" | custom-call | flops 88080384 | bytes 10485760 | tf_op jit(solution)/shard_map/backward_far/pallas_call | solution.py:64
  206.2 3.9 add_convert_fusion.1
  215.2 4.8 %collective-permute-done.41 = bf16[144,768]{1,0:T(8,128)(2,1)} collective-permute-done((bf16[144,768]{1,0:T(8,128)(2,1)}, bf16[144,768]{1,0:T(8,128)(2,1)}, u32[]{:S(2)}, u32[]{:S(2)}) %collective-permute-start.41) | collective-permute-done | bytes 221216 | tf_op jit(solution)/shard_map/ppermute | solution.py:468
  224.1 4.6 %collective-permute-done.42 = bf16[72,768]{1,0:T(8,128)(2,1)S(1)} collective-permute-done((bf16[72,768]{1,0:T(8,128)(2,1)S(1)}, bf16[72,768]{1,0:T(8,128)(2,1)S(1)}, u32[]{:S(2)}, u32[]{:S(2)}) %collective-permute-start.42) | collective-permute-done | bytes 110624 | tf_op jit(solution)/shard_map/ppermute | solution.py:468
  230.3 2.8 collective-permute-done.43
  241.6 29.2 %collective-permute-done.49 = bf16[1728,768]{1,0:T(8,128)(2,1)} collective-permute-done((bf16[1728,768]{1,0:T(8,128)(2,1)}, bf16[1728,768]{1,0:T(8,128)(2,1)}, u32[]{:S(2)}, u32[]{:S(2)}) %collective-permute-start.49) | collective-permute-done | bytes 2654240 | tf_op jit(solution)/shard_map/ppermute | solution.py:468
  277.2 5.3 %collective-permute-done.45 = bf16[72,768]{1,0:T(8,128)(2,1)S(1)} collective-permute-done((bf16[72,768]{1,0:T(8,128)(2,1)S(1)}, bf16[72,768]{1,0:T(8,128)(2,1)S(1)}, u32[]{:S(2)}, u32[]{:S(2)}) %collective-permute-start.45) | collective-permute-done | bytes 110624 | tf_op jit(solution)/shard_map/ppermute | solution.py:468
  288.3 4.8 %final_rows.1 = (bf16[528,768]{1,0:T(8,128)(2,1)}, f32[8,768]{1,0:T(8,128)}) custom-call(s32[1]{0:T(128)} %bitcast.1.where, bf16[2048,768]{1,0:T(8,128)(2,1)} %tok.5, bf16[64,768]{1,0:T(8,128)(2,1)} %copy-done.4, bf16[528,768]{1,0:T(8,128)(2,1)} %pad_maximum_fusion.3.a, bf16[528,768]{1,0:T(8,128)(2,1)} %slice.199.b, bf16[528,768]{1,0:T(8,128)(2,1)} %copy-done.22, ...), custom_call_target="tpu_custom_call" | custom-call | bytes 8388608 | tf_op jit(solution)/shard_map/final_rows/pallas_call | solution.py:64
  302.3 3.2 collective-permute-done.32
  307.6 5.5 %collective-permute-done.56 = bf16[432,768]{1,0:T(8,128)(2,1)} collective-permute-done((bf16[432,768]{1,0:T(8,128)(2,1)}, bf16[432,768]{1,0:T(8,128)(2,1)}, u32[]{:S(2)}, u32[]{:S(2)}) %collective-permute-start.56) | collective-permute-done | bytes 663584 | tf_op jit(solution)/shard_map/ppermute | solution.py:468
  316.2 5.5 %collective-permute-done.51 = bf16[216,768]{1,0:T(8,128)(2,1)S(1)} collective-permute-done((bf16[216,768]{1,0:T(8,128)(2,1)S(1)}, bf16[216,768]{1,0:T(8,128)(2,1)S(1)}, u32[]{:S(2)}, u32[]{:S(2)}) %collective-permute-start.51) | collective-permute-done | bytes 331808 | tf_op jit(solution)/shard_map/ppermute | solution.py:468
  324.5 13.2 %collective-permute-done.57 = bf16[216,768]{1,0:T(8,128)(2,1)S(1)} collective-permute-done((bf16[216,768]{1,0:T(8,128)(2,1)S(1)}, bf16[216,768]{1,0:T(8,128)(2,1)S(1)}, u32[]{:S(2)}, u32[]{:S(2)}) %collective-permute-start.57) | collective-permute-done | bytes 331808 | tf_op jit(solution)/shard_map/ppermute | solution.py:468
  337.8 9.9 %collective-permute-done.52 = bf16[108,768]{1,0:T(8,128)(2,1)S(1)} collective-permute-done((bf16[108,768]{1,0:T(8,128)(2,1)S(1)}, bf16[108,768]{1,0:T(8,128)(2,1)S(1)}, u32[]{:S(2)}, u32[]{:S(2)}) %collective-permute-start.52) | collective-permute-done | bytes 165920 | tf_op jit(solution)/shard_map/ppermute | solution.py:468
  349.2 4.0 collective-permute-done.58
  355.1 6.9 %collective-permute-done.53 = bf16[108,768]{1,0:T(8,128)(2,1)S(1)} collective-permute-done((bf16[108,768]{1,0:T(8,128)(2,1)S(1)}, bf16[108,768]{1,0:T(8,128)(2,1)S(1)}, u32[]{:S(2)}, u32[]{:S(2)}) %collective-permute-start.53) | collective-permute-done | bytes 165920 | tf_op jit(solution)/shard_map/ppermute | solution.py:468
  367.6 4.7 %place_rows.2 = (bf16[2048,768]{1,0:T(8,128)(2,1)}, bf16[64,768]{1,0:T(8,128)(2,1)}) custom-call(s32[4]{0:T(128)} %get-tuple-element.190.order, bf16[528,768]{1,0:T(8,128)(2,1)} %get-tuple-element.100.a, bf16[528,768]{1,0:T(8,128)(2,1)} %copy-done.18, bf16[528,768]{1,0:T(8,128)(2,1)} %collective-permute-done.17.c, bf16[528,768]{1,0:T(8,128)(2,1)} %copy-done.19), custom_call_target="tpu_custom_call" | custom-call | bytes 8388608 | tf_op jit(solution)/shard_map/place_rows/pallas_call | solution.py:64
  374.7 4.1 %collective-permute-done.54 = bf16[216,768]{1,0:T(8,128)(2,1)S(1)} collective-permute-done((bf16[216,768]{1,0:T(8,128)(2,1)S(1)}, bf16[216,768]{1,0:T(8,128)(2,1)S(1)}, u32[]{:S(2)}, u32[]{:S(2)}) %collective-permute-start.54) | collective-permute-done | bytes 331808 | tf_op jit(solution)/shard_map/ppermute | solution.py:468
  379.0 3.2 collective-permute-start.55
  386.3 4.7 %place_rows.3 = (bf16[2048,768]{1,0:T(8,128)(2,1)}, bf16[64,768]{1,0:T(8,128)(2,1)}) custom-call(s32[4]{0:T(128)} %get-tuple-element.190.order, bf16[528,768]{1,0:T(8,128)(2,1)} %get-tuple-element.133.a, bf16[528,768]{1,0:T(8,128)(2,1)} %copy-done.20, bf16[528,768]{1,0:T(8,128)(2,1)} %copy-done.17, bf16[528,768]{1,0:T(8,128)(2,1)} %copy-done.21), custom_call_target="tpu_custom_call" | custom-call | bytes 8388608 | tf_op jit(solution)/shard_map/place_rows/pallas_call | solution.py:64
  391.0 5.6 %collective-permute-done.55 = bf16[432,768]{1,0:T(8,128)(2,1)S(1)} collective-permute-done((bf16[432,768]{1,0:T(8,128)(2,1)S(1)}, bf16[432,768]{1,0:T(8,128)(2,1)S(1)}, u32[]{:S(2)}, u32[]{:S(2)}) %collective-permute-start.55) | collective-permute-done | bytes 663584 | tf_op jit(solution)/shard_map/ppermute | solution.py:468
  (344 shorter events, 133.1 us)
Async XLA Ops:
  4.6 29.2 %collective-permute-start.13 = (bf16[768,768]{1,0:T(8,128)(2,1)}, bf16[768,768]{1,0:T(8,128)(2,1)}, u32[]{:S(2)}, u32[]{:S(2)}) collective-permute-start(bf16[768,768]{1,0:T(8,128)(2,1)} %constant_dynamic-slice_fusion.14), channel_id=1, source_target_pairs={{0,2},{1,3},{2,0},{3,1},{4,6},{5,7},{6,4},{7,5},{8,10},{9,11},{10,... | collective-permute-start | bytes 3538952 | tf_op jit(solution)/shard_map/ppermute | solution.py:468
  7.5 91.5 %collective-permute-start.12 = (bf16[1536,768]{1,0:T(8,128)(2,1)S(1)}, bf16[1536,768]{1,0:T(8,128)(2,1)}, u32[]{:S(2)}, u32[]{:S(2)}) collective-permute-start(bf16[1536,768]{1,0:T(8,128)(2,1)S(1)} %constant_dynamic-update-slice_fusion), channel_id=1, source_target_pairs={{0,1},{1,0},{2,3},{3,2},{4,5},{5,4},{6,7},{7,6},{8,9},{9,8},{10,11... | collective-permute-start | bytes 7077896 | tf_op jit(solution)/shard_map/ppermute | solution.py:468
  8.4 48.8 %collective-permute-start.3 = (bf16[64,768]{1,0:T(8,128)(2,1)S(1)}, bf16[64,768]{1,0:T(8,128)(2,1)S(1)}, u32[]{:S(2)}, u32[]{:S(2)}) collective-permute-start(bf16[64,768]{1,0:T(8,128)(2,1)S(1)} %bitcast_select_fusion.lat), channel_id=1, source_target_pairs={{0,4},{1,5},{2,6},{3,7},{4,0},{5,1},{6,2},{7,3},{8,12},{9,13},{10,... | collective-permute-start | bytes 294920 | tf_op jit(solution)/shard_map/ppermute | solution.py:468
  33.8 40.5 %collective-permute-start.14 = (bf16[768,768]{1,0:T(8,128)(2,1)}, bf16[768,768]{1,0:T(8,128)(2,1)}, u32[]{:S(2)}, u32[]{:S(2)}) collective-permute-start(bf16[768,768]{1,0:T(8,128)(2,1)} %collective-permute-done.13), channel_id=1, source_target_pairs={{0,4},{1,5},{2,6},{3,7},{4,0},{5,1},{6,2},{7,3},{8,12},{9,13},{10,... | collective-permute-start | bytes 3538952 | tf_op jit(solution)/shard_map/ppermute | solution.py:468
  66.6 19.6 %collective-permute-start.5 = (bf16[256,768]{1,0:T(8,128)(2,1)S(1)}, bf16[256,768]{1,0:T(8,128)(2,1)S(1)}, u32[]{:S(2)}, u32[]{:S(2)}) collective-permute-start(bf16[256,768]{1,0:T(8,128)(2,1)S(1)} %pad_maximum_fusion.6), channel_id=1, source_target_pairs={{0,16},{1,17},{2,18},{3,19},{4,20},{5,21},{6,22},{7,23},{8,24},{9,... | collective-permute-start | bytes 1179656 | tf_op jit(solution)/shard_map/ppermute | solution.py:468
  71.9 22.2 %collective-permute-start.9 = (bf16[208,768]{1,0:T(8,128)(2,1)}, bf16[208,768]{1,0:T(8,128)(2,1)S(1)}, u32[]{:S(2)}, u32[]{:S(2)}) collective-permute-start(bf16[208,768]{1,0:T(8,128)(2,1)} %concatenate.151.o0), channel_id=1, source_target_pairs={{0,1},{1,0},{2,3},{3,2},{4,5},{5,4},{6,7},{7,6},{8,9},{9,8},{10,11... | collective-permute-start | bytes 958472 | tf_op jit(solution)/shard_map/ppermute | solution.py:468
  74.3 19.2 %collective-permute-start.2 = (bf16[512,192]{1,0:T(8,128)(2,1)}, bf16[512,192]{1,0:T(8,128)(2,1)S(1)}, u32[]{:S(2)}, u32[]{:S(2)}) collective-permute-start(bf16[512,192]{1,0:T(8,128)(2,1)} %get-tuple-element.88), channel_id=1, source_target_pairs={{0,3},{1,2},{2,1},{3,0},{4,7},{5,6},{6,5},{7,4},{8,11},{9,10},{10,... | collective-permute-start | bytes 589832 | tf_op jit(solution)/shard_map/ppermute | solution.py:468
  74.3 21.3 %collective-permute-start.11 = (bf16[208,768]{1,0:T(8,128)(2,1)}, bf16[208,768]{1,0:T(8,128)(2,1)S(1)}, u32[]{:S(2)}, u32[]{:S(2)}) collective-permute-start(bf16[208,768]{1,0:T(8,128)(2,1)} %collective-permute-done.10.o2), channel_id=1, source_target_pairs={{0,1},{1,0},{2,3},{3,2},{4,5},{5,4},{6,7},{7,6},{8,9},{9,8},{10,11... | collective-permute-start | bytes 958472 | tf_op jit(solution)/shard_map/ppermute | solution.py:468
  86.1 36.5 %collective-permute-start.15 = (bf16[1536,768]{1,0:T(8,128)(2,1)}, bf16[1536,768]{1,0:T(8,128)(2,1)}, u32[]{:S(2)}, u32[]{:S(2)}) collective-permute-start(bf16[1536,768]{1,0:T(8,128)(2,1)} %maximum_select_fusion.p2), channel_id=1, source_target_pairs={{0,1},{1,0},{2,3},{3,2},{4,5},{5,4},{6,7},{7,6},{8,9},{9,8},{10,11... | collective-permute-start | bytes 7077896 | tf_op jit(solution)/shard_map/ppermute | solution.py:468
  117.2 33.6 %collective-permute-start.47 = (bf16[1536,768]{1,0:T(8,128)(2,1)}, bf16[1536,768]{1,0:T(8,128)(2,1)S(1)}, u32[]{:S(2)}, u32[]{:S(2)}) collective-permute-start(bf16[1536,768]{1,0:T(8,128)(2,1)} %get-tuple-element.144), channel_id=1, source_target_pairs={{0,1},{1,0},{2,3},{3,2},{4,5},{5,4},{6,7},{7,6},{8,9},{9,8},{10,11... | collective-permute-start | bytes 7077896 | tf_op jit(solution)/shard_map/ppermute | solution.py:468
  137.7 18.4 %collective-permute-start.20 = (bf16[528,192]{1,0:T(8,128)(2,1)}, bf16[528,192]{1,0:T(8,128)(2,1)S(1)}, u32[]{:S(2)}, u32[]{:S(2)}) collective-permute-start(bf16[528,192]{1,0:T(8,128)(2,1)} %get-tuple-element.117), channel_id=1, source_target_pairs={{0,2},{1,3},{2,0},{3,1},{4,6},{5,7},{6,4},{7,5},{8,10},{9,11},{10,... | collective-permute-start | bytes 608264 | tf_op jit(solution)/shard_map/ppermute | solution.py:468
  138.3 17.8 %collective-permute-start.21 = (bf16[528,192]{1,0:T(8,128)(2,1)}, bf16[528,192]{1,0:T(8,128)(2,1)S(1)}, u32[]{:S(2)}, u32[]{:S(2)}) collective-permute-start(bf16[528,192]{1,0:T(8,128)(2,1)} %get-tuple-element.118), channel_id=1, source_target_pairs={{0,3},{1,2},{2,1},{3,0},{4,7},{5,6},{6,5},{7,4},{8,11},{9,10},{10,... | collective-permute-start | bytes 608264 | tf_op jit(solution)/shard_map/ppermute | solution.py:468
  139.5 16.5 %collective-permute-start.19 = (bf16[528,192]{1,0:T(8,128)(2,1)}, bf16[528,192]{1,0:T(8,128)(2,1)S(1)}, u32[]{:S(2)}, u32[]{:S(2)}) collective-permute-start(bf16[528,192]{1,0:T(8,128)(2,1)} %get-tuple-element.112), channel_id=1, source_target_pairs={{0,1},{1,0},{2,3},{3,2},{4,5},{5,4},{6,7},{7,6},{8,9},{9,8},{10,11... | collective-permute-start | bytes 608264 | tf_op jit(solution)/shard_map/ppermute | solution.py:468
  150.6 55.6 %collective-permute-start.48 = (bf16[1920,768]{1,0:T(8,128)(2,1)}, bf16[1920,768]{1,0:T(8,128)(2,1)}, u32[]{:S(2)}, u32[]{:S(2)}) collective-permute-start(bf16[1920,768]{1,0:T(8,128)(2,1)} %get-tuple-element.151), channel_id=1, source_target_pairs={{0,1},{1,0},{2,3},{3,2},{4,5},{5,4},{6,7},{7,6},{8,9},{9,8},{10,11... | collective-permute-start | bytes 8847368 | tf_op jit(solution)/shard_map/ppermute | solution.py:468
  150.8 148.0 %collective-permute-start.17 = (bf16[528,768]{1,0:T(8,128)(2,1)}, bf16[528,768]{1,0:T(8,128)(2,1)}, u32[]{:S(2)}, u32[]{:S(2)}) collective-permute-start(bf16[528,768]{1,0:T(8,128)(2,1)} %get-tuple-element.100.a), channel_id=1, source_target_pairs={{0,2},{1,3},{2,0},{3,1},{4,6},{5,7},{6,4},{7,5},{8,10},{9,11},{10,... | collective-permute-start | bytes 2433032 | tf_op jit(solution)/shard_map/ppermute | solution.py:468
  176.5 17.2 %collective-permute-start.24 = (bf16[256,640]{1,0:T(8,128)(2,1)S(1)}, bf16[256,640]{1,0:T(8,128)(2,1)S(1)}, u32[]{:S(2)}, u32[]{:S(2)}) collective-permute-start(bf16[256,640]{1,0:T(8,128)(2,1)S(1)} %pad_maximum_fusion.7), channel_id=1, source_target_pairs={{0,16},{1,17},{2,18},{3,19},{4,20},{5,21},{6,22},{7,23},{8,24},{9,... | collective-permute-start | bytes 983048 | tf_op jit(solution)/shard_map/ppermute | solution.py:468
  203.1 34.0 %collective-permute-start.25 = (bf16[1056,768]{1,0:T(8,128)(2,1)}, bf16[1056,768]{1,0:T(8,128)(2,1)}, u32[]{:S(2)}, u32[]{:S(2)}) collective-permute-start(bf16[1056,768]{1,0:T(8,128)(2,1)} %pad_maximum_fusion), channel_id=1, source_target_pairs={{0,1},{1,0},{2,3},{3,2},{4,5},{5,4},{6,7},{7,6},{8,9},{9,8},{10,11... | collective-permute-start | bytes 4866056 | tf_op jit(solution)/shard_map/ppermute | solution.py:468
  210.2 60.7 %collective-permute-start.49 = (bf16[1728,768]{1,0:T(8,128)(2,1)}, bf16[1728,768]{1,0:T(8,128)(2,1)}, u32[]{:S(2)}, u32[]{:S(2)}) collective-permute-start(bf16[1728,768]{1,0:T(8,128)(2,1)} %add_convert_fusion.1), channel_id=1, source_target_pairs={{0,2},{1,3},{2,0},{3,1},{4,6},{5,7},{6,4},{7,5},{8,10},{9,11},{10,... | collective-permute-start | bytes 7962632 | tf_op jit(solution)/shard_map/ppermute | solution.py:468
  233.1 42.4 %collective-permute-start.44 = (bf16[36,768]{1,0:T(8,128)(2,1)S(1)}, bf16[36,768]{1,0:T(8,128)(2,1)S(1)}, u32[]{:S(2)}, u32[]{:S(2)}) collective-permute-start(bf16[36,768]{1,0:T(8,128)(2,1)S(1)} %add_convert_fusion.15), channel_id=1, source_target_pairs={{0,4},{1,5},{2,6},{3,7},{4,0},{5,1},{6,2},{7,3},{8,12},{9,13},{10,... | collective-permute-start | bytes 165896 | tf_op jit(solution)/shard_map/ppermute | solution.py:468
  236.6 39.3 %collective-permute-start.39 = (bf16[72,768]{1,0:T(8,128)(2,1)S(1)}, bf16[72,768]{1,0:T(8,128)(2,1)S(1)}, u32[]{:S(2)}, u32[]{:S(2)}) collective-permute-start(bf16[72,768]{1,0:T(8,128)(2,1)S(1)} %maximum_select_fusion.11), channel_id=1, source_target_pairs={{0,8},{1,9},{2,10},{3,11},{4,12},{5,13},{6,14},{7,15},{8,0},{9,1},... | collective-permute-start | bytes 331784 | tf_op jit(solution)/shard_map/ppermute | solution.py:468
  238.4 49.0 %collective-permute-start.26 = (bf16[528,768]{1,0:T(8,128)(2,1)S(1)}, bf16[528,768]{1,0:T(8,128)(2,1)S(1)}, u32[]{:S(2)}, u32[]{:S(2)}) collective-permute-start(bf16[528,768]{1,0:T(8,128)(2,1)S(1)} %add_convert_fusion.3), channel_id=1, source_target_pairs={{0,2},{1,3},{2,0},{3,1},{4,6},{5,7},{6,4},{7,5},{8,10},{9,11},{10,... | collective-permute-start | bytes 2433032 | tf_op jit(solution)/shard_map/ppermute | solution.py:468
  274.4 31.6 %collective-permute-start.50 = (bf16[432,768]{1,0:T(8,128)(2,1)}, bf16[432,768]{1,0:T(8,128)(2,1)}, u32[]{:S(2)}, u32[]{:S(2)}) collective-permute-start(bf16[432,768]{1,0:T(8,128)(2,1)} %constant_dynamic-slice_fusion.6), channel_id=1, source_target_pairs={{0,4},{1,5},{2,6},{3,7},{4,0},{5,1},{6,2},{7,3},{8,12},{9,13},{10,... | collective-permute-start | bytes 1990664 | tf_op jit(solution)/shard_map/ppermute | solution.py:468
  276.0 21.1 %collective-permute-start.40 = (bf16[144,768]{1,0:T(8,128)(2,1)S(1)}, bf16[144,768]{1,0:T(8,128)(2,1)}, u32[]{:S(2)}, u32[]{:S(2)}) collective-permute-start(bf16[144,768]{1,0:T(8,128)(2,1)S(1)} %maximum_select_fusion.9), channel_id=1, source_target_pairs={{0,4},{1,5},{2,6},{3,7},{4,0},{5,1},{6,2},{7,3},{8,12},{9,13},{10,... | collective-permute-start | bytes 663560 | tf_op jit(solution)/shard_map/ppermute | solution.py:468
  282.5 18.7 %collective-permute-start.46 = (bf16[144,768]{1,0:T(8,128)(2,1)S(1)}, bf16[144,768]{1,0:T(8,128)(2,1)S(1)}, u32[]{:S(2)}, u32[]{:S(2)}) collective-permute-start(bf16[144,768]{1,0:T(8,128)(2,1)S(1)} %maximum_select_fusion.10), channel_id=1, source_target_pairs={{0,8},{1,9},{2,10},{3,11},{4,12},{5,13},{6,14},{7,15},{8,0},{9,1},... | collective-permute-start | bytes 663560 | tf_op jit(solution)/shard_map/ppermute | solution.py:468
  295.3 17.8 %collective-permute-start.56 = (bf16[432,768]{1,0:T(8,128)(2,1)}, bf16[432,768]{1,0:T(8,128)(2,1)}, u32[]{:S(2)}, u32[]{:S(2)}) collective-permute-start(bf16[432,768]{1,0:T(8,128)(2,1)} %constant_dynamic-slice_fusion.3), channel_id=1, source_target_pairs={{0,8},{1,9},{2,10},{3,11},{4,12},{5,13},{6,14},{7,15},{8,0},{9,1},... | collective-permute-start | bytes 1990664 | tf_op jit(solution)/shard_map/ppermute | solution.py:468
  298.8 65.4 %collective-permute-start.16 = (bf16[528,768]{1,0:T(8,128)(2,1)}, bf16[528,768]{1,0:T(8,128)(2,1)S(1)}, u32[]{:S(2)}, u32[]{:S(2)}) collective-permute-start(bf16[528,768]{1,0:T(8,128)(2,1)} %get-tuple-element.100.a), channel_id=1, source_target_pairs={{0,1},{1,0},{2,3},{3,2},{4,5},{5,4},{6,7},{7,6},{8,9},{9,8},{10,11... | collective-permute-start | bytes 2433032 | tf_op jit(solution)/shard_map/ppermute | solution.py:468
  301.2 65.5 %collective-permute-start.18 = (bf16[528,768]{1,0:T(8,128)(2,1)}, bf16[528,768]{1,0:T(8,128)(2,1)S(1)}, u32[]{:S(2)}, u32[]{:S(2)}) collective-permute-start(bf16[528,768]{1,0:T(8,128)(2,1)} %collective-permute-done.17.c), channel_id=1, source_target_pairs={{0,1},{1,0},{2,3},{3,2},{4,5},{5,4},{6,7},{7,6},{8,9},{9,8},{10,11... | collective-permute-start | bytes 2433032 | tf_op jit(solution)/shard_map/ppermute | solution.py:468
  305.5 68.7 %collective-permute-start.28 = (bf16[528,768]{1,0:T(8,128)(2,1)S(1)}, bf16[528,768]{1,0:T(8,128)(2,1)S(1)}, u32[]{:S(2)}, u32[]{:S(2)}) collective-permute-start(bf16[528,768]{1,0:T(8,128)(2,1)S(1)} %copy-done.16), channel_id=1, source_target_pairs={{0,2},{1,3},{2,0},{3,1},{4,6},{5,7},{6,4},{7,5},{8,10},{9,11},{10,... | collective-permute-start | bytes 2433032 | tf_op jit(solution)/shard_map/ppermute | solution.py:468
  306.0 47.2 %collective-permute-start.33 = (f32[16,768]{1,0:T(8,128)S(1)}, f32[16,768]{1,0:T(8,128)S(1)}, u32[]{:S(2)}, u32[]{:S(2)}) collective-permute-start(f32[16,768]{1,0:T(8,128)S(1)} %add.190), channel_id=1, source_target_pairs={{0,8},{1,9},{2,10},{3,11},{4,12},{5,13},{6,14},{7,15},{8,0},{9,1},... | collective-permute-start | bytes 147464 | tf_op jit(solution)/shard_map/ppermute | solution.py:468
  362.1 16.6 %collective-permute-start.54 = (bf16[216,768]{1,0:T(8,128)(2,1)S(1)}, bf16[216,768]{1,0:T(8,128)(2,1)S(1)}, u32[]{:S(2)}, u32[]{:S(2)}) collective-permute-start(bf16[216,768]{1,0:T(8,128)(2,1)S(1)} %maximum_select_fusion.7), channel_id=1, source_target_pairs={{0,8},{1,9},{2,10},{3,11},{4,12},{5,13},{6,14},{7,15},{8,0},{9,1},... | collective-permute-start | bytes 995336 | tf_op jit(solution)/shard_map/ppermute | solution.py:468
  364.3 17.9 %collective-permute-start.60 = (bf16[216,768]{1,0:T(8,128)(2,1)S(1)}, bf16[216,768]{1,0:T(8,128)(2,1)S(1)}, u32[]{:S(2)}, u32[]{:S(2)}) collective-permute-start(bf16[216,768]{1,0:T(8,128)(2,1)S(1)} %maximum_select_fusion.8), channel_id=1, source_target_pairs={{0,16},{1,17},{2,18},{3,19},{4,20},{5,21},{6,22},{7,23},{8,24},{9,... | collective-permute-start | bytes 995336 | tf_op jit(solution)/shard_map/ppermute | solution.py:468
  379.0 17.6 %collective-permute-start.55 = (bf16[432,768]{1,0:T(8,128)(2,1)S(1)}, bf16[432,768]{1,0:T(8,128)(2,1)S(1)}, u32[]{:S(2)}, u32[]{:S(2)}) collective-permute-start(bf16[432,768]{1,0:T(8,128)(2,1)S(1)} %maximum_select_fusion.3), channel_id=1, source_target_pairs={{0,4},{1,5},{2,6},{3,7},{4,0},{5,1},{6,2},{7,3},{8,12},{9,13},{10,... | collective-permute-start | bytes 1990664 | tf_op jit(solution)/shard_map/ppermute | solution.py:468
  (80 other events, 751.2 us)

commit v2 on v0

v2 whole, which is shorter than its diff:
```python
import jax
import jax.numpy as jnp
from jax import lax
from jax.experimental import pallas as pl
from jax.experimental.pallas import tpu as pltpu
from jax.sharding import PartitionSpec as P

HEAD = 64
LANES = 128
GROUP = 256
LAT = 8
BF = jnp.bfloat16
F32 = jnp.float32
FAR = -1e30
MIB = 1 << 20
GAIN1, SHIFT1, B_OUT, GAIN2, SHIFT2, B_DOWN, B_UP = range(7)


def dot(a, b, ca, cb):
    return lax.dot_general(a, b, (((ca,), (cb,)), ((), ())), preferred_element_type=F32)


def norm_parts(values):
    center = values - jnp.mean(values, axis=-1, keepdims=True)
    spread = jnp.mean(center * center, axis=-1, keepdims=True)
    inverse = lax.rsqrt(spread + 1e-06)
    return center * inverse, inverse


def norm_back(grad, unit, inverse, gain):
    scaled = grad * gain
    inner = jnp.mean(scaled * unit, axis=-1, keepdims=True)
    return inverse * (scaled - jnp.mean(scaled, axis=-1, keepdims=True) - unit * inner)


def gelu_both(values):
    square = values * values
    inner = jnp.tanh(values * (0.7978845608028654 + 0.035677408136300125 * square))
    half = 0.5 + 0.5 * inner
    slope = values * (0.3989422804014327 + 0.05351611220494518 * square)
    return values * half, half + (1.0 - inner * inner) * slope


def split3(v):
    hi = v.astype(BF)
    mid = (v - hi.astype(F32)).astype(BF)
    low = (v - hi.astype(F32) - mid.astype(F32)).astype(BF)
    return hi, mid, low


def head_lanes(v, h):
    lane = lax.broadcasted_iota(jnp.int32, v.shape, v.ndim - 1)
    return jnp.where((lane >= h * HEAD) & (lane < (h + 1) * HEAD), v, jnp.zeros_like(v))


def kept(shape):
    return pl.BlockSpec(shape, lambda *_: (0,) * len(shape))


def whole(shape):
    return pl.BlockSpec(shape, lambda *_: (0,) * len(shape), pipeline_mode=pl.Buffered(1))


ANY = pl.BlockSpec(memory_space=pl.ANY)
OWN, SENT = (0, 1, 2, 3), (0, 2, 1, 3)


def call(body, *, name, scalars, ins, outs, grid=(1,), scratch=(), deps=(), us=1.0):
    first, extra = scalars + len(ins), len(deps)

    def wrapped(*refs):
        body(*refs[:first], *refs[first + extra :])

    def run(*args):
        return pl.pallas_call(
            wrapped,
            name=name,
            out_shape=[jax.ShapeDtypeStruct(s, d) for s, d, _ in outs],
            grid_spec=pltpu.PrefetchScalarGridSpec(
                num_scalar_prefetch=scalars,
                grid=grid,
                in_specs=list(ins) + [ANY] * extra,
                out_specs=[spec for _, _, spec in outs],
                scratch_shapes=list(scratch),
            ),
            compiler_params=pltpu.CompilerParams(
                dimension_semantics=("arbitrary",) * len(grid), vmem_limit_bytes=56 * MIB
            ),
            cost_estimate=pl.CostEstimate(
                flops=int(us * 1.0e10), bytes_accessed=1 << 16, transcendentals=0
            ),
        )(*args, *deps)

    return run


def mover(sems):
    used = []

    def start(src, dst):
        copy = pltpu.make_async_copy(src, dst, sems.at[len(used)])
        used.append(copy)
        copy.start()
        return copy

    return start


def sides(meta):
    return meta[0] & 1, (meta[0] >> 1) & 1


def combine(name, meta, arrays, outs, deps=(), us=1.0):
    def body(meta, *refs):
        x, z = sides(meta)

        def rows_at(at, n):
            return pl.ds(pl.multiple_of(at(x, z), 16), n) if callable(at) else slice(at, at + n)

        for ref, (_, kind, segments) in zip(refs[len(arrays) :], outs):
            for to, n, terms in segments:
                parts = [refs[i][rows_at(at, n), :] for i, at in terms]
                value = parts[0]
                if len(parts) > 1:
                    value = parts[0].astype(F32)
                    for part in parts[1:]:
                        value = value + part.astype(F32)
                ref[rows_at(to, n), :] = value.astype(kind)

    width = arrays[0].shape[1]
    return call(
        body,
        name=name,
        scalars=1,
        ins=[whole(a.shape) for a in arrays],
        outs=[((rows, width), kind, whole((rows, width))) for rows, kind, _ in outs],
        deps=deps,
        us=us,
    )(meta, *arrays)


def group_at(meta, count, slot, i):
    return count[(meta[1] ^ slot) * 2 + i]


def image_list(meta, image, devices, per_device, slots):
    each = per_device // 4
    return [
        image[(meta[0] ^ j) * per_device + (meta[1] ^ s) * each + i]
        for j in range(devices)
        for s in slots
        for i in range(each)
    ]


def image_column(images):
    return jnp.concatenate([jnp.full((LAT, 1), im, jnp.int32) for im in images], 0)


def image_row(images):
    group = lax.broadcasted_iota(jnp.int32, (1, len(images) * LAT), 1) // LAT
    out = jnp.zeros(group.shape, jnp.int32)
    for g, im in enumerate(images):
        out = jnp.where(group == g, im, out)
    return out


def key_stack(tok, lat8):
    pad = jnp.concatenate([lat8, jnp.zeros_like(lat8)], 0).astype(BF)
    return jnp.concatenate([tok, pad], 0)


def near_mask(count, columns):
    row = lax.broadcasted_iota(jnp.int32, (GROUP + 2 * LAT, columns), 0)
    return (row < count) | ((row >= GROUP) & (row < GROUP + LAT))


def param(params, i):
    return params[i : i + 1, :]


def project(rows, params, w, bias):
    unit, _ = norm_parts(rows.astype(F32))
    rows = (unit * param(params, GAIN1) + param(params, SHIFT1)).astype(BF)
    return (
        rows,
        (dot(rows, w[0], 1, 1) + bias[0:1]).astype(BF),
        dot(rows, w[1], 1, 1).astype(BF),
        (dot(rows, w[2], 1, 1) + bias[1:2]).astype(BF),
    )


def prepare(meta, lat, w_out, g1, s1, bo, g2, s2, bd, bu, up, down, lat_rel, lat_half, out_pack, part, params):
    n = lat.shape[0] // 4
    for s in range(4):
        rows = lat[pl.ds(pl.multiple_of((meta[1] ^ s) * n, 16), n), :]
        lat_rel[s * n : (s + 1) * n, :] = rows
        if s % 2 == 0:
            lat_half[s // 2 * n : (s // 2 + 1) * n, :] = rows
    for i, ref in enumerate((g1, s1, bo, g2, s2, bd, bu)):
        params[i : i + 1, :] = ref[...].reshape(1, ref.shape[0])
    params[7:8, :] = jnp.zeros_like(params[7:8, :])
    wide = w_out.shape[0]
    out_pack[0:wide, :] = w_out[...]
    bias = param(params, B_UP)
    rows = [v.astype(F32) for v in split3(bias)]
    out_pack[wide : wide + 16, :] = jnp.concatenate(rows + [jnp.zeros((13, bias.shape[1]), F32)], 0).astype(BF)
    n = up.shape[0]
    part[0:n, :], part[n : 2 * n, :] = up[...], down[...]


def latent_rows(lat, params, w, bias, normed, ql, kl, vl):
    normed[...], a, b, c = project(lat[...], params, w, bias)
    ql[...], kl[...], vl[...] = a.astype(F32), b.astype(F32), c.astype(F32)


def forward_near(base, meta, count, tok, kl, vl, params, w, bias, normed, q, k, v, mixed_out, log):
    step = pl.program_id(0)
    wide = w.shape[1]
    rows, qs, ks, vs = project(tok[...], params, w, bias)
    normed[...], q[...], k[...], v[...] = rows, qs, ks, vs
    qs = qs * jnp.asarray(0.125, BF)
    for i in range(tok.shape[0] // GROUP):
        here = slice(i * LAT, (i + 1) * LAT)
        at = slice(i * GROUP, (i + 1) * GROUP)
        keys = key_stack(ks[at], kl[here, :])
        values = key_stack(vs[at], vl[here, :]).T
        mask = near_mask(group_at(meta, count, step + base, i), GROUP)
        logs, outs = [], []
        for h in range(wide // HEAD):
            s = jnp.where(mask, dot(head_lanes(keys, h), qs[at], 1, 1), FAR)
            top = jnp.max(s, 0, keepdims=True)
            e = jnp.exp(s - top)
            total = jnp.sum(e, 0, keepdims=True)
            logs.append(top + jnp.log(total))
            outs.append(dot(values[h * HEAD : (h + 1) * HEAD], e.astype(BF), 1, 0) * (1.0 / total))
        log[i] = jnp.concatenate(logs + [jnp.zeros((8 - len(logs), GROUP), F32)], 0)
        mixed_out[:, at] = jnp.concatenate(outs, 0).astype(BF)


def forward_far(meta, count, image, lat, params, w, bias, k_near, k_away, v_near, v_away, ql, qa, ka, va, m_near, m_away, far, logs_out):
    step = pl.program_id(0)
    wide = w.shape[1]
    rows_step = lat.shape[0]
    own = ql.shape[0]
    groups = own // LAT

    def rows_of(near, away, g):
        half = groups // 2
        ref, at = (near, g) if g < half else (away, g - half)
        return ref[at * GROUP : (at + 1) * GROUP, :]

    _, a, b, c = project(lat[...], params, w, bias)
    here = pl.ds(pl.multiple_of(step * rows_step, rows_step), rows_step)
    qa[here, :], ka[here, :], va[here, :] = a, b, c

    @pl.when(step == pl.num_programs(0) - 1)
    def _():
        q32 = ql[...] * 0.125
        images = image_list(meta, image, qa.shape[0] // own, groups, SENT)
        mask = image_column(image_list(meta, image, 1, groups, OWN)) == image_row(images)
        lane = lax.broadcasted_iota(jnp.int32, (LAT, GROUP), 1)
        full = jnp.zeros((own, wide), F32)
        logs = []
        for h in range(wide // HEAD):
            qh = head_lanes(q32, h)
            s_lat = jnp.where(mask, dot(qh.astype(BF), ka[...], 1, 1), FAR)
            s_tok = jnp.concatenate(
                [
                    jnp.where(
                        lane < group_at(meta, count, g // 2, g % 2),
                        dot(qh[g * LAT : (g + 1) * LAT].astype(BF), rows_of(k_near, k_away, g), 1, 1),
                        FAR,
                    )
                    for g in range(groups)
                ],
                0,
            )
            top = jnp.maximum(jnp.max(s_lat, 1, keepdims=True), jnp.max(s_tok, 1, keepdims=True))
            e_lat, e_tok = jnp.exp(s_lat - top), jnp.exp(s_tok - top)
            total = jnp.sum(e_lat, 1, keepdims=True) + jnp.sum(e_tok, 1, keepdims=True)
            logs.append(top + jnp.log(total))
            near = jnp.concatenate(
                [
                    dot(e_tok[g * LAT : (g + 1) * LAT].astype(BF), rows_of(v_near, v_away, g), 1, 0)
                    for g in range(groups)
                ],
                0,
            )
            full = full + head_lanes((dot(e_lat.astype(BF), va[...], 1, 0) + near) * (1.0 / total), h)
        mixed = full.astype(BF)
        m_near[...], m_away[...] = mixed[: own // 2], mixed[own // 2 :]
        parts = [split3(x) for x in logs]
        cols = [p[i] for i in range(3) for p in parts]
        lane = lax.broadcasted_iota(jnp.int32, (own, 2 * HEAD), 1)
        extra = jnp.zeros((own, 2 * HEAD), F32)
        for i, c in enumerate(cols):
            extra = jnp.where(lane == i, c.astype(F32), extra)
        far[...] = mixed
        logs_out[...] = extra.astype(BF)


def valid_rows(meta, count, rows):
    row = lax.broadcasted_iota(jnp.int32, (rows, 1), 0)
    first = (row < GROUP) & (row < group_at(meta, count, 0, 0))
    return first | ((row >= GROUP) & (row < GROUP + group_at(meta, count, 0, 1)))


def slot_block(meta, ref, slot):
    n = ref.shape[0] // 4
    return ref.at[pl.ds(pl.multiple_of((meta[1] ^ slot) * n, 16), n)]


def project_out(t_near, t_far, l_near, l_far, o0, o2, out):
    wide, n = t_near.shape
    value = dot(t_near[...], o0[0:wide, :], 0, 0) + dot(t_far[...], o2[0:wide, :], 0, 0)
    out[0:n, :] = value.astype(out.dtype)
    value = dot(l_near[...], o0[0:wide, :], 1, 0) + dot(l_far[...], o2[0:wide, :], 1, 0)
    out[n:, :] = value.astype(out.dtype)


def cot_back(meta, cot_tok, cot_lat, down_w, out):
    n = cot_tok.shape[0]
    out[0:n, :] = dot(cot_tok[...], down_w[...], 1, 1).astype(BF)
    out[n:, :] = dot(cot_lat[...], down_w[...], 1, 1).astype(BF)


def add_norm(meta, count, params, own, got, tok, lat, residual, n2, stats):
    n, m = tok.shape[0], lat.shape[0]
    stats[...] = jnp.zeros_like(stats)
    for at, size, x in ((0, n, tok), (n, m, lat)):
        rows = slice(at, at + size)
        attn = own[rows, :] + got[rows, :].astype(F32) + param(params, B_OUT)
        if at == 0:
            real = valid_rows(meta, count, n)
            stats[0:1, :] = jnp.sum(jnp.where(real, attn * attn, 0.0), 0, keepdims=True)
        res = x[...].astype(F32) + attn
        residual[rows, :] = res
        unit, _ = norm_parts(res)
        n2[rows, :] = (unit * param(params, GAIN2) + param(params, SHIFT2)).astype(BF)


def hidden_part(n2, cot, up_w, down_w, bias, act_out, grad_out):
    cut = 256
    sums = []
    for at in range(0, up_w.shape[1], cut):
        cols = slice(at, at + cut)
        up = dot(n2, up_w[:, cols], 1, 0) + bias[:, cols]
        active, slope = gelu_both(up)
        grad_up = (dot(cot, down_w[cols, :], 1, 1) * slope).astype(BF)
        act_out[:, cols] = active.astype(BF)
        grad_out[:, cols] = grad_up
        sums.append(jnp.sum(grad_up.astype(F32), 0, keepdims=True))
    return jnp.concatenate(sums, 1)


def two_halves(meta, fetch, n2_own, n2_sib, cot_tok, cot_lat, vn2, vcot):
    rows = n2_own.shape[0]
    n = cot_tok.shape[0] // 4
    copies = [fetch(n2_own, vn2.at[0:rows]), fetch(n2_sib, vn2.at[rows:])]
    for s in (0, 1):
        at = s * rows
        copies.append(fetch(slot_block(meta, cot_tok, s), vcot.at[at : at + n]))
        copies.append(fetch(slot_block(meta, cot_lat, s), vcot.at[at + n : at + rows]))
    return copies


def send_parts(meta, flush, pack, parts):
    x, z = sides(meta)
    n = parts[0].shape[0] // 2
    copies = []
    for ref, (dx, dz) in zip(parts, ((0, 0), (1, 0), (0, 1), (1, 1))):
        q = (x ^ dx) * 2 + (z ^ dz)
        for i in (0, 1):
            src = pack.at[pl.ds(pl.multiple_of(i * 4 * n + q * n, 16), n)]
            copies.append(flush(src, ref.at[i * n : (i + 1) * n]))
    return copies


def hidden_rows(n2, up_w, bias, got, act_out, grad_out, sums):
    cut = 256
    for at in range(0, up_w.shape[1], cut):
        cols = slice(at, at + cut)
        active, slope = gelu_both(dot(n2, up_w[:, cols], 1, 0) + bias[:, cols])
        grad_up = (got[:, cols].astype(F32) * slope).astype(BF)
        act_out[:, cols] = active.astype(BF)
        grad_out[:, cols] = grad_up
        sums[0:1, cols] = jnp.sum(grad_up.astype(F32), 0, keepdims=True)


def hidden_first(params, n2, up_w, got, act, grad, stats):
    stats[...] = jnp.zeros_like(stats)
    hidden_rows(n2[...], up_w, param(params, B_UP), got, act, grad, stats)


def hidden_own(
    meta, params, n2_own, n2_sib, cot_tok, cot_lat, up_w, down_w, got_in, act_in, grad_in,
    branch_out, back_out, p0, p1, p2, p3, stats,
    vn2, vcot, vw, branch, back, act, grad, got, vpack, in_sems, out_sems,
):
    width, hidden = vw.shape[1], vw.shape[2]
    rows = got.shape[0]
    fetch, flush = mover(in_sems), mover(out_sems)
    first = [fetch(n2_sib, vn2.at[rows:]), fetch(up_w, vw.at[0]), fetch(got_in, got)]
    copies = [fetch(grad_in, grad.at[0:rows]), fetch(act_in, act.at[0:rows]), fetch(down_w, vw.at[1])]
    copies.append(fetch(n2_own, vn2.at[0:rows]))
    n = cot_tok.shape[0] // 4
    for s in (0, 1):
        at = s * rows
        copies.append(fetch(slot_block(meta, cot_tok, s), vcot.at[at : at + n]))
        copies.append(fetch(slot_block(meta, cot_lat, s), vcot.at[at + n : at + rows]))
    for copy in first:
        copy.wait()
    stats[...] = jnp.zeros_like(stats)
    hidden_rows(vn2[rows:, :], vw.at[0], param(params, B_UP), got, act.at[rows:], grad.at[rows:], stats)
    for copy in copies:
        copy.wait()
    back[...] = dot(grad[...], vw[0], 1, 1)
    outs = [flush(back, back_out)]
    branch[...] = dot(act[...], vw[1], 1, 0)
    outs.append(flush(branch, branch_out))
    vpack[0:width, :] = dot(vn2[...], grad[...], 0, 0).astype(BF)
    vpack[width : width + hidden, :] = dot(act[...], vcot[...], 0, 0).astype(BF)
    outs += send_parts(meta, flush, vpack, (p0, p1, p2, p3))
    for copy in outs:
        copy.wait()


def hidden_away(
    meta, o2, n2_own, n2_sib, cot_tok, cot_lat, w0, w1, w2, w3, branch_in, back_in,
    branch_own, back_own, send, act_out, grad_out, stats,
    vn2, vcot, vw, branch, back, act, grad, vsend, in_sems, out_sems,
):
    rows, width = n2_own.shape
    x, z = sides(meta)
    quarter = w0.shape[0] // 2
    fetch, flush = mover(in_sems), mover(out_sems)
    copies = two_halves(meta, fetch, n2_own, n2_sib, cot_tok, cot_lat, vn2, vcot)
    for ref, (dx, dz) in zip((w0, w1, w2, w3), ((0, 0), (1, 0), (0, 1), (1, 1))):
        q = pl.multiple_of(((x ^ dx) * 2 + (z ^ dz)) * quarter, 16)
        for i in (0, 1):
            copies.append(fetch(ref.at[i * quarter : (i + 1) * quarter], vw.at[i, pl.ds(q, quarter)]))
    late = [fetch(back_in, back), fetch(branch_in, branch)]
    for copy in copies:
        copy.wait()
    base = o2.shape[0] - 16
    bias = o2[base : base + 16, :].astype(F32)
    bias = bias[0:1] + bias[1:2] + bias[2:3]
    n2, ct = vn2[...], vcot[...]
    stats[...] = jnp.zeros_like(stats)
    stats[0:1, :] = hidden_part(n2, ct, vw.at[0], vw.at[1], bias, act, grad)
    outs = [flush(act, act_out), flush(grad, grad_out)]
    for i, (ref, src, w, turn, own) in enumerate(
        ((back, grad, vw.at[0], 1, back_own), (branch, act, vw.at[1], 0, branch_own))
    ):
        late[i].wait()
        ref[...] += dot(src[...], w[...], 1, turn)
        vsend[i * rows : (i + 1) * rows, :] = ref[rows:, :].astype(BF)
        outs.append(flush(ref.at[0:rows], own))
        outs.append(flush(vsend.at[i * rows : (i + 1) * rows], send.at[i * rows : (i + 1) * rows]))
    for copy in outs:
        copy.wait()


def away_grads(
    meta, n2_own, n2_sib, cot_tok, cot_lat, act_in, grad_in, p0, p1, p2, p3,
    vn2, vcot, act, grad, vpack, in_sems, out_sems,
):
    width, hidden = vn2.shape[1], act.shape[1]
    fetch, flush = mover(in_sems), mover(out_sems)
    copies = [fetch(grad_in, grad)] + two_halves(meta, fetch, n2_own, n2_sib, cot_tok, cot_lat, vn2, vcot)
    last = fetch(act_in, act)
    for copy in copies:
        copy.wait()
    vpack[0:width, :] = dot(vn2[...], grad[...], 0, 0).astype(BF)
    last.wait()
    vpack[width : width + hidden, :] = dot(act[...], vcot[...], 0, 0).astype(BF)
    for copy in send_parts(meta, flush, vpack, (p0, p1, p2, p3)):
        copy.wait()


def middle_rows(meta, count, params, residual, branch, back, got, cot_tok, cot_lat, out_rows, grad_res, grad_attn, stats):
    n, m = cot_tok.shape[0], cot_lat.shape[0]
    rows_own = n + m
    stats[...] = jnp.zeros_like(stats)
    for at, size, cot in ((0, n, cot_tok), (n, m, cot_lat)):
        rows = slice(at, at + size)
        bk = back[rows, :] + got[rows, :].astype(F32)
        br = branch[rows, :] + got[rows_own + at : rows_own + at + size, :].astype(F32) + param(params, B_DOWN)
        res = residual[rows, :]
        out = res + br
        out_rows[rows, :] = out.astype(BF)
        if at == 0:
            real = valid_rows(meta, count, n)
            stats[0:1, :] = jnp.sum(jnp.where(real, out * out, 0.0), 0, keepdims=True)
            stats[1:2, :] = jnp.sum(jnp.where(real, br * br, 0.0), 0, keepdims=True)
        unit, inverse = norm_parts(res)
        stats[2:3, :] += jnp.sum(bk * unit, 0, keepdims=True)
        stats[3:4, :] += jnp.sum(bk, 0, keepdims=True)
        cot32 = cot[...].astype(F32)
        gr = cot32 + norm_back(bk, unit, inverse, param(params, GAIN2))
        grad_res[rows, :] = gr
        ga = gr.astype(BF)
        grad_attn[rows, :] = ga
        stats[4:5, :] += jnp.sum(ga.astype(F32), 0, keepdims=True)
        stats[5:6, :] += jnp.sum(cot32, 0, keepdims=True)


def back_out(ga_own, ga_sib, o0, o2, t_near, t_far, l_near, l_far, g0, g2, d0, d2, w0, w2):
    wide, n = t_near.shape[0], t_near.shape[1] // 2
    m = l_near.shape[0] // 2
    for o, g, d in ((o2, g2, d2), (o0, g0, d0)):
        for i, ga in enumerate((ga_own, ga_sib)):
            g[:, i * n : (i + 1) * n] = dot(o[0:wide, :], ga[0:n, :], 1, 1).astype(BF)
            d[i * m : (i + 1) * m, :] = dot(ga[n : n + m, :], o[0:wide, :], 1, 1).astype(BF)
    for t, l, w in ((t_far, l_far, w2), (t_near, l_near, w0)):
        total = jnp.zeros(w.shape, F32)
        for i, ga in enumerate((ga_own, ga_sib)):
            total += dot(t[:, i * n : (i + 1) * n], ga[0:n, :], 1, 0)
            total += dot(l[i * m : (i + 1) * m, :], ga[n : n + m, :], 0, 0)
        w[...] = total.astype(BF)


def near_slot(
    slot, meta, count, normed, q, k, v, ql, kl, vl, log, far, logs_far, d_in, d_lat_in, w, grad_w, bias,
    dq_far, dk_near, dv_near,
):
    wide = q.shape[1]
    heads = wide // HEAD
    rows = normed[...]
    slot_rows = rows.shape[0]
    d_lat = d_lat_in[...].astype(F32)
    eighth = jnp.asarray(0.125, BF)
    q_all, k_all, v_all = q[...] * eighth, k[...], v[...]
    far32 = far[...].astype(F32)
    far_log = logs_far[...].astype(F32)
    dqs, dks, dvs = [], [], []
    for i in range(slot_rows // GROUP):
        at, lat_at = slice(i * GROUP, (i + 1) * GROUP), slice(i * LAT, (i + 1) * LAT)
        number = group_at(meta, count, slot, i)
        d_cols = d_in[:, at]
        d_tok, qs, ks, vs = d_cols.T, q_all[at], k_all[at], v_all[at]
        keys, values = key_stack(ks, kl[lat_at, :]), key_stack(vs, vl[lat_at, :])
        keys_t = keys.T
        mask = near_mask(number, GROUP)
        ps, gs, dq_t, d_heads, q_heads = [], [], [], [], []
        for h in range(heads):
            s = dot(head_lanes(keys, h), qs, 1, 1)
            p = jnp.where(mask, jnp.exp(s - log[i, h : h + 1, :]), 0.0)
            gp = p * dot(head_lanes(values, h), d_cols, 1, 0)
            g = (gp - p * jnp.sum(gp, 0, keepdims=True)).astype(BF)
            dq_t.append(dot(keys_t[h * HEAD : (h + 1) * HEAD], g, 1, 0))
            ps.append(p.astype(BF))
            gs.append(g)
            d_heads.append(head_lanes(d_tok, h))
            q_heads.append(head_lanes(qs, h))
        dv = dot(jnp.concatenate(ps, 1), jnp.concatenate(d_heads, 0), 1, 0)
        dk = dot(jnp.concatenate(gs, 1), jnp.concatenate(q_heads, 0), 1, 0)
        dqs.append((jnp.concatenate(dq_t, 0).T * 0.125).astype(BF))
        pad = jnp.zeros((LAT, wide), F32)
        q8, o8, d8, lg = ql[lat_at, :] * 0.125, far32[lat_at], d_lat[lat_at], far_log[lat_at]
        q_rows, do_rows, log_col, del_col = [], [], [], []
        big = jnp.full((LAT, 1), 1e30, F32)
        zero = jnp.zeros((LAT, 1), F32)
        for h in range(heads):
            q_rows += [head_lanes(q8, h), pad]
            dh = head_lanes(d8, h)
            do_rows += [dh, pad]
            col = lg[:, h : h + 1] + lg[:, heads + h : heads + h + 1] + lg[:, 2 * heads + h : 2 * heads + h + 1]
            log_col += [col, big]
            del_col += [jnp.sum(dh * o8, 1, keepdims=True), zero]
        q_f, d_f = jnp.concatenate(q_rows, 0).astype(BF), jnp.concatenate(do_rows, 0).astype(BF)
        l_f, x_f = jnp.concatenate(log_col, 0), jnp.concatenate(del_col, 0)
        lane = lax.broadcasted_iota(jnp.int32, (2 * LAT * heads, GROUP), 1)
        p_f = jnp.where(lane < number, jnp.exp(dot(q_f, ks, 1, 1) - l_f), 0.0)
        g_f = (p_f * (dot(d_f, vs, 1, 1) - x_f)).astype(BF)
        dks.append((dk[0:GROUP] + dot(g_f, q_f, 0, 0)).astype(BF))
        dvs.append((dv[0:GROUP] + dot(p_f.astype(BF), d_f, 0, 0)).astype(BF))
        dk_near[lat_at, :] = dk[GROUP : GROUP + LAT]
        dv_near[lat_at, :] = dv[GROUP : GROUP + LAT]
        dq_all = dot(g_f, ks, 1, 0)
        dq_lat = jnp.zeros((LAT, wide), F32)
        for h in range(heads):
            dq_lat += head_lanes(dq_all[2 * LAT * h : 2 * LAT * h + LAT], h)
        dq_far[lat_at, :] = dq_lat

    dq, dk, dv = (jnp.concatenate(v, 0) for v in (dqs, dks, dvs))
    total = dot(dq, w[0], 1, 0) + dot(dk, w[1], 1, 0) + dot(dv, w[2], 1, 0)
    for i, g in enumerate((dq, dk, dv)):
        grad_w[i] += dot(g, rows, 0, 0)
    bias[0:1, :] += jnp.sum(dq.astype(F32), 0, keepdims=True)
    bias[1:2, :] += jnp.sum(dv.astype(F32), 0, keepdims=True)
    bias[2:3, :] += jnp.sum(dk.astype(F32), 0, keepdims=True)
    return total.astype(BF)


def backward_rows(
    first, begin, meta, count, normed, q, k, v, ql, kl, vl, log, far, logs_far, d_in, d_lat, w, gw_in, bias_in, *outs,
):
    step = pl.program_id(0)
    parts, (grad_w, bias, dq_far, dk_near, dv_near) = outs[:-5], outs[-5:]

    @pl.when(step == 0)
    def _():
        grad_w[...] = jnp.zeros_like(grad_w) if begin else gw_in[...]
        bias[...] = jnp.zeros_like(bias) if begin else bias_in[...]

    total = near_slot(
        step + first, meta, count, normed, q, k, v, ql, kl, vl, log, far, logs_far, d_in, d_lat, w, grad_w, bias,
        dq_far, dk_near, dv_near,
    )
    for slot, ref in enumerate(parts):

        @pl.when(step == slot)
        def _(ref=ref):
            ref[...] = total


def latent_bundle(d_near, d_far, far, logs_far, own, sent):
    count, wide = far.shape
    heads = wide // HEAD
    n = count // 4
    d32 = jnp.concatenate([d_near[...], d_far[...]], 0).astype(F32)
    prod = d32 * far[...].astype(F32)
    lg = logs_far[...].astype(F32)
    deltas = [split3(jnp.sum(head_lanes(prod, h), 1, keepdims=True)) for h in range(heads)]
    cols = [lg[:, i : i + 1] for i in range(3 * heads)] + [p[i].astype(F32) for i in (0, 1) for p in deltas]
    lane = lax.broadcasted_iota(jnp.int32, (count, 4 * HEAD), 1)
    value = jnp.concatenate([d32, jnp.zeros((count, HEAD), F32)], 1)
    for i, c in enumerate(cols):
        value = jnp.where(lane == wide + i, c, value)
    value = value.astype(BF)
    own[...] = value
    for i, s in enumerate(SENT):
        sent[i * n : (i + 1) * n, :] = value[s * n : (s + 1) * n]


def backward_far(
    meta, tokens_real, image, qa, ka, va, ql, kl, vl, own, bundle, normed, w, gw, bias_in, wo_a, wo_b,
    params, stats1, stats2, hid_first, hid_near, hid_away, *refs,
):
    near, (lat_keep, lat_send, p0, p1, p2, p3, small, pack, out_sems) = refs[:-9], refs[-9:]
    count, wide = ql.shape
    heads = wide // HEAD
    groups = count // LAT
    q_all, k_all, v_all = qa[...] * jnp.asarray(0.125, BF), ka[...], va[...]
    q_own, k_own, v_own = (ql[...] * 0.125).astype(BF), kl[...].astype(BF), vl[...].astype(BF)
    d_own, d_all = own[:, 0:wide], bundle[:, 0:wide]

    def stats(ref, h):
        x = ref[...].astype(F32)
        col = [x[:, wide + i : wide + i + 1] for i in range(5 * heads)]
        return col[h] + col[heads + h] + col[2 * heads + h], col[3 * heads + h] + col[4 * heads + h]

    mine = image_list(meta, image, 1, groups, OWN)
    images = image_list(meta, image, qa.shape[0] // count, groups, SENT)
    mask_q = image_column(mine) == image_row(images)
    mask_k = image_column(images) == image_row(mine)
    each = len(near) // 3
    dq, dk, dv = (jnp.concatenate([ref[...] for ref in near[i * each : (i + 1) * each]], 0) for i in range(3))
    for h in range(heads):
        log, delta = stats(own, h)
        s = dot(head_lanes(q_own, h), k_all, 1, 1)
        p = jnp.where(mask_q, jnp.exp(s - log), 0.0)
        g = (p * (dot(head_lanes(d_own, h), v_all, 1, 1) - delta)).astype(BF)
        dq += head_lanes(dot(g, k_all, 1, 0), h)
        log, delta = stats(bundle, h)
        s = dot(q_all, head_lanes(k_own, h), 1, 1)
        p = jnp.where(mask_k, jnp.exp(s - log), 0.0)
        g = (p * (dot(d_all, head_lanes(v_own, h), 1, 1) - delta)).astype(BF)
        dk += head_lanes(dot(g, q_all, 0, 0), h)
        dv += head_lanes(dot(p.astype(BF), d_all, 0, 0), h)
    dq, dk, dv = (dq * 0.125).astype(BF), dk.astype(BF), dv.astype(BF)
    lat_rows = normed[...]
    sums = [bias_in[i : i + 1, :] for i in (0, 2, 1)]
    sums = [b + jnp.sum(g.astype(F32), 0, keepdims=True) for b, g in zip(sums, (dq, dk, dv))]
    columns = jnp.concatenate(sums + [jnp.zeros((5, wide), F32)], 0).T
    first_gain = jnp.zeros((1, pack.shape[1]), F32)
    first_shift = first_gain
    for i, g in enumerate((dq, dk, dv)):
        total = gw[i] + dot(g, lat_rows, 0, 0)
        pack[i * wide : (i + 1) * wide, :] = total.astype(BF)
        col, weight = columns[:, i : i + 1], w[i].astype(F32)
        first_shift += jnp.sum(weight * col, 0, keepdims=True)
        first_gain += jnp.sum(weight * (total - col * param(params, SHIFT1)), 0, keepdims=True)
    first_gain = first_gain / param(params, GAIN1)
    pack[3 * wide :, :] = (wo_a[...].astype(F32) + wo_b[...].astype(F32)).astype(BF)
    x, z = sides(meta)
    flush = mover(out_sems)
    copies = []
    for ref, (dx, dz) in zip((p0, p1, p2, p3), ((0, 0), (1, 0), (0, 1), (1, 1))):
        part = (x ^ dx) * 2 + (z ^ dz)
        at = 0
        for base, size in ((0, 3 * wide // 4), (3 * wide, wide // 4)):
            src = pack.at[pl.ds(pl.multiple_of(base + part * size, 16), size)]
            copies.append(flush(src, ref.at[at : at + size]))
            at += size
    rows = (dot(dq, w[0], 1, 0) + dot(dk, w[1], 1, 0) + dot(dv, w[2], 1, 0)).astype(BF)
    n = count // 4
    lat_keep[0:n, :], lat_keep[n : 2 * n, :] = rows[0:n], rows[2 * n : 3 * n]
    lat_send[0:n, :], lat_send[n : 2 * n, :] = rows[n : 2 * n], rows[3 * n :]
    small[...] = jnp.zeros_like(small)
    small[0:1, :] = stats1[0:1, :]
    small[1:7, :] = stats2[0:6, :]
    small[7:8, :], small[8:9, :] = first_gain, first_shift
    real = tokens_real[0]
    for i in range(1, tokens_real.shape[0]):
        real = real + tokens_real[i]
    for at, part in ((9, real - real % 64), (22, real % 64)):
        small[at : at + 1, :] = jnp.full((1, small.shape[1]), 0.25, F32) * part.astype(F32)
    for s, row in ((0, hid_first[0:1, :] + hid_near[0:1, :]), (2, hid_away[0:1, :])):
        small[pl.ds(10 + (meta[1] ^ s), 1), :] = row
    small[pl.ds(14 + meta[1], 1), 0:wide] = sums[0]
    small[pl.ds(18 + meta[1], 1), 0:wide] = sums[2]
    for copy in copies:
        copy.wait()


def final_rows(meta, tok, lat, a, b, c, la, lb, grad_res, params, out):
    n, m = tok.shape[0], lat.shape[0]
    for x, at, terms in ((tok, slice(0, n), (a, b)), (lat, slice(n, n + m), (la, lb))):
        grad = c[at, :].astype(F32)
        for term in terms:
            grad += term[0 : x.shape[0], :].astype(F32)
        unit, inverse = norm_parts(x[...].astype(F32))
        out[at, :] = (grad_res[at, :] + norm_back(grad, unit, inverse, param(params, GAIN1))).astype(BF)


def place_rows(meta, a, b, c, d, tok_out, lat_out):
    n = tok_out.shape[0]
    for i, ref in enumerate((a, b, c, d)):

        @pl.when(pl.program_id(0) == i)
        def _(ref=ref):
            tok_out[...] = ref[0:n, :]
            lat_out[...] = ref[n:, :]


def after(v, *deps):
    return lax.optimization_barrier((v,) + deps)[0]


def make(mesh):
    dp_size, mp_size = mesh.shape["dp"], mesh.shape["mp"]
    assert mp_size == 4 and dp_size >= 4
    dp_bits = [1 << i for i in range(dp_size.bit_length() - 1)]
    assert 1 << len(dp_bits) == dp_size
    x_bit, z_bit, rest_bits = dp_bits[0], dp_bits[1], dp_bits[2:]

    def swap(v, dp_bit, mp_bit):
        pairs = [
            (d * mp_size + m, (d ^ dp_bit) * mp_size + (m ^ mp_bit))
            for d in range(dp_size)
            for m in range(mp_size)
        ]
        return lax.ppermute(v, ("dp", "mp"), pairs)

    def per_device(
        tokens,
        latents,
        image_of_group,
        token_valid,
        norm1_gain,
        norm1_shift,
        w_qkv,
        b_qv,
        w_out,
        b_out,
        norm2_gain,
        norm2_shift,
        w_up,
        b_up,
        w_down,
        b_down,
        cot_tokens,
        cot_latents,
    ):
        dp_at, mp_at = lax.axis_index("dp"), lax.axis_index("mp")
        tok_count, width = tokens.shape
        lat_count = latents.shape[0]
        groups = lat_count // LAT
        wide = w_qkv.shape[2]
        hidden = w_up.shape[1]
        tok_own, lat_own = tok_count // 4, lat_count // 4
        rows_own = tok_own + lat_own
        all_lat = dp_size * lat_count
        meta = jnp.stack([dp_at, mp_at]).astype(jnp.int32)
        count = jnp.sum(token_valid.reshape(groups, GROUP), 1).astype(jnp.int32)
        par = whole((8, width))
        w_t = jnp.transpose(w_qkv, (0, 2, 1))
        w_all = (3, wide, width)
        quarter, small = width // 4, wide // 4
        half = 2 * quarter
        big = (rows_own, width)
        chip_rows, chip_tok, chip_lat = 2 * rows_own, 2 * tok_own, 2 * lat_own
        vec = pl.BlockSpec((width,), lambda *_: (0,))

        def out(shape, kind=BF):
            return (shape, kind, whole(shape))

        def kept_out(shape, kind=BF):
            return (shape, kind, kept(shape))

        def any_out(shape, kind=BF):
            return (shape, kind, ANY)

        def dma(n):
            return pltpu.SemaphoreType.DMA((n,))

        def cube(v, vx=None, vz=None, vxz=None):
            vx, vz, vxz = (v if w is None else w for w in (vx, vz, vxz))
            return swap(vx, x_bit, 0), swap(vz, z_bit, 0), swap(vxz, x_bit | z_bit, 0)

        def all_latents(v):
            v = jnp.concatenate((v,) + cube(v), 0)
            for bit in rest_bits:
                v = jnp.concatenate([v, swap(v, bit, 0)], 0)
            return v

        part_block = pl.BlockSpec((quarter, width), lambda i, meta: ((meta[0] & 1) * 2 + ((meta[0] >> 1) & 1), 0))
        lat_rel, lat_half, o0, weight_part, params = call(
            prepare,
            name="prepare",
            scalars=1,
            ins=[whole((lat_count, width)), whole((wide, width))] + [vec] * 7 + [part_block, part_block],
            outs=[out((lat_count, width)), out((chip_lat, width)), out((wide + 16, width)), out((half, width)), out((8, width), F32)],
            us=2,
        )(meta, latents, w_out, norm1_gain, norm1_shift, b_out, norm2_gain, norm2_shift, b_down, b_up, w_up, w_down)
        lat_four = jnp.concatenate((lat_half,) + cube(lat_half), 0)
        w_own = swap(weight_part, 0, 2)
        o2 = swap(o0, 0, 2)

        normed_lat, ql, kl, vl = call(
            latent_rows,
            name="latent_rows",
            scalars=0,
            ins=[whole((lat_count, width)), par, whole(w_all), whole((2, wide))],
            outs=[out((lat_count, width))] + [out((lat_count, wide), F32)] * 3,
            us=2,
        )(lat_rel, params, w_t, b_qv)

        def cot_through(slot, meta):
            return call(
                cot_back,
                name="cot_back",
                scalars=1,
                ins=[
                    pl.BlockSpec((tok_own, width), lambda i, meta: (meta[1] ^ slot, 0), pipeline_mode=pl.Buffered(1)),
                    pl.BlockSpec((lat_own, width), lambda i, meta: (meta[1] ^ slot, 0), pipeline_mode=pl.Buffered(1)),
                    whole((hidden, width)),
                ],
                outs=[out((rows_own, hidden))],
                us=4,
            )(meta, cot_tokens, cot_latents, w_down)[0]

        cot_own = cot_through(0, after(meta, kl))
        lat_here = lat_four = after(lat_four, cot_own)
        for bit in rest_bits:
            lat_here = jnp.concatenate([lat_here, swap(lat_here, bit, 0)], 0)

        def near_forward(base, *deps):
            def run(*args):
                return forward_near(base, *args)

            rows = lambda wide_here: pl.BlockSpec((tok_own, wide_here), lambda i, *_: (i, 0))
            lat_block = pl.BlockSpec((lat_own, wide), lambda i, *_: (i + base, 0))
            each = groups // 4
            return call(
                run,
                name="forward_near",
                grid=(2,),
                scalars=2,
                ins=[
                    pl.BlockSpec((tok_own, width), lambda i, meta, _: (meta[1] ^ (i + base), 0)),
                    lat_block,
                    lat_block,
                    par,
                    whole(w_all),
                    whole((2, wide)),
                ],
                outs=[((chip_tok, width), BF, rows(width))]
                + [((chip_tok, wide), BF, rows(wide))] * 3
                + [((wide, chip_tok), BF, pl.BlockSpec((wide, tok_own), lambda i, *_: (0, i)))]
                + [((2 * each, 8, GROUP), F32, pl.BlockSpec((each, 8, GROUP), lambda i, *_: (i, 0, 0)))],
                us=8,
            )(meta, count, tokens, after(kl, *deps), vl, params, w_t, b_qv)

        normed_b, q_b, k_b, v_b, t_b, log_b = near_forward(2, lat_four)
        t_far = swap(t_b, 0, 2)
        lat_here = after(lat_here, t_b)
        normed_a, q_a, k_a, v_a, t_near, log_a = near_forward(0, lat_here)
        w_x, w_z, w_xz = cube(after(w_own, t_near))
        lat_all = [v.reshape(dp_size, chip_lat, width) for v in (lat_here, swap(lat_here, 0, 1))]
        lat_all = jnp.concatenate(lat_all, 1).reshape(all_lat, width)
        lat_all = after(lat_all, t_near)

        chunk = min(512, all_lat)
        qa, ka, va, l_near, l_b, far, far_logs = call(
            forward_far,
            name="forward_far",
            grid=(all_lat // chunk,),
            scalars=3,
            ins=[pl.BlockSpec((chunk, width), lambda i, *_: (i, 0)), par, whole(w_all), whole((2, wide))]
            + [whole((chip_tok, wide))] * 4
            + [whole((lat_count, wide))],
            outs=[out((all_lat, wide))] * 3
            + [kept_out((chip_lat, wide))] * 2
            + [kept_out((lat_count, wide)), kept_out((lat_count, 2 * HEAD))],
            us=6,
        )(meta, count, image_of_group, lat_all, params, w_t, b_qv, k_a, k_b, v_a, v_b, ql)
        l_far = swap(l_b, 0, 2)

        out_pack = whole((wide + 16, width))
        mixed_specs = [whole((wide, chip_tok))] * 2 + [whole((chip_lat, wide))] * 2
        cot_sib = cot_through(1, after(meta, far))

        def out_rows_of(slot, kind, o0):
            return call(
                project_out,
                name="project_out",
                scalars=0,
                ins=[pl.BlockSpec((wide, tok_own), lambda *_: (0, slot), pipeline_mode=pl.Buffered(1))] * 2
                + [pl.BlockSpec((lat_own, wide), lambda *_: (slot, 0), pipeline_mode=pl.Buffered(1))] * 2
                + [out_pack] * 2,
                outs=[out(big, kind)],
                us=3,
            )(t_near, t_far, l_near, l_far, o0, o2)[0]

        attn_send = out_rows_of(1, BF, after(o0, cot_sib))
        attn_own = out_rows_of(0, F32, after(o0, attn_send))
        attn_got = swap(attn_send, 0, 1)
        own_tok = pl.BlockSpec((tok_own, width), lambda i, meta, _: (meta[1], 0), pipeline_mode=pl.Buffered(1))
        own_lat = pl.BlockSpec((lat_own, width), lambda i, meta, _: (meta[1], 0), pipeline_mode=pl.Buffered(1))
        residual, n2, stats1 = call(
            add_norm,
            name="add_norm",
            scalars=2,
            ins=[par, whole(big), whole(big), own_tok, whole((lat_own, width))],
            outs=[out(big, F32), out(big), out((8, width), F32)],
            us=3,
        )(meta, count, params, attn_own, attn_got, tokens, lat_rel)
        n2_sib = swap(n2, 0, 1)

        chip = (chip_rows, width)
        piece = (half, width)
        vm = pltpu.VMEM
        act_first, grad_first, bias_first = call(
            hidden_first,
            name="hidden_first",
            scalars=0,
            ins=[par, whole(big), whole((width, hidden)), whole((rows_own, hidden))],
            outs=[out((rows_own, hidden))] * 2 + [out((8, hidden), F32)],
            us=4,
        )(params, n2, w_up, cot_own)
        branch, back, a0, a1, a2, a3, bias_near = call(
            hidden_own,
            name="hidden_own",
            scalars=1,
            ins=[par] + [ANY] * 9,
            outs=[any_out(chip, F32), any_out(chip, F32)] + [any_out(piece)] * 4 + [out((8, hidden), F32)],
            scratch=[
                vm(chip, BF),
                vm(chip, BF),
                vm((2, width, hidden), BF),
                vm(chip, F32),
                vm(chip, F32),
                vm((chip_rows, hidden), BF),
                vm((chip_rows, hidden), BF),
                vm((rows_own, hidden), BF),
                vm((width + hidden, width), BF),
                dma(11),
                dma(10),
            ],
            us=12,
        )(meta, params, n2, n2_sib, cot_tokens, cot_latents, w_up, w_down, cot_sib, act_first, grad_first)
        near_parts = (a0,) + cube(None, a1, a2, a3)

        branch, back, middle_send, act, grad, bias_away = call(
            hidden_away,
            name="hidden_away",
            scalars=1,
            ins=[out_pack] + [ANY] * 10,
            outs=[any_out(big, F32), any_out(big, F32), any_out(chip), any_out((chip_rows, hidden)), any_out((chip_rows, hidden))]
            + [out((8, hidden), F32)],
            scratch=[
                vm(chip, BF),
                vm(chip, BF),
                vm((2, width, hidden), BF),
                vm(chip, F32),
                vm(chip, F32),
                vm((chip_rows, hidden), BF),
                vm((chip_rows, hidden), BF),
                vm(chip, BF),
                dma(16),
                dma(6),
            ],
            us=10,
        )(meta, o2, n2, n2_sib, cot_tokens, cot_latents, w_own, w_x, w_z, w_xz, branch, back)
        middle_got = swap(middle_send, 0, 1)

        b0, b1, b2, b3 = call(
            away_grads,
            name="away_grads",
            scalars=1,
            ins=[ANY] * 6,
            outs=[any_out(piece)] * 4,
            scratch=[
                vm(chip, BF),
                vm(chip, BF),
                vm((chip_rows, hidden), BF),
                vm((chip_rows, hidden), BF),
                vm((width + hidden, width), BF),
                dma(8),
                dma(8),
            ],
            us=6,
        )(meta, n2, n2_sib, cot_tokens, cot_latents, act, grad)

        out_rows, grad_res, grad_attn, stats2 = call(
            middle_rows,
            name="middle_rows",
            scalars=2,
            ins=[par, whole(big), whole(big), whole(big), whole(chip), own_tok, own_lat],
            outs=[out(big), out(big, F32), out(big), out((8, width), F32)],
            us=5,
            deps=(b0,),
        )(meta, count, params, residual, branch, back, middle_got, cot_tokens, cot_latents)
        grad_attn_sib = swap(grad_attn, 0, 1)

        def terms(n, at=0):
            return [(i, at) for i in range(n)]

        sides4 = ((0, 0), (1, 0), (0, 1), (1, 1))

        def at(d, size, base=0):
            return lambda x, z: base + ((x ^ d[0]) * 2 + (z ^ d[1])) * size


        (near_sum,) = combine("near_sum", meta, near_parts, [(half, BF, [(0, half, terms(4))])], us=2)
        away_parts = (b0,) + cube(None, *(after(v, near_sum) for v in (b1, b2, b3)))

        g_near, g_send, d_near, d_send, out_grad, out_grad_send = call(
            back_out,
            name="back_out",
            scalars=0,
            ins=[whole(big), whole(big), out_pack, out_pack] + mixed_specs,
            outs=[out((wide, chip_tok))] * 2 + [out((chip_lat, wide))] * 2 + [out((wide, width))] * 2,
            us=4,
            deps=(near_sum,),
        )(grad_attn, grad_attn_sib, o0, o2, t_near, t_far, l_near, l_far)
        d_far = swap(d_send, 0, 2)
        g_far = swap(g_send, 0, 2)
        out_grad_got = swap(after(out_grad_send, g_far), 0, 2)

        zero_w, zero_b = jnp.zeros((8, LANES), F32), jnp.zeros((8, LANES), F32)

        def rows_backward(first, steps, half_in, g, d, gw, bias, *deps):
            normed, q, k, v, log = half_in
            base = first % 2

            def rows(n, wide_here, shift):
                return pl.BlockSpec((n, wide_here), lambda i, *_: (i + shift, 0))

            def run(*args):
                return backward_rows(first, gw is None, *args)

            init = (zero_w, zero_b) if gw is None else (gw, bias)
            return call(
                run,
                name="backward_rows",
                grid=(steps,),
                scalars=2,
                ins=[
                    rows(tok_own, width, base),
                    *[rows(tok_own, wide, base)] * 3,
                    *[rows(lat_own, wide, first)] * 3,
                    pl.BlockSpec((groups // 4, 8, GROUP), lambda i, *_: (i + base, 0, 0)),
                    rows(lat_own, wide, first),
                    rows(lat_own, 2 * HEAD, first),
                    pl.BlockSpec((wide, tok_own), lambda i, *_: (0, i + base)),
                    rows(lat_own, wide, base),
                    whole(w_all),
                    whole(init[0].shape),
                    whole(init[1].shape),
                ],
                outs=[kept_out((tok_own, width))] * steps
                + [kept_out(w_all, F32), kept_out((8, wide), F32)]
                + [((steps * lat_own, wide), F32, rows(lat_own, wide, 0))] * 3,
                us=7 * steps,
                deps=deps,
            )(meta, count, normed, q, k, v, ql, kl, vl, log, far, far_logs, g, d, w_t, *init)

        half_a, half_b = (normed_a, q_a, k_a, v_a, log_a), (normed_b, q_b, k_b, v_b, log_b)
        part0, gw, bias, *near_0 = rows_backward(0, 1, half_a, g_near, d_near, None, None)
        bundle_own, bundle = call(
            latent_bundle,
            name="latent_bundle",
            scalars=0,
            ins=[whole((chip_lat, wide))] * 2 + [whole((lat_count, wide)), whole((lat_count, 2 * HEAD))],
            outs=[out((lat_count, 4 * HEAD))] * 2,
            us=2,
            deps=(part0,),
        )(d_near, d_far, far, far_logs)
        steps = [bundle]

        def spread(bit):
            got = swap(steps[0], bit, 0)
            return lambda done: steps.__setitem__(0, jnp.concatenate([after(steps[0], done), got], 0))

        join = spread(x_bit)
        part1, gw, bias, *near_1 = rows_backward(1, 1, half_a, g_near, d_near, gw, bias, bundle_own)
        got1 = swap(part1, 0, 1)
        join(part1)
        join = spread(z_bit)
        part3, gw, bias, *near_3 = rows_backward(3, 1, half_b, g_far, d_far, gw, bias)
        join(part3)
        for bit in rest_bits[:-1]:
            spread(bit)(part3)
        join = spread(rest_bits[-1]) if rest_bits else None
        (away_sum,) = combine("away_sum", meta, away_parts, [(half, BF, [(0, half, terms(4))])], us=2, deps=(part3,))
        away_got = swap(away_sum, 0, 2)
        got3 = swap(part3, 0, 1)
        part2, gw, bias, *near_2 = rows_backward(2, 1, half_b, g_far, d_far, gw, bias, away_sum)
        if rest_bits:
            join(part2)
        bundle = steps[0]
        near_all = [v for three in zip(near_0, near_1, near_2, near_3) for v in three]
        shard = (small * 4, width)
        lat_keep, lat_send, c0, c1, c2, c3, small_rows = call(
            backward_far,
            name="backward_far",
            scalars=3,
            ins=[whole((all_lat, wide))] * 3
            + [whole((lat_count, wide))] * 3
            + [whole((lat_count, 4 * HEAD)), whole((all_lat, 4 * HEAD)), whole((lat_count, width)), whole(w_all), whole(w_all)]
            + [whole((8, wide))]
            + [whole((wide, width))] * 2
            + [par]
            + [whole((8, width))] * 5
            + [whole(v.shape) for v in near_all],
            outs=[out((chip_lat, width))] * 2 + [any_out(shard)] * 4 + [out((32, width), F32)],
            scratch=[vm((4 * wide, width), BF), dma(8)],
            us=8,
        )(
            meta, count, image_of_group, qa, ka, va, ql, kl, vl, bundle_own, bundle, normed_lat, w_t, gw, bias, out_grad,
            out_grad_got, params, stats1, stats2, bias_first, bias_near, bias_away, *near_all,
        )

        lat_got = swap(lat_send, 0, 1)
        (total,) = combine(
            "weights_sum", meta, [near_sum, away_got], [(half, BF, [(0, half, terms(2))])], us=20, deps=(lat_keep,)
        )
        (there,) = combine(
            "rows_sum", meta, [part2, got3, lat_keep, lat_got],
            [(rows_own, BF, [(0, tok_own, terms(2)), (tok_own, lat_own, [(2, lat_own), (3, lat_own)])])],
            us=2, deps=(total,),
        )
        from_y = swap(there, 0, 2)
        small_rows = small_rows + swap(small_rows, 0, 1)
        small_got = swap(small_rows, 0, 2)
        rows4 = 4 * small
        qkv_parts = (c0,) + cube(None, c1, c2, c3)
        (qkv,) = combine(
            "qkv_sum", meta, qkv_parts + (small_rows, small_got),
            [(rows4 + 32, BF, [(0, rows4, terms(4)), (rows4, 32, [(4, 0), (5, 0)])])],
            us=2, deps=(there,),
        )
        (grad_rows,) = call(
            final_rows,
            name="final_rows",
            scalars=1,
            ins=[
                pl.BlockSpec((tok_own, width), lambda i, meta: (meta[1], 0), pipeline_mode=pl.Buffered(1)),
                whole((lat_own, width)),
                *[whole((tok_own, width))] * 2,
                whole(big),
                *[whole((chip_lat, width))] * 2,
                whole(big),
                par,
            ],
            outs=[out(big)],
            us=4,
            deps=(qkv,),
        )(meta, tokens, lat_rel, part0, got1, from_y, lat_keep, lat_got, grad_res, params)

        out_y = swap(after(out_rows, there), 0, 2)
        grad_y = swap(grad_rows, 0, 2)
        for bit in rest_bits:
            (total,) = combine(
                "rest_sum", meta, [total, swap(total, bit, 0)], [(half, BF, [(0, half, terms(2))])], us=2,
                deps=(grad_rows,),
            )
        four = (total,) + cube(total)
        grad_w_up, grad_w_down = combine(
            "weights_out", meta, four,
            [
                (4 * quarter, F32, [(at(d, quarter), quarter, [(i, r * quarter)]) for i, d in enumerate(sides4)])
                for r in (0, 1)
            ]
            ,
            us=5,
            deps=(grad_y, qkv,),
        )
        for bit in rest_bits:
            (qkv,) = combine("qkv_rest", meta, [qkv, swap(qkv, bit, 0)], [(rows4 + 32, BF, [(0, rows4 + 32, terms(2))])], us=2, deps=(total, total))
        four = (qkv,) + cube(after(qkv, *four[1:]))
        grad_w_qkv, grad_w_out, small_rows = combine(
            "qkv_out", meta, four,
            [
                (3 * wide, F32, [(at(d, 3 * small), 3 * small, [(i, 0)]) for i, d in enumerate(sides4)]),
                (wide, F32, [(at(d, small), small, [(i, 3 * small)]) for i, d in enumerate(sides4)]),
                (32, F32, [(0, 32, terms(4, rows4))]),
            ],
            us=3,
        )
        grad_w_qkv = grad_w_qkv.reshape(3, wide, width).transpose(0, 2, 1)

        def all_rows(v, v_y):
            v_c, v_yc = swap(v, 0, 1), swap(v_y, 0, 1)
            place = lambda n: pl.BlockSpec((n, width), lambda i, meta: (meta[1] ^ i, 0))
            return call(
                place_rows,
                name="place_rows",
                grid=(4,),
                scalars=1,
                ins=[whole(big)] * 4,
                outs=[((tok_count, width), BF, place(tok_own)), ((lat_count, width), BF, place(lat_own))],
                us=4,
            )(meta, v, v_c, v_y, v_yc)

        grad_tok, grad_lat = all_rows(grad_rows, grad_y)
        out_tok, out_lat = all_rows(out_rows, out_y)

        squares = jnp.sum(jnp.stack([small_rows[1], small_rows[0], small_rows[2]]), 1)
        root_means = jnp.sqrt(squares / ((small_rows[9, 0] + small_rows[22, 0]) * width))
        grad_b_qv = jnp.stack([small_rows[14 + 4 * i : 18 + 4 * i, :wide] for i in (0, 1)])
        grad_b_qv = lax.dynamic_index_in_dim(grad_b_qv, mp_at, 1, keepdims=False)
        grad_b_up = lax.dynamic_index_in_dim(small_rows[10:14], mp_at, 0, keepdims=False)
        return (
            out_tok,
            out_lat,
            grad_tok,
            grad_lat,
            small_rows[7],
            small_rows[8],
            grad_w_qkv,
            grad_b_qv,
            grad_w_out,
            small_rows[5],
            small_rows[3],
            small_rows[4],
            grad_w_up,
            grad_b_up,
            grad_w_down,
            small_rows[6],
            root_means,
        )

    return per_device


def solution(mesh):
    rows, whole = P("dp", None), P()
    return jax.shard_map(
        make(mesh),
        mesh=mesh,
        in_specs=(
            rows,
            rows,
            whole,
            P("dp"),
            whole,
            whole,
            P(None, None, "mp"),
            P(None, "mp"),
            P("mp", None),
            whole,
            whole,
            whole,
            P(None, "mp"),
            P("mp"),
            P("mp", None),
            whole,
            rows,
            rows,
        ),
        out_specs=(
            rows,
            rows,
            rows,
            rows,
            whole,
            whole,
            P(None, None, "mp"),
            P(None, "mp"),
            P("mp", None),
            whole,
            whole,
            whole,
            P(None, "mp"),
            P("mp"),
            P("mp", None),
            whole,
            whole,
        ),
        check_vma=False,
    )
```

time: 844 us -> 313 us (0.37)
  waiting for transfers between devices: 514 us -> 47.8 us
  Pallas kernels: 0 us -> 186 us
  blocking collectives: 104 us -> 0 us
  matrix products: 80.5 us -> 0 us
  other arithmetic: 68.5 us -> 5.12 us
  starting transfers between devices: 1.66 us -> 48.6 us
  local copies, waits for them, and re-layouts: 53.7 us -> 17.4 us
  between operations: 16.2 us -> 2.49 us
    psum x4 -> x0, waiting for transfers between devices: 406 us -> none  [the longest x3 227 us: reduce_rows(): return lax.psum(partial_rows.astype(jnp.bfloat16), 'mp').astype(jnp.float32)]
    pallas_call x0 -> x34, Pallas kernels: none -> 186 us  [run(): pl.pallas_call(wrapped, name=name, out_shape=[jax.ShapeDtypeStruct(s, d)...]
    unnamed x8 -> x0, waiting for transfers between devices: 108 us -> none
    dot_general x23 -> x0, matrix products: 78 us -> none  [the longest x1 9.93 us: per_device(): jnp.einsum('rd,fd->rf', cot_rows, w_down, preferred_element_type=jnp.floa...]
    all_gather x2 -> x0, blocking collectives: 63.5 us -> none  [the longest x1 32.5 us: per_device(): lax.all_gather(lat_values, 'dp', axis=0, tiled=True)]
    reduce_sum x16 -> x2, other arithmetic: 53.5 us -> 0.75 us  [the longest x1 0.63 us: per_device(): count = jnp.sum(token_valid.reshape(groups, GROUP), 1).astype(jnp.int32)]
    ppermute x0 -> x52, starting transfers between devices: none -> 48.6 us  [swap(): return lax.ppermute(v, ('dp', 'mp'), pairs)]
    ppermute x0 -> x52, waiting for transfers between devices: none -> 47.8 us  [swap(): return lax.ppermute(v, ('dp', 'mp'), pairs)]
  transfers between devices with their start and end apart: 6 -> 52, of which waited for: 6 -> 10; matrix products, arithmetic and copies ran while one was open for 9% -> 3% of each run, Pallas kernels for 0% -> 58%
where the time goes in v2:
time: 313 us; the launch traced here: 307 us
  Pallas kernels  186 us (59%)
  starting transfers between devices  48.6 us (16%)
  waiting for transfers between devices  47.8 us (15%)
  local copies, waits for them, and re-layouts  17.4 us (6%)
  other arithmetic  5.12 us (2%)
    pallas_call x34, Pallas kernels, run(): pl.pallas_call(wrapped, name=name, out_shape=[jax.ShapeDtypeStruct(s, d)...  186 us
    ppermute x52, starting transfers between devices, swap(): return lax.ppermute(v, ('dp', 'mp'), pairs)  48.6 us
    ppermute x52, waiting for transfers between devices, swap(): return lax.ppermute(v, ('dp', 'mp'), pairs)  47.8 us
    unnamed x65, local copies, waits for them, and re-layouts  12.3 us
  transfers between devices with their start and end apart: 52, of which 10 were waited for; matrix products, arithmetic and copies ran while one was open for 3% of the time, Pallas kernels for 58%

profile of v2, /device:TPU:0, one launch (start us, length us, event | category | flops | bytes accessed | tf_op | source)
XLA Modules:
  0.0 307.3 jit_solution(11581478046858753151)
XLA Ops:
  13.2 4.3 %cot_back.2.refs_3_ = bf16[528,768]{1,0:T(8,128)(2,1)} custom-call(s32[2]{0:T(128)} %pad_add_fusion.refs_0_, bf16[2048,768]{1,0:T(8,128)(2,1)} %refs_7_.9, bf16[64,768]{1,0:T(8,128)(2,1)} %refs_8_.3, bf16[768,768]{1,0:T(8,128)(2,1)} %refs_7_.8), custom_call_target="tpu_custom_call" | custom-call | flops 40000000000 | bytes 65536 | tf_op jit(solution)/shard_map/cot_back/pallas_call | solution.py:75
  21.2 7.5 %forward_near.2 = (bf16[1024,768]{1,0:T(8,128)(2,1)}, bf16[1024,192]{1,0:T(8,128)(2,1)}, bf16[1024,192]{1,0:T(8,128)(2,1)}, bf16[1024,192]{1,0:T(8,128)(2,1)}, b...) custom-call(s32[2]{0:T(128)} %pad_add_fusion.refs_0_, s32[8]{0:T(128)} %reduce_sum.18.refs_1_, bf16[2048,768]{1,0:T(8,128)(2,1)} %refs_1_.7, ...), custom_call_target="tpu_custom_call" | custom-call | flops 80000000000 | bytes 65536 | tf_op jit(solution)/shard_map/forward_near/pallas_call | solution.py:75
  30.5 8.2 %forward_near.3 = (bf16[1024,768]{1,0:T(8,128)(2,1)}, bf16[1024,192]{1,0:T(8,128)(2,1)}, bf16[1024,192]{1,0:T(8,128)(2,1)}, bf16[1024,192]{1,0:T(8,128)(2,1)}, b...) custom-call(s32[2]{0:T(128)} %pad_add_fusion.refs_0_, s32[8]{0:T(128)} %reduce_sum.18.refs_1_, bf16[2048,768]{1,0:T(8,128)(2,1)} %refs_1_.7, ...), custom_call_target="tpu_custom_call" | custom-call | flops 80000000000 | bytes 65536 | tf_op jit(solution)/shard_map/forward_near/pallas_call | solution.py:75
  42.8 6.3 %forward_far.1 = (bf16[512,192]{1,0:T(8,128)(2,1)}, bf16[512,192]{1,0:T(8,128)(2,1)}, bf16[512,192]{1,0:T(8,128)(2,1)}, bf16[32,192]{1,0:T(8,128)(2,1)}, bf16[32...) custom-call(s32[2]{0:T(128)} %pad_add_fusion.refs_0_, s32[8]{0:T(128)} %reduce_sum.18.refs_1_, ...), custom_call_target="tpu_custom_call" | custom-call | flops 60000002048 | bytes 65536 | tf_op jit(solution)/shard_map/forward_far/pallas_call | solution.py:75
  49.5 4.2 %cot_back.3.refs_8_ = bf16[528,768]{1,0:T(8,128)(2,1)} custom-call(s32[2]{0:T(128)} %pad_add_fusion.refs_0_, bf16[2048,768]{1,0:T(8,128)(2,1)} %refs_7_.9, bf16[64,768]{1,0:T(8,128)(2,1)} %refs_8_.3, bf16[768,768]{1,0:T(8,128)(2,1)} %refs_7_.8), custom_call_target="tpu_custom_call" | custom-call | flops 40000000000 | bytes 65536 | tf_op jit(solution)/shard_map/cot_back/pallas_call | solution.py:75
  57.6 3.1 %project_out.3.refs_3_ = f32[528,768]{1,0:T(8,128)} custom-call(bf16[192,1024]{1,0:T(8,128)(2,1)} %get-tuple-element.150.refs_0_.refs_4_, bf16[192,1024]{1,0:T(8,128)(2,1)} %collective-permute-done.4.refs_1_.refs_5_, bf16[32,192]{1,0:T(8,128)(2,1)} %get-tuple-element.157.refs_2_.refs_6_, bf16[32,192]{1,0:T(8,128)(2,1)} %copy-done.29, ...), custom_call_target="tpu_custom_call" | custom-call | flops 30000001024 | bytes 65536 | tf_op jit(solution)/shard_map/project_out/pallas_call | solution.py:75
  61.6 4.5 %add_norm.1 = (f32[528,768]{1,0:T(8,128)}, bf16[528,768]{1,0:T(8,128)(2,1)}, f32[8,768]{1,0:T(8,128)}) custom-call(s32[2]{0:T(128)} %pad_add_fusion.refs_0_, s32[8]{0:T(128)} %reduce_sum.18.refs_1_, f32[8,768]{1,0:T(8,128)} %get-tuple-element.139.refs_1_.refs_5_.refs_4_.refs_2_.refs_0_.refs_17_.refs_9_, f32[528,768]{1,0:T(8,128)} %project_out.3.refs_3_, ...), custom_call_target="tpu_custom_call" | custom-call | flops 30000001024 | bytes 65536 | tf_op jit(solution)/shard_map/add_norm/pallas_call | solution.py:75
  66.6 4.5 %hidden_first.1 = (bf16[528,768]{1,0:T(8,128)(2,1)}, bf16[528,768]{1,0:T(8,128)(2,1)}, f32[8,768]{1,0:T(8,128)}) custom-call(f32[8,768]{1,0:T(8,128)} %get-tuple-element.139.refs_1_.refs_5_.refs_4_.refs_2_.refs_0_.refs_17_.refs_9_, bf16[528,768]{1,0:T(8,128)(2,1)} %get-tuple-element.165.refs_1_.refs_2_, bf16[768,768]{1,0:T(8,128)(2,1)} %refs_6_.5, ...), custom_call_target="tpu_custom_call" | custom-call | flops 40000000000 | bytes 65536 | tf_op jit(solution)/shard_map/hidden_first/pallas_call | solution.py:75
  72.0 13.2 %hidden_own.1 = (f32[1056,768]{1,0:T(8,128)}, f32[1056,768]{1,0:T(8,128)}, bf16[384,768]{1,0:T(8,128)(2,1)}, bf16[384,768]{1,0:T(8,128)(2,1)}, bf16[384,768]{1,0...) custom-call(s32[2]{0:T(128)} %pad_add_fusion.refs_0_, ...), custom_call_target="tpu_custom_call" | custom-call | flops 120000004096 | bytes 65536 | tf_op jit(solution)/shard_map/hidden_own/pallas_call | solution.py:75
  88.8 13.8 %hidden_away.1 = (f32[528,768]{1,0:T(8,128)}, f32[528,768]{1,0:T(8,128)}, bf16[1056,768]{1,0:T(8,128)(2,1)}, bf16[1056,768]{1,0:T(8,128)(2,1)}, bf16[1056,768]{1,0:T(8,128)(2,1)}, /*index=5*/f32[8,768]{1,0:T(8,128)}) custom-call(s32[2]{0:T(128)} %pad_add_fusion.refs_0_, bf16[208,768]{1,0:T(8,128)(2,1)} %collective-permute-done.7.refs_5_.refs_1_.refs_3_, ...), custom_call_target="tpu_custom_call" | custom-call | flops 99999997952 | bytes 65536 | tf_op jit(solution)/shard_map/hidden_away/pallas_call | solution.py:75
  102.7 9.0 %away_grads.1 = (bf16[384,768]{1,0:T(8,128)(2,1)}, bf16[384,768]{1,0:T(8,128)(2,1)}, bf16[384,768]{1,0:T(8,128)(2,1)}, bf16[384,768]{1,0:T(8,128)(2,1)}) custom-call(s32[2]{0:T(128)} %pad_add_fusion.refs_0_, bf16[528,768]{1,0:T(8,128)(2,1)} %get-tuple-element.165.refs_1_.refs_2_, bf16[528,768]{1,0:T(8,128)(2,1)} %copy-done.11, bf16[2048,768]{1,0:T(8,128)(2,1)} %refs_7_.9, ...), custom_call_target="tpu_custom_call" | custom-call | flops 60000002048 | bytes 65536 | tf_op jit(solution)/shard_map/away_grads/pallas_call | solution.py:75
  112.8 7.7 %middle_rows.1 = (bf16[528,768]{1,0:T(8,128)(2,1)}, f32[528,768]{1,0:T(8,128)}, bf16[528,768]{1,0:T(8,128)(2,1)}, f32[8,768]{1,0:T(8,128)}) custom-call(s32[2]{0:T(128)} %pad_add_fusion.refs_0_, s32[8]{0:T(128)} %reduce_sum.18.refs_1_, f32[8,768]{1,0:T(8,128)} %get-tuple-element.139.refs_1_.refs_5_.refs_4_.refs_2_.refs_0_.refs_17_.refs_9_, ...), custom_call_target="tpu_custom_call" | custom-call | flops 49999998976 | bytes 65536 | tf_op jit(solution)/shard_map/middle_rows/pallas_call | solution.py:75
  121.1 3.4 %near_sum.1.refs_8_.refs_1_ = bf16[384,768]{1,0:T(8,128)(2,1)} custom-call(s32[2]{0:T(128)} %pad_add_fusion.refs_0_, bf16[384,768]{1,0:T(8,128)(2,1)} %get-tuple-element.184.refs_1_, bf16[384,768]{1,0:T(8,128)(2,1)} %collective-permute-done.17.refs_2_, bf16[384,768]{1,0:T(8,128)(2,1)} %collective-permute-done.18.refs_3_, ...), custom_call_target="tpu_custom_call" | custom-call | flops 20000000000 | bytes 65536 | tf_op jit(solution)/shard_map/near_sum/pallas_call | solution.py:75
  128.8 4.9 %back_out.1 = (bf16[192,1024]{1,0:T(8,128)(2,1)}, bf16[192,1024]{1,0:T(8,128)(2,1)}, bf16[32,192]{1,0:T(8,128)(2,1)}, bf16[32,192]{1,0:T(8,128)(2,1)}, bf16[192,...) custom-call(bf16[528,768]{1,0:T(8,128)(2,1)} %get-tuple-element.183.refs_0_, bf16[528,768]{1,0:T(8,128)(2,1)} %copy-done.13, ...), custom_call_target="tpu_custom_call" | custom-call | flops 40000000000 | bytes 65536 | tf_op jit(solution)/shard_map/back_out/pallas_call | solution.py:75
  136.3 7.7 %backward_rows.4 = (bf16[512,768]{1,0:T(8,128)(2,1)}, f32[3,192,768]{2,1,0:T(8,128)}, f32[8,192]{1,0:T(8,128)}, f32[16,192]{1,0:T(8,128)}, f32[16,192]{1,0:T(8,128)}, /*index=5*/f32[16,192]{1,0:T(8,128)}) custom-call(s32[2]{0:T(128)} %pad_add_fusion.refs_0_, s32[8]{0:T(128)} %reduce_sum.18.refs_1_, bf16[1024,768]{1,0:T(8,128)(2,1)} %get-tuple-element.190.refs_2_, ...), custom_call_target="tpu_custom_call" | custom-call | flops 70000001024 | bytes 65536 | tf_op jit(solution)/shard_map/backward_rows/pallas_call | solution.py:75
  148.2 8.4 %backward_rows.5 = (bf16[512,768]{1,0:T(8,128)(2,1)}, f32[3,192,768]{2,1,0:T(8,128)}, f32[8,192]{1,0:T(8,128)}, f32[16,192]{1,0:T(8,128)}, f32[16,192]{1,0:T(8,128)}, /*index=5*/f32[16,192]{1,0:T(8,128)}) custom-call(s32[2]{0:T(128)} %pad_add_fusion.refs_0_, s32[8]{0:T(128)} %reduce_sum.18.refs_1_, bf16[1024,768]{1,0:T(8,128)(2,1)} %get-tuple-element.190.refs_2_, ...), custom_call_target="tpu_custom_call" | custom-call | flops 70000001024 | bytes 65536 | tf_op jit(solution)/shard_map/backward_rows/pallas_call | solution.py:75
  159.7 8.4 %backward_rows.6 = (bf16[512,768]{1,0:T(8,128)(2,1)}, f32[3,192,768]{2,1,0:T(8,128)}, f32[8,192]{1,0:T(8,128)}, f32[16,192]{1,0:T(8,128)}, f32[16,192]{1,0:T(8,128)}, /*index=5*/f32[16,192]{1,0:T(8,128)}) custom-call(s32[2]{0:T(128)} %pad_add_fusion.refs_0_, s32[8]{0:T(128)} %reduce_sum.18.refs_1_, bf16[1024,768]{1,0:T(8,128)(2,1)} %get-tuple-element.179.refs_2_, ...), custom_call_target="tpu_custom_call" | custom-call | flops 70000001024 | bytes 65536 | tf_op jit(solution)/shard_map/backward_rows/pallas_call | solution.py:75
  169.4 3.4 %away_sum.1.refs_17_ = bf16[384,768]{1,0:T(8,128)(2,1)} custom-call(s32[2]{0:T(128)} %pad_add_fusion.refs_0_, bf16[384,768]{1,0:T(8,128)(2,1)} %get-tuple-element.177.refs_9_.refs_1_, bf16[384,768]{1,0:T(8,128)(2,1)} %collective-permute-done.22.refs_2_, bf16[384,768]{1,0:T(8,128)(2,1)} %collective-permute-done.23.refs_3_, ...), custom_call_target="tpu_custom_call" | custom-call | flops 20000000000 | bytes 65536 | tf_op jit(solution)/shard_map/away_sum/pallas_call | solution.py:75
  174.3 8.2 %backward_rows.7 = (bf16[512,768]{1,0:T(8,128)(2,1)}, f32[3,192,768]{2,1,0:T(8,128)}, f32[8,192]{1,0:T(8,128)}, f32[16,192]{1,0:T(8,128)}, f32[16,192]{1,0:T(8,128)}, /*index=5*/f32[16,192]{1,0:T(8,128)}) custom-call(s32[2]{0:T(128)} %pad_add_fusion.refs_0_, s32[8]{0:T(128)} %reduce_sum.18.refs_1_, bf16[1024,768]{1,0:T(8,128)(2,1)} %get-tuple-element.179.refs_2_, ...), custom_call_target="tpu_custom_call" | custom-call | flops 70000001024 | bytes 65536 | tf_op jit(solution)/shard_map/backward_rows/pallas_call | solution.py:75
  183.3 7.9 %backward_far.1 = (bf16[32,768]{1,0:T(8,128)(2,1)}, bf16[32,768]{1,0:T(8,128)(2,1)}, bf16[192,768]{1,0:T(8,128)(2,1)}, bf16[192,768]{1,0:T(8,128)(2,1)}, bf16[19...) custom-call(s32[2]{0:T(128)} %pad_add_fusion.refs_0_, s32[8]{0:T(128)} %reduce_sum.18.refs_1_, ...), custom_call_target="tpu_custom_call" | custom-call | flops 80000000000 | bytes 65536 | tf_op jit(solution)/shard_map/backward_far/pallas_call | solution.py:75
  201.4 3.1 %rows_sum.1.refs_7_ = bf16[528,768]{1,0:T(8,128)(2,1)} custom-call(s32[2]{0:T(128)} %pad_add_fusion.refs_0_, bf16[512,768]{1,0:T(8,128)(2,1)} %get-tuple-element.210.refs_1_, bf16[512,768]{1,0:T(8,128)(2,1)} %collective-permute-done.25.refs_2_, bf16[32,768]{1,0:T(8,128)(2,1)} %get-tuple-element.242.refs_3_.refs_6_, ...), custom_call_target="tpu_custom_call" | custom-call | flops 20000000000 | bytes 65536 | tf_op jit(solution)/shard_map/rows_sum/pallas_call | solution.py:75
  207.8 7.1 %collective-permute-done.38.refs_4_ = bf16[192,768]{1,0:T(8,128)(2,1)S(1)} collective-permute-done((bf16[192,768]{1,0:T(8,128)(2,1)S(1)}, bf16[192,768]{1,0:T(8,128)(2,1)S(1)}, u32[]{:S(2)}, u32[]{:S(2)}) %collective-permute-start.38) | collective-permute-done | bytes 294944 | tf_op jit(solution)/shard_map/ppermute | solution.py:756
  219.7 7.9 %collective-permute-done.35.refs_5_ = bf16[528,768]{1,0:T(8,128)(2,1)S(1)} collective-permute-done((bf16[528,768]{1,0:T(8,128)(2,1)}, bf16[528,768]{1,0:T(8,128)(2,1)S(1)}, u32[]{:S(2)}, u32[]{:S(2)}) %collective-permute-start.35) | collective-permute-done | bytes 811040 | tf_op jit(solution)/shard_map/ppermute | solution.py:756
  228.5 5.2 %final_rows.1.refs_1_.refs_3_ = bf16[528,768]{1,0:T(8,128)(2,1)} custom-call(s32[2]{0:T(128)} %pad_add_fusion.refs_0_, bf16[2048,768]{1,0:T(8,128)(2,1)} %refs_1_.7, bf16[64,768]{1,0:T(8,128)(2,1)} %get-tuple-element.140.refs_0_.refs_6_.refs_2_, bf16[512,768]{1,0:T(8,128)(2,1)} %get-tuple-element.197.refs_4_.refs_3_, ...), custom_call_target="tpu_custom_call" | custom-call | flops 40000000000 | bytes 65536 | tf_op jit(solution)/shard_map/final_rows/pallas_call | solution.py:75
  233.7 8.6 %collective-permute-done.45.refs_2_ = bf16[384,768]{1,0:T(8,128)(2,1)S(1)} collective-permute-done((bf16[384,768]{1,0:T(8,128)(2,1)S(1)}, bf16[384,768]{1,0:T(8,128)(2,1)S(1)}, u32[]{:S(2)}, u32[]{:S(2)}) %collective-permute-start.45) | collective-permute-done | bytes 589856 | tf_op jit(solution)/shard_map/ppermute | solution.py:756
  253.2 5.1 %collective-permute-done.46.refs_2_ = bf16[384,768]{1,0:T(8,128)(2,1)S(1)} collective-permute-done((bf16[384,768]{1,0:T(8,128)(2,1)}, bf16[384,768]{1,0:T(8,128)(2,1)S(1)}, u32[]{:S(2)}, u32[]{:S(2)}) %collective-permute-start.46) | collective-permute-done | bytes 589856 | tf_op jit(solution)/shard_map/ppermute | solution.py:756
  258.3 5.1 %collective-permute-done.47.refs_3_ = bf16[384,768]{1,0:T(8,128)(2,1)S(1)} collective-permute-done((bf16[384,768]{1,0:T(8,128)(2,1)}, bf16[384,768]{1,0:T(8,128)(2,1)S(1)}, u32[]{:S(2)}, u32[]{:S(2)}) %collective-permute-start.47) | collective-permute-done | bytes 589856 | tf_op jit(solution)/shard_map/ppermute | solution.py:756
  263.4 9.6 %collective-permute-done.48.refs_4_ = bf16[384,768]{1,0:T(8,128)(2,1)S(1)} collective-permute-done((bf16[384,768]{1,0:T(8,128)(2,1)}, bf16[384,768]{1,0:T(8,128)(2,1)S(1)}, u32[]{:S(2)}, u32[]{:S(2)}) %collective-permute-start.48) | collective-permute-done | bytes 589856 | tf_op jit(solution)/shard_map/ppermute | solution.py:756
  275.3 4.7 %weights_out.1 = (f32[768,768]{1,0:T(8,128)}, f32[768,768]{1,0:T(8,128)}) custom-call(s32[2]{0:T(128)} %pad_add_fusion.refs_0_, bf16[384,768]{1,0:T(8,128)(2,1)} %rest_sum.1.refs_3_.refs_4_.refs_1_, bf16[384,768]{1,0:T(8,128)(2,1)} %copy-done.18, bf16[384,768]{1,0:T(8,128)(2,1)} %copy-done.20, bf16[384,768]{1,0:T(8,128)(2,1)} %copy-done.21, ...), custom_call_target="tpu_custom_call" | custom-call | flops 49999998976 | bytes 65536 | tf_op jit(solution)/shard_map/weights_out/pallas_call | solution.py:75
  282.2 4.7 %place_rows.2 = (bf16[2048,768]{1,0:T(8,128)(2,1)}, bf16[64,768]{1,0:T(8,128)(2,1)}) custom-call(s32[2]{0:T(128)} %pad_add_fusion.refs_0_, bf16[528,768]{1,0:T(8,128)(2,1)} %get-tuple-element.244.refs_1_, bf16[528,768]{1,0:T(8,128)(2,1)} %copy-done.12, bf16[528,768]{1,0:T(8,128)(2,1)} %copy-done.9, bf16[528,768]{1,0:T(8,128)(2,1)} %copy-done.14), custom_call_target="tpu_custom_call" | custom-call | flops 40000000000 | bytes 65536 | tf_op jit(solution)/shard_map/place_rows/pallas_call | solution.py:75
  290.0 3.5 %qkv_out.1 = (f32[576,768]{1,0:T(8,128)}, f32[192,768]{1,0:T(8,128)}, f32[32,768]{1,0:T(8,128)}) custom-call(s32[2]{0:T(128)} %pad_add_fusion.refs_0_, bf16[224,768]{1,0:T(8,128)(2,1)} %qkv_rest.1.refs_1_, bf16[224,768]{1,0:T(8,128)(2,1)} %copy-done.23, bf16[224,768]{1,0:T(8,128)(2,1)} %collective-permute-done.50.refs_3_, bf16[224,768]{1,0:T(8,128)(2,1)} %copy-done.25), custom_call_target="tpu_custom_call" | custom-call | flops 30000001024 | bytes 65536 | tf_op jit(solution)/shard_map/qkv_out/pallas_call | solution.py:75
  302.3 4.7 %place_rows.3 = (bf16[2048,768]{1,0:T(8,128)(2,1)}, bf16[64,768]{1,0:T(8,128)(2,1)}) custom-call(s32[2]{0:T(128)} %pad_add_fusion.refs_0_, bf16[528,768]{1,0:T(8,128)(2,1)} %final_rows.1.refs_1_.refs_3_, bf16[528,768]{1,0:T(8,128)(2,1)} %copy-done.8, bf16[528,768]{1,0:T(8,128)(2,1)} %copy-done.7, bf16[528,768]{1,0:T(8,128)(2,1)} %copy-done.10), custom_call_target="tpu_custom_call" | custom-call | flops 40000000000 | bytes 65536 | tf_op jit(solution)/shard_map/place_rows/pallas_call | solution.py:75
  (189 shorter events, 96.7 us)
Async XLA Ops:
  4.2 13.9 %collective-permute-start = (bf16[32,768]{1,0:T(8,128)(2,1)}, bf16[32,768]{1,0:T(8,128)(2,1)S(1)}, u32[]{:S(2)}, u32[]{:S(2)}) collective-permute-start(bf16[32,768]{1,0:T(8,128)(2,1)} %get-tuple-element.142), channel_id=1, source_target_pairs={{0,4},{1,5},{2,6},{3,7},{4,0},{5,1},{6,2},{7,3},{8,12},{9,13},{10,... | collective-permute-start | bytes 147464 | tf_op jit(solution)/shard_map/ppermute | solution.py:756
  8.7 45.0 %collective-permute-start.7 = (bf16[208,768]{1,0:T(8,128)(2,1)}, bf16[208,768]{1,0:T(8,128)(2,1)}, u32[]{:S(2)}, u32[]{:S(2)}) collective-permute-start(bf16[208,768]{1,0:T(8,128)(2,1)} %get-tuple-element.163.refs_4_.refs_2_), channel_id=1, source_target_pairs={{0,2},{1,3},{2,0},{3,1},{4,6},{5,7},{6,4},{7,5},{8,10},{9,11},{10,... | collective-permute-start | bytes 958472 | tf_op jit(solution)/shard_map/ppermute | solution.py:756
  10.7 28.0 %collective-permute-start.10 = (bf16[384,768]{1,0:T(8,128)(2,1)}, bf16[384,768]{1,0:T(8,128)(2,1)}, u32[]{:S(2)}, u32[]{:S(2)}) collective-permute-start(bf16[384,768]{1,0:T(8,128)(2,1)} %get-tuple-element.166), channel_id=1, source_target_pairs={{0,2},{1,3},{2,0},{3,1},{4,6},{5,7},{6,4},{7,5},{8,10},{9,11},{10,... | collective-permute-start | bytes 1769480 | tf_op jit(solution)/shard_map/ppermute | solution.py:756
  28.8 25.3 %collective-permute-start.4 = (bf16[192,1024]{1,0:T(8,128)(2,1)}, bf16[192,1024]{1,0:T(8,128)(2,1)}, u32[]{:S(2)}, u32[]{:S(2)}) collective-permute-start(bf16[192,1024]{1,0:T(8,128)(2,1)} %get-tuple-element.147), channel_id=1, source_target_pairs={{0,2},{1,3},{2,0},{3,1},{4,6},{5,7},{6,4},{7,5},{8,10},{9,11},{10,... | collective-permute-start | bytes 1179656 | tf_op jit(solution)/shard_map/ppermute | solution.py:756
  38.7 49.7 %collective-permute-start.11 = (bf16[384,768]{1,0:T(8,128)(2,1)}, bf16[384,768]{1,0:T(8,128)(2,1)}, u32[]{:S(2)}, u32[]{:S(2)}) collective-permute-start(bf16[384,768]{1,0:T(8,128)(2,1)} %collective-permute-done.10.refs_6_), channel_id=1, source_target_pairs={{0,4},{1,5},{2,6},{3,7},{4,0},{5,1},{6,2},{7,3},{8,12},{9,13},{10,... | collective-permute-start | bytes 1769480 | tf_op jit(solution)/shard_map/ppermute | solution.py:756
  40.2 48.6 %collective-permute-start.12 = (bf16[384,768]{1,0:T(8,128)(2,1)}, bf16[384,768]{1,0:T(8,128)(2,1)}, u32[]{:S(2)}, u32[]{:S(2)}) collective-permute-start(bf16[384,768]{1,0:T(8,128)(2,1)} %collective-permute-done.10.refs_6_), channel_id=1, source_target_pairs={{0,8},{1,9},{2,10},{3,11},{4,12},{5,13},{6,14},{7,15},{8,0},{9,1},... | collective-permute-start | bytes 1769480 | tf_op jit(solution)/shard_map/ppermute | solution.py:756
  53.7 35.1 %collective-permute-start.13 = (bf16[384,768]{1,0:T(8,128)(2,1)}, bf16[384,768]{1,0:T(8,128)(2,1)}, u32[]{:S(2)}, u32[]{:S(2)}) collective-permute-start(bf16[384,768]{1,0:T(8,128)(2,1)} %collective-permute-done.10.refs_6_), channel_id=1, source_target_pairs={{0,12},{1,13},{2,14},{3,15},{4,8},{5,9},{6,10},{7,11},{8,4},{9,5},... | collective-permute-start | bytes 1769480 | tf_op jit(solution)/shard_map/ppermute | solution.py:756
  85.2 35.8 %collective-permute-start.17 = (bf16[384,768]{1,0:T(8,128)(2,1)}, bf16[384,768]{1,0:T(8,128)(2,1)}, u32[]{:S(2)}, u32[]{:S(2)}) collective-permute-start(bf16[384,768]{1,0:T(8,128)(2,1)} %get-tuple-element.185), channel_id=1, source_target_pairs={{0,4},{1,5},{2,6},{3,7},{4,0},{5,1},{6,2},{7,3},{8,12},{9,13},{10,... | collective-permute-start | bytes 1769480 | tf_op jit(solution)/shard_map/ppermute | solution.py:756
  86.8 34.3 %collective-permute-start.18 = (bf16[384,768]{1,0:T(8,128)(2,1)}, bf16[384,768]{1,0:T(8,128)(2,1)}, u32[]{:S(2)}, u32[]{:S(2)}) collective-permute-start(bf16[384,768]{1,0:T(8,128)(2,1)} %get-tuple-element.186), channel_id=1, source_target_pairs={{0,8},{1,9},{2,10},{3,11},{4,12},{5,13},{6,14},{7,15},{8,0},{9,1},... | collective-permute-start | bytes 1769480 | tf_op jit(solution)/shard_map/ppermute | solution.py:756
  88.4 32.7 %collective-permute-start.19 = (bf16[384,768]{1,0:T(8,128)(2,1)}, bf16[384,768]{1,0:T(8,128)(2,1)}, u32[]{:S(2)}, u32[]{:S(2)}) collective-permute-start(bf16[384,768]{1,0:T(8,128)(2,1)} %get-tuple-element.187), channel_id=1, source_target_pairs={{0,12},{1,13},{2,14},{3,15},{4,8},{5,9},{6,10},{7,11},{8,4},{9,5},... | collective-permute-start | bytes 1769480 | tf_op jit(solution)/shard_map/ppermute | solution.py:756
  124.4 45.0 %collective-permute-start.24 = (bf16[384,768]{1,0:T(8,128)(2,1)}, bf16[384,768]{1,0:T(8,128)(2,1)}, u32[]{:S(2)}, u32[]{:S(2)}) collective-permute-start(bf16[384,768]{1,0:T(8,128)(2,1)} %get-tuple-element.208), channel_id=1, source_target_pairs={{0,12},{1,13},{2,14},{3,15},{4,8},{5,9},{6,10},{7,11},{8,4},{9,5},... | collective-permute-start | bytes 1769480 | tf_op jit(solution)/shard_map/ppermute | solution.py:756
  126.9 42.5 %collective-permute-start.23 = (bf16[384,768]{1,0:T(8,128)(2,1)}, bf16[384,768]{1,0:T(8,128)(2,1)}, u32[]{:S(2)}, u32[]{:S(2)}) collective-permute-start(bf16[384,768]{1,0:T(8,128)(2,1)} %get-tuple-element.206), channel_id=1, source_target_pairs={{0,8},{1,9},{2,10},{3,11},{4,12},{5,13},{6,14},{7,15},{8,0},{9,1},... | collective-permute-start | bytes 1769480 | tf_op jit(solution)/shard_map/ppermute | solution.py:756
  127.4 42.0 %collective-permute-start.22 = (bf16[384,768]{1,0:T(8,128)(2,1)}, bf16[384,768]{1,0:T(8,128)(2,1)}, u32[]{:S(2)}, u32[]{:S(2)}) collective-permute-start(bf16[384,768]{1,0:T(8,128)(2,1)} %get-tuple-element.204), channel_id=1, source_target_pairs={{0,4},{1,5},{2,6},{3,7},{4,0},{5,1},{6,2},{7,3},{8,12},{9,13},{10,... | collective-permute-start | bytes 1769480 | tf_op jit(solution)/shard_map/ppermute | solution.py:756
  133.7 24.5 %collective-permute-start.20 = (bf16[192,1024]{1,0:T(8,128)(2,1)}, bf16[192,1024]{1,0:T(8,128)(2,1)}, u32[]{:S(2)}, u32[]{:S(2)}) collective-permute-start(bf16[192,1024]{1,0:T(8,128)(2,1)} %get-tuple-element.188), channel_id=1, source_target_pairs={{0,2},{1,3},{2,0},{3,1},{4,6},{5,7},{6,4},{7,5},{8,10},{9,11},{10,... | collective-permute-start | bytes 1179656 | tf_op jit(solution)/shard_map/ppermute | solution.py:756
  158.2 25.0 %collective-permute-start.29 = (bf16[192,768]{1,0:T(8,128)(2,1)}, bf16[192,768]{1,0:T(8,128)(2,1)}, u32[]{:S(2)}, u32[]{:S(2)}) collective-permute-start(bf16[192,768]{1,0:T(8,128)(2,1)} %get-tuple-element.224), channel_id=1, source_target_pairs={{0,2},{1,3},{2,0},{3,1},{4,6},{5,7},{6,4},{7,5},{8,10},{9,11},{10,... | collective-permute-start | bytes 884744 | tf_op jit(solution)/shard_map/ppermute | solution.py:756
  168.2 14.3 %collective-permute-start.28 = (bf16[256,256]{1,0:T(8,128)(2,1)S(1)}, bf16[256,256]{1,0:T(8,128)(2,1)S(1)}, u32[]{:S(2)}, u32[]{:S(2)}) collective-permute-start(bf16[256,256]{1,0:T(8,128)(2,1)S(1)} %constant_dynamic-update-slice_fusion.2), channel_id=1, source_target_pairs={{0,16},{1,17},{2,18},{3,19},{4,20},{5,21},{6,22},{7,23},{8,24},{9,... | collective-permute-start | bytes 393224 | tf_op jit(solution)/shard_map/ppermute | solution.py:756
  172.8 22.1 %collective-permute-start.31 = (bf16[384,768]{1,0:T(8,128)(2,1)}, bf16[384,768]{1,0:T(8,128)(2,1)}, u32[]{:S(2)}, u32[]{:S(2)}) collective-permute-start(bf16[384,768]{1,0:T(8,128)(2,1)} %away_sum.1.refs_17_), channel_id=1, source_target_pairs={{0,2},{1,3},{2,0},{3,1},{4,6},{5,7},{6,4},{7,5},{8,10},{9,11},{10,... | collective-permute-start | bytes 1769480 | tf_op jit(solution)/shard_map/ppermute | solution.py:756
  191.3 28.4 %collective-permute-start.34 = (bf16[512,768]{1,0:T(8,128)(2,1)}, bf16[512,768]{1,0:T(8,128)(2,1)}, u32[]{:S(2)}, u32[]{:S(2)}) collective-permute-start(bf16[512,768]{1,0:T(8,128)(2,1)} %get-tuple-element.215), channel_id=1, source_target_pairs={{0,1},{1,0},{2,3},{3,2},{4,5},{5,4},{6,7},{7,6},{8,9},{9,8},{10,11... | collective-permute-start | bytes 2359304 | tf_op jit(solution)/shard_map/ppermute | solution.py:756
  192.8 13.6 %collective-permute-start.36 = (bf16[192,768]{1,0:T(8,128)(2,1)}, bf16[192,768]{1,0:T(8,128)(2,1)}, u32[]{:S(2)}, u32[]{:S(2)}) collective-permute-start(bf16[192,768]{1,0:T(8,128)(2,1)} %get-tuple-element.249), channel_id=1, source_target_pairs={{0,4},{1,5},{2,6},{3,7},{4,0},{5,1},{6,2},{7,3},{8,12},{9,13},{10,... | collective-permute-start | bytes 884744 | tf_op jit(solution)/shard_map/ppermute | solution.py:756
  198.2 16.8 %collective-permute-start.38 = (bf16[192,768]{1,0:T(8,128)(2,1)S(1)}, bf16[192,768]{1,0:T(8,128)(2,1)S(1)}, u32[]{:S(2)}, u32[]{:S(2)}) collective-permute-start(bf16[192,768]{1,0:T(8,128)(2,1)S(1)} %copy-done.26), channel_id=1, source_target_pairs={{0,12},{1,13},{2,14},{3,15},{4,8},{5,9},{6,10},{7,11},{8,4},{9,5},... | collective-permute-start | bytes 884744 | tf_op jit(solution)/shard_map/ppermute | solution.py:756
  205.5 36.8 %collective-permute-start.45 = (bf16[384,768]{1,0:T(8,128)(2,1)S(1)}, bf16[384,768]{1,0:T(8,128)(2,1)S(1)}, u32[]{:S(2)}, u32[]{:S(2)}) collective-permute-start(bf16[384,768]{1,0:T(8,128)(2,1)S(1)} %copy-done.17), channel_id=1, source_target_pairs={{0,16},{1,17},{2,18},{3,19},{4,20},{5,21},{6,22},{7,23},{8,24},{9,... | collective-permute-start | bytes 1769480 | tf_op jit(solution)/shard_map/ppermute | solution.py:756
  206.4 21.2 %collective-permute-start.35 = (bf16[528,768]{1,0:T(8,128)(2,1)}, bf16[528,768]{1,0:T(8,128)(2,1)S(1)}, u32[]{:S(2)}, u32[]{:S(2)}) collective-permute-start(bf16[528,768]{1,0:T(8,128)(2,1)} %rows_sum.1.refs_7_), channel_id=1, source_target_pairs={{0,2},{1,3},{2,0},{3,1},{4,6},{5,7},{6,4},{7,5},{8,10},{9,11},{10,... | collective-permute-start | bytes 2433032 | tf_op jit(solution)/shard_map/ppermute | solution.py:756
  218.7 30.9 %collective-permute-start.44 = (bf16[224,768]{1,0:T(8,128)(2,1)}, bf16[224,768]{1,0:T(8,128)(2,1)S(1)}, u32[]{:S(2)}, u32[]{:S(2)}) collective-permute-start(bf16[224,768]{1,0:T(8,128)(2,1)} %qkv_sum.1.refs_10_.refs_1_.refs_6_), channel_id=1, source_target_pairs={{0,16},{1,17},{2,18},{3,19},{4,20},{5,21},{6,22},{7,23},{8,24},{9,... | collective-permute-start | bytes 1032200 | tf_op jit(solution)/shard_map/ppermute | solution.py:756
  218.7 34.4 %collective-permute-start.32 = (bf16[528,768]{1,0:T(8,128)(2,1)S(1)}, bf16[528,768]{1,0:T(8,128)(2,1)S(1)}, u32[]{:S(2)}, u32[]{:S(2)}) collective-permute-start(bf16[528,768]{1,0:T(8,128)(2,1)S(1)} %copy-done.5), channel_id=1, source_target_pairs={{0,2},{1,3},{2,0},{3,1},{4,6},{5,7},{6,4},{7,5},{8,10},{9,11},{10,... | collective-permute-start | bytes 2433032 | tf_op jit(solution)/shard_map/ppermute | solution.py:756
  246.9 16.5 %collective-permute-start.47 = (bf16[384,768]{1,0:T(8,128)(2,1)}, bf16[384,768]{1,0:T(8,128)(2,1)S(1)}, u32[]{:S(2)}, u32[]{:S(2)}) collective-permute-start(bf16[384,768]{1,0:T(8,128)(2,1)} %rest_sum.1.refs_3_.refs_4_.refs_1_), channel_id=1, source_target_pairs={{0,8},{1,9},{2,10},{3,11},{4,12},{5,13},{6,14},{7,15},{8,0},{9,1},... | collective-permute-start | bytes 1769480 | tf_op jit(solution)/shard_map/ppermute | solution.py:756
  246.9 26.0 %collective-permute-start.48 = (bf16[384,768]{1,0:T(8,128)(2,1)}, bf16[384,768]{1,0:T(8,128)(2,1)S(1)}, u32[]{:S(2)}, u32[]{:S(2)}) collective-permute-start(bf16[384,768]{1,0:T(8,128)(2,1)} %rest_sum.1.refs_3_.refs_4_.refs_1_), channel_id=1, source_target_pairs={{0,12},{1,13},{2,14},{3,15},{4,8},{5,9},{6,10},{7,11},{8,4},{9,5},... | collective-permute-start | bytes 1769480 | tf_op jit(solution)/shard_map/ppermute | solution.py:756
  249.5 24.9 %collective-permute-start.42 = (bf16[528,768]{1,0:T(8,128)(2,1)S(1)}, bf16[528,768]{1,0:T(8,128)(2,1)S(1)}, u32[]{:S(2)}, u32[]{:S(2)}) collective-permute-start(bf16[528,768]{1,0:T(8,128)(2,1)S(1)} %copy-done.6), channel_id=1, source_target_pairs={{0,2},{1,3},{2,0},{3,1},{4,6},{5,7},{6,4},{7,5},{8,10},{9,11},{10,... | collective-permute-start | bytes 2433032 | tf_op jit(solution)/shard_map/ppermute | solution.py:756
  253.1 26.9 %collective-permute-start.15 = (bf16[528,768]{1,0:T(8,128)(2,1)S(1)}, bf16[528,768]{1,0:T(8,128)(2,1)S(1)}, u32[]{:S(2)}, u32[]{:S(2)}) collective-permute-start(bf16[528,768]{1,0:T(8,128)(2,1)S(1)} %copy-done.5), channel_id=1, source_target_pairs={{0,1},{1,0},{2,3},{3,2},{4,5},{5,4},{6,7},{7,6},{8,9},{9,8},{10,11... | collective-permute-start | bytes 2433032 | tf_op jit(solution)/shard_map/ppermute | solution.py:756
  258.3 42.2 %collective-permute-start.41 = (bf16[528,768]{1,0:T(8,128)(2,1)S(1)}, bf16[528,768]{1,0:T(8,128)(2,1)S(1)}, u32[]{:S(2)}, u32[]{:S(2)}) collective-permute-start(bf16[528,768]{1,0:T(8,128)(2,1)S(1)} %copy-done.6), channel_id=1, source_target_pairs={{0,1},{1,0},{2,3},{3,2},{4,5},{5,4},{6,7},{7,6},{8,9},{9,8},{10,11... | collective-permute-start | bytes 2433032 | tf_op jit(solution)/shard_map/ppermute | solution.py:756
  263.4 17.9 %collective-permute-start.33 = (bf16[528,768]{1,0:T(8,128)(2,1)S(1)}, bf16[528,768]{1,0:T(8,128)(2,1)S(1)}, u32[]{:S(2)}, u32[]{:S(2)}) collective-permute-start(bf16[528,768]{1,0:T(8,128)(2,1)S(1)} %collective-permute-done.32.refs_3_), channel_id=1, source_target_pairs={{0,1},{1,0},{2,3},{3,2},{4,5},{5,4},{6,7},{7,6},{8,9},{9,8},{10,11... | collective-permute-start | bytes 2433032 | tf_op jit(solution)/shard_map/ppermute | solution.py:756
  273.0 13.9 %collective-permute-start.49 = (bf16[224,768]{1,0:T(8,128)(2,1)}, bf16[224,768]{1,0:T(8,128)(2,1)S(1)}, u32[]{:S(2)}, u32[]{:S(2)}) collective-permute-start(bf16[224,768]{1,0:T(8,128)(2,1)} %qkv_rest.1.refs_1_), channel_id=1, source_target_pairs={{0,4},{1,5},{2,6},{3,7},{4,0},{5,1},{6,2},{7,3},{8,12},{9,13},{10,... | collective-permute-start | bytes 1032200 | tf_op jit(solution)/shard_map/ppermute | solution.py:756
  281.3 19.3 %collective-permute-start.43 = (bf16[528,768]{1,0:T(8,128)(2,1)}, bf16[528,768]{1,0:T(8,128)(2,1)S(1)}, u32[]{:S(2)}, u32[]{:S(2)}) collective-permute-start(bf16[528,768]{1,0:T(8,128)(2,1)} %copy-done.7), channel_id=1, source_target_pairs={{0,1},{1,0},{2,3},{3,2},{4,5},{5,4},{6,7},{7,6},{8,9},{9,8},{10,11... | collective-permute-start | bytes 2433032 | tf_op jit(solution)/shard_map/ppermute | solution.py:756
  (51 other events, 333.8 us)
